TPU v7x, 512 devices: a whole 4x4x16 slice. The times are simulated.
512 devices in a mesh: lat: 2 (over core), lon: 32 (over z_hi, y, x), tp: 8 (over z_lo).
Axes of the slice: x: 4, y: 4, z: 16 (z_hi: 2, z_lo: 8; z = z_hi * 8 + z_lo), core: 2. Of those that a mesh axis runs over, the one named last changes fastest.
Arguments:
- fine_tokens: bfloat16 [2, 24, 1536, 512], P(None, 'lat', ('lon', 'tp')), may hold values from -6 to 6
- fine_qkv: bfloat16 [512, 1536], replicated, may hold values from -1.5 to 1.5
- fine_out: bfloat16 [512, 512], replicated, may hold values from -0.25 to 0.25
- merge_weight: bfloat16 [2048, 1024], P(None, 'tp'), may hold values from -0.125 to 0.125
- up_weight: bfloat16 [1024, 4096], P(None, 'tp'), may hold values from -0.1875 to 0.1875
- down_weight: bfloat16 [4096, 1024], P('tp'), may hold values from -0.09375 to 0.09375
- cotangent: bfloat16 [2, 12, 768, 1024], P(None, 'lat', ('lon', 'tp')), may hold values from -24 to 24
Outputs:
- coarse_out: bfloat16 [2, 12, 768, 1024], P(None, 'lat', ('lon', 'tp'))
- grad_merged: bfloat16 [2, 12, 768, 1024], P(None, 'lat', ('lon', 'tp'))
- grad_down: float32 [4096, 1024], P('tp', ('lat', 'lon'))
All inputs are finite; a program needn't handle non-finite values.
Results may differ from a plain program's by a relative error of at most 0.023.
The roundings to bfloat16 on the way count: a program that leaves them out, or rounds other values in their place, can miss the bound.
Values may be sent and summed in bfloat16 or wider, within the bound.
No kernel may reach another device: no remote copies, remote signals or barrier semaphores. Data moves between devices by JAX's collectives and lax.ppermute only.
A program may use at most 64 MiB of HBM per device.

v0:
```python
import jax
import jax.numpy as jnp
from jax import lax
from jax.sharding import PartitionSpec as P

HEAD_DIM = 32


EPS = 1e-05


def passed_along(value, axis, steps):
    count = lax.axis_size(axis)
    pairs = [(source, (source + steps) % count) for source in range(count)]
    return lax.ppermute(value, axis, pairs)


def norm_rows(values):
    values = values.astype(jnp.float32)
    centred = values - jnp.mean(values, axis=-1, keepdims=True)
    variance = jnp.mean(centred * centred, axis=-1, keepdims=True)
    return centred * lax.rsqrt(variance + EPS)


def gelu_exact(values):
    return jax.nn.gelu(values, approximate=False)


def to_windows(block):
    levels, lat_rows, columns, feats = block.shape
    shaped = block.reshape(levels // 2, 2, lat_rows // 12, 12, columns // 6, 6, feats)
    return shaped.transpose(4, 0, 2, 1, 3, 5, 6).reshape(-1, 144, feats)


def from_windows(windows, levels, lat_rows, columns):
    feats = windows.shape[-1]
    shaped = windows.reshape(columns // 6, levels // 2, lat_rows // 12, 2, 12, 6, feats)
    return shaped.transpose(1, 3, 2, 4, 0, 5, 6).reshape(levels, lat_rows, columns, feats)


def attend_columns(block, channels):
    levels, lat_rows, columns, feats = block.shape
    windows = to_windows(block)
    count = windows.shape[0]
    heads = channels // HEAD_DIM
    queries = windows[..., :channels].reshape(count, 144, heads, HEAD_DIM)
    key_rows = windows[..., channels : 2 * channels].reshape(count, 144, heads, HEAD_DIM)
    value_rows = windows[..., 2 * channels :].reshape(count, 144, heads, HEAD_DIM)
    scores = jnp.einsum(
        "wqhd,wkhd->whqk", queries, key_rows, preferred_element_type=jnp.float32
    ) * HEAD_DIM ** (-0.5)
    probs = jax.nn.softmax(scores, axis=-1).astype(jnp.bfloat16)
    mixed = jnp.einsum("whqk,wkhd->wqhd", probs, value_rows, preferred_element_type=jnp.float32)
    mixed = mixed.astype(jnp.bfloat16).reshape(count, 144, channels)
    return from_windows(mixed, levels, lat_rows, columns)


def on_device(fine_tokens, fine_qkv, fine_out, merge_weight, up_weight, down_weight, cotangent):
    levels, lat_rows, columns, channels = fine_tokens.shape
    normed = norm_rows(fine_tokens).astype(jnp.bfloat16)
    packed = jnp.dot(normed.reshape(-1, channels), fine_qkv, preferred_element_type=jnp.float32)
    packed = packed.astype(jnp.bfloat16).reshape(levels, lat_rows, columns, 3 * channels)
    west_cols = passed_along(packed[:, :, columns - 3 :], ("lon", "tp"), 1)
    mixed = attend_columns(
        jnp.concatenate([west_cols, packed[:, :, : columns - 3]], axis=2), channels
    )
    returned = passed_along(mixed[:, :, :3], ("lon", "tp"), -1)
    mixed = jnp.concatenate([mixed[:, :, 3:], returned], axis=2)
    projected = jnp.dot(mixed.reshape(-1, channels), fine_out, preferred_element_type=jnp.float32)
    section = (fine_tokens.astype(jnp.float32) + projected.reshape(fine_tokens.shape)).astype(
        jnp.bfloat16
    )
    blocks = section.reshape(levels, lat_rows // 2, 2, columns // 2, 2, channels).transpose(
        0, 1, 3, 2, 4, 5
    )
    merged_in = norm_rows(blocks.reshape(-1, 4 * channels)).astype(jnp.bfloat16)
    coarse_width = cotangent.shape[-1]
    cot_rows = cotangent.reshape(1, -1, coarse_width)
    own_merged = jnp.dot(
        merged_in,
        lax.all_gather(merge_weight, "tp", axis=1, tiled=True),
        preferred_element_type=jnp.float32,
    ).astype(jnp.bfloat16)
    group_merged, group_cot = (
        lax.all_gather(own_merged[None], "tp", axis=0, tiled=True),
        lax.all_gather(cot_rows, "tp", axis=0, tiled=True),
    )
    flat_merged = group_merged.reshape(-1, coarse_width)
    flat_cot = group_cot.reshape(-1, coarse_width)
    coarse_normed = norm_rows(flat_merged).astype(jnp.bfloat16)
    preact = jnp.dot(coarse_normed, up_weight, preferred_element_type=jnp.float32)
    hidden_f, gelu_back = jax.vjp(gelu_exact, preact)
    hidden = hidden_f.astype(jnp.bfloat16)
    grad_hidden = lax.dot_general(
        flat_cot, down_weight, (((1,), (1,)), ((), ())), preferred_element_type=jnp.float32
    )
    grad_preact = gelu_back(grad_hidden)[0].astype(jnp.bfloat16)
    picked = hidden
    summed = lax.psum_scatter(
        jnp.dot(picked, down_weight, preferred_element_type=jnp.float32).astype(jnp.bfloat16),
        "tp",
        scatter_dimension=0,
        tiled=True,
    ).astype(jnp.float32)
    picked = grad_preact
    grad_normed = lax.psum_scatter(
        lax.dot_general(
            picked, up_weight, (((1,), (1,)), ((), ())), preferred_element_type=jnp.float32
        ).astype(jnp.bfloat16),
        "tp",
        scatter_dimension=0,
        tiled=True,
    ).astype(jnp.float32)
    coarse_out = (
        (own_merged.astype(jnp.float32) + summed).astype(jnp.bfloat16).reshape(cotangent.shape)
    )
    merged_f = own_merged.astype(jnp.float32)
    centred = merged_f - jnp.mean(merged_f, axis=-1, keepdims=True)
    scale_inv = lax.rsqrt(jnp.mean(centred * centred, axis=-1, keepdims=True) + EPS)
    nhat = centred * scale_inv
    grad_merged = cot_rows[0].astype(jnp.float32) + scale_inv * (
        grad_normed
        - jnp.mean(grad_normed, axis=-1, keepdims=True)
        - nhat * jnp.mean(grad_normed * nhat, axis=-1, keepdims=True)
    )
    grad_merged = grad_merged.astype(jnp.bfloat16).reshape(cotangent.shape)
    weight_term = lax.dot_general(
        hidden, flat_cot, (((0,), (0,)), ((), ())), preferred_element_type=jnp.float32
    )
    grad_down = lax.psum_scatter(weight_term, ("lat", "lon"), scatter_dimension=1, tiled=True)
    return (coarse_out, grad_merged, grad_down)


def solution(mesh):
    placed = (
        P(None, "lat", ("lon", "tp"), None),
        P(),
        P(),
        P(None, "tp"),
        P(None, "tp"),
        P("tp", None),
        P(None, "lat", ("lon", "tp"), None),
    )
    return jax.shard_map(
        on_device,
        mesh=mesh,
        in_specs=placed,
        out_specs=(
            P(None, "lat", ("lon", "tp"), None),
            P(None, "lat", ("lon", "tp"), None),
            P("tp", ("lat", "lon")),
        ),
        check_vma=False,
    )
```

profile of v0, /device:TPU:1, one launch (start us, length us, event | category | flops | bytes accessed | tf_op | source)
XLA Modules:
  0.0 784.7 jit_solution(7623382720738741030)
XLA Ops:
  8.0 1.0 convert_reduce_fusion.1
  9.0 1.1 fusion.22
  10.1 1.0 fusion.23
  12.1 4.4 collective-permute-start
  16.6 18.8 %collective-permute-done = bf16[2,12,3,1536]{3,2,1,0:T(4,128)(2,1)S(1)} collective-permute-done((bf16[2,12,3,1536]{3,2,1,0:T(4,128)(2,1)S(1)}, bf16[2,12,3,1536]{3,2,1,0:T(4,128)(2,1)S(1)}, u32[]{:S(2)}, u32[]{:S(2)}) %collective-permute-start) | collective-permute-done | bytes 221216 | tf_op jit(solution)/shard_map/ppermute | solution.py:15
  36.3 2.4 fusion.54
  38.7 2.0 fusion.9
  41.8 3.1 collective-permute-start.1
  44.8 46.1 %all_gather.11 = bf16[8,36,1024]{2,1,0:T(8,128)(2,1)S(1)} all-gather(bf16[1,36,1024]{2,1,0:T(8,128)(2,1)S(1)} %reshape.178), channel_id=1, replica_groups=mesh['lat'=2,'lon'=32,'tp'=8] {'tp'}, dimensions={0}, use_global_device_ids=true | all-gather | bytes 663552 | tf_op jit(solution)/shard_map/all_gather | solution.py:86
  91.1 1.4 fusion.8
  94.1 40.6 %all-gather.4.cloned.1.call-done = bf16[2048,1024]{1,0:T(8,128)(2,1)} async-done(((bf16[2048,128]{1,0:T(8,128)(2,1)}), bf16[2048,1024]{1,0:T(8,128)(2,1)}) %all-gather.4.cloned.1.call-update) | async-done | bytes 4194320 | tf_op jit(solution)/shard_map/all_gather | solution.py:81
  134.7 3.2 convert_reduce_fusion.3
  137.9 42.7 %all-gather.1 = bf16[8,36,1024]{2,1,0:T(8,128)(2,1)S(1)} all-gather(bf16[1,36,1024]{2,1,0:T(8,128)(2,1)S(1)} %bitcast.43), channel_id=2, replica_groups=mesh['lat'=2,'lon'=32,'tp'=8] {'tp'}, dimensions={0}, use_global_device_ids=true | all-gather | bytes 663552 | tf_op jit(solution)/shard_map/all_gather | solution.py:85
  180.7 1.1 reshape.196
  182.4 4.2 multiply_convert_fusion.2
  186.6 2.1 fusion.57
  188.9 1.3 dynamic-slice.6
  190.8 1.7 convolution_convert_fusion.2
  192.5 3.7 convolution_convert_fusion.1
  196.3 38.4 %fusion.49 = (bf16[40,1024]{1,0:T(8,128)(2,1)S(1)}, bf16[40,1024]{1,0:T(8,128)(2,1)S(1)}) fusion(bf16[288,1024]{1,0:T(8,128)(2,1)S(1)} %convolution_convert_fusion.2, bf16[288,1024]{1,0:T(8,128)(2,1)} %convolution_convert_fusion.1), kind=kCustom, calls=%all-reduce-scatter.2 | all-reduce-scatter fusion | flops 655361 | bytes 1345536
  234.7 1.3 collective-permute-start.2
  236.0 1.3 collective-permute-start.3
  238.1 1.0 collective-permute-done.3
  241.2 536.7 %reduce-scatter.6.cloned.1.call-done = f32[512,16]{0,1:T(8,128)} async-done(((f32[512,1024]{0,1:T(8,128)}), f32[512,16]{0,1:T(8,128)}) %reduce-scatter.6.cloned.1.call-update) | async-done | bytes 32784 | tf_op jit(solution)/shard_map/reduce_scatter | solution.py:130
  (63 shorter events, 9.0 us)
Async XLA Ops:
  7.2 4.1 copy-start
  7.2 127.6 %all-gather.4.cloned.1.call-start = ((), (), s32[]{:S(2)}) async-start(), calls=%async_computation.1 | async-start | bytes 4718592 | tf_op jit(solution)/shard_map/all_gather | solution.py:81
  7.9 769.9 %reduce-scatter.6.cloned.1.call-start = ((), (), s32[]{:S(2)}) async-start(), calls=%async_computation.2 | async-start | bytes 2129920 | tf_op jit(solution)/shard_map/reduce_scatter | solution.py:130
  11.7 4.8 copy-start.2
  12.1 23.3 %collective-permute-start = (bf16[2,12,3,1536]{3,2,1,0:T(4,128)(2,1)S(1)}, bf16[2,12,3,1536]{3,2,1,0:T(4,128)(2,1)S(1)}, u32[]{:S(2)}, u32[]{:S(2)}) collective-permute-start(bf16[2,12,3,1536]{3,2,1,0:T(4,128)(2,1)S(1)} %get-tuple-element.23), channel_id=1, source_target_pairs={{0,1},{1,2},{2,3},{3,4},{4,5},{5,6},{6,7},{7,8},{8,9},{9,10},{10,1... | collective-permute-start | bytes 663560 | tf_op jit(solution)/shard_map/ppermute | solution.py:15
  41.1 49.9 %copy-start.1 = (bf16[2,12,6,512]{3,0,2,1:T(2,128)(2,1)S(1)}, bf16[2,12,6,512]{3,0,2,1:T(2,128)(2,1)}, u32[]{:S(2)}) copy-start(bf16[2,12,6,512]{3,0,2,1:T(2,128)(2,1)} %param.7) | copy-start | bytes 442372
  41.8 49.3 %collective-permute-start.1 = (bf16[2,12,3,512]{3,2,1,0:T(4,128)(2,1)S(1)}, bf16[2,12,3,512]{3,2,1,0:T(4,128)(2,1)S(1)}, u32[]{:S(2)}, u32[]{:S(2)}) collective-permute-start(bf16[2,12,3,512]{3,2,1,0:T(4,128)(2,1)S(1)} %get-tuple-element.29), channel_id=1, source_target_pairs={{0,255},{1,0},{2,1},{3,2},{4,3},{5,4},{6,5},{7,6},{8,7},{9,8},{10,... | collective-permute-start | bytes 221192 | tf_op jit(solution)/shard_map/ppermute | solution.py:15
  234.7 3.3 collective-permute-start.2
  236.0 3.1 collective-permute-start.3
Sparse Core Ops, SparseCore 0:
  10.0 124.6 all-gather.3
  188.9 588.9 reduce-scatter.5
where the time goes:
time: 799 us; the launch traced here: 785 us
  waiting for transfers between devices  598 us (75%)
  blocking collectives  127 us (16%)
  matrix products  21.2 us (3%)
  between operations  15.1 us (2%)
  starting transfers between devices  10.1 us (1%)
    reduce_scatter x1, waiting for transfers between devices, on_device(): lax.psum_scatter(weight_term, ('lat', 'lon'), scatter_dimension=1, tiled=...  537 us
    all_gather x1, blocking collectives, on_device(): lax.all_gather(cot_rows, 'tp', axis=0, tiled=True)  46.1 us
    all_gather x1, blocking collectives, on_device(): lax.all_gather(own_merged[None], 'tp', axis=0, tiled=True)  42.7 us
    all_gather x1, waiting for transfers between devices, on_device(): lax.all_gather(merge_weight, 'tp', axis=1, tiled=True)  40.6 us
    unnamed x1, blocking collectives  38.4 us
    ppermute x2, waiting for transfers between devices, passed_along(): return lax.ppermute(value, axis, pairs)  18.8 us
  transfers between devices with their start and end apart: 6, of which 5 were waited for; matrix products, arithmetic and copies ran while one was open for 8% of the time, Pallas kernels for 0%

commit v1 on v0

v1 whole, which is shorter than its diff:
```python
import functools

import jax
import jax.numpy as jnp
import numpy as np
from jax import lax
from jax.experimental import pallas as pl
from jax.experimental.pallas import tpu as pltpu
from jax.sharding import PartitionSpec as P

EPS = 1e-05
F32 = jnp.float32
BF16 = jnp.bfloat16
LINE = ("lon", "tp")
COUNT = 256
RING = (0, 1, 3, 2)
ROWS = 40


def dot(a, b):
    return lax.dot_general(a, b, (((1,), (0,)), ((), ())), preferred_element_type=F32)


def dot_nt(a, b):
    return lax.dot_general(a, b, (((1,), (1,)), ((), ())), preferred_element_type=F32)


def dot_tn(a, b):
    return lax.dot_general(a, b, (((0,), (0,)), ((), ())), preferred_element_type=F32)


def moved(value, target):
    return lax.ppermute(value, LINE, [(s, target(s)) for s in range(COUNT)])


def swapped(value, bits):
    return moved(value, lambda s: s ^ bits)


def across(value):
    return lax.ppermute(value, "lat", [(0, 1), (1, 0)])


def z_bits(index):
    return index


def x_bits(index):
    return index << 3


def y_bits(index):
    return index << 5


Z_HALF = 4
Z_HI = 1 << 7


def norm_rows(values):
    centred = values - jnp.mean(values, axis=-1, keepdims=True)
    variance = jnp.mean(centred * centred, axis=-1, keepdims=True)
    return centred * lax.rsqrt(variance + EPS)


def call(kernel, out_shape, *args, flops=0, scalars=0, **kw):
    specs = [
        pl.BlockSpec(memory_space=pltpu.SMEM if i < scalars else pltpu.VMEM)
        for i in range(len(args))
    ]
    size = sum(a.size * a.dtype.itemsize for a in args)
    return pl.pallas_call(
        kernel,
        out_shape=out_shape,
        in_specs=specs,
        out_specs=jax.tree.map(lambda _: pl.BlockSpec(memory_space=pltpu.VMEM), out_shape),
        compiler_params=pltpu.CompilerParams(vmem_limit_bytes=40 * 1024 * 1024),
        cost_estimate=pl.CostEstimate(flops=flops, bytes_accessed=size, transcendentals=0),
        **kw,
    )(*args)


def shaped(shape, dtype=BF16):
    return jax.ShapeDtypeStruct(shape, dtype)


def merge_order():
    order = np.zeros((4 * ROWS, 144), np.float32)
    for quarter in range(4):
        d_lat, d_lon = quarter // 2, quarter % 2
        for token in range(36):
            lat, lon, lev = token // 6, token % 6 // 2, token % 2
            row, column = 2 * lat + d_lat, 2 * lon + d_lon
            source = 72 * (column // 3) + 6 * row + 2 * (column % 3) + lev
            order[ROWS * quarter + token, source] = 1.0
    return order.astype(jnp.bfloat16)


def attend_kernel(own0, own1, west, east, qkv, out_w, order, result):
    tokens = jnp.concatenate(
        [r[...].astype(F32) for r in (own0, own1, west, east)], axis=0
    )
    normed = norm_rows(tokens).astype(BF16)
    packed = dot(normed, qkv[...]).astype(BF16).astype(F32)
    lane = lax.broadcasted_iota(jnp.int32, (1, 128), 1) // 32
    masks = [(lane == h).astype(F32) for h in range(4)]
    scale = 32 ** -0.5
    halves = []
    for window in range(2):
        rows = slice(72 * window, 72 * window + 72)
        other = slice(144 + 72 * window, 216 + 72 * window)
        parts = []
        for group in range(4):
            low = 128 * group
            queries = packed[rows, low : low + 128]
            keys = jnp.concatenate(
                [packed[rows, 512 + low : 640 + low], packed[other, 512 + low : 640 + low]], axis=0
            ).astype(BF16)
            values = jnp.concatenate(
                [packed[rows, 1024 + low : 1152 + low], packed[other, 1024 + low : 1152 + low]], axis=0
            ).astype(BF16)
            stacked = jnp.concatenate([queries * m for m in masks], axis=0).astype(BF16)
            scores = dot_nt(stacked, keys) * scale
            scores = scores - jnp.max(scores, axis=-1, keepdims=True)
            scores = jnp.exp(scores)
            probs = (scores / jnp.sum(scores, axis=-1, keepdims=True)).astype(BF16)
            mixed = dot(probs, values)
            total = mixed[0:72] * masks[0]
            for h in range(1, 4):
                total = total + mixed[72 * h : 72 * h + 72] * masks[h]
            parts.append(total)
        halves.append(jnp.concatenate(parts, axis=1))
    mixed = jnp.concatenate(halves, axis=0).astype(BF16)
    section = (tokens[0:144] + dot(mixed, out_w[...])).astype(BF16)
    spread = dot(order[...], section)
    wide = jnp.concatenate([spread[ROWS * q : ROWS * q + ROWS] for q in range(4)], axis=1)
    result[...] = norm_rows(wide).astype(BF16)


def merge_kernel(b0, b1, b2, b3, own_w, far_w, result):
    blocks = jnp.concatenate([b[...].astype(F32) for b in (b0, b1, b2, b3)], axis=0).astype(BF16)
    for half, weight in enumerate((own_w, far_w)):
        part = dot(blocks, weight[...])
        for j in range(4):
            result[j, :, 128 * half : 128 * half + 128] = part[ROWS * j : ROWS * j + ROWS].astype(BF16)


def pack_kernel(place, merge, up, down, packed):
    r = place[0]
    packed[0:32, :] = up[pl.ds(pl.multiple_of(r * 32, 32), 32), :]
    half = lax.rem(r, 2)
    row = pl.multiple_of((r // 2) * 32, 32)
    packed[32:64, :] = down[pl.ds(row, 32), pl.ds(pl.multiple_of(half * 512, 512), 512)]
    for q in range(4):
        packed[64:80, 128 * q : 128 * q + 128] = merge[pl.ds(pl.multiple_of(512 * q + r * 16, 16), 16), :]


def unpack_kernel(place, near, far, merge, up, down):
    for side, source in enumerate((near, far)):
        for b in range(4):
            for a in range(4):
                r = (place[0] ^ side) * 16 + (place[1] ^ RING[b]) * 4 + (place[2] ^ RING[a])
                piece = 4 * b + a
                up[pl.ds(pl.multiple_of(r * 32, 32), 32), :] = source[piece, 0:32, :]
                row = pl.multiple_of((r // 2) * 32, 32)
                column = pl.multiple_of(lax.rem(r, 2) * 512, 512)
                down[pl.ds(row, 32), pl.ds(column, 512)] = source[piece, 32:64, :]
                for q in range(4):
                    at = pl.multiple_of(512 * q + r * 16, 16)
                    merge[pl.ds(at, 16), :] = source[piece, 64:80, 128 * q : 128 * q + 128]


def far_weights(place, merge, up, down):
    lat, y, x = place[0], place[1], place[2]
    index = (lat * 16 + y * 4 + x).reshape(1)
    packed = call(pack_kernel, shaped((80, 512)), index, merge, up, down, scalars=1)
    held = swapped(packed, Z_HALF)[None]
    for axis_bits in (x_bits, y_bits):
        for step in (1, 3):
            held = jnp.concatenate([held, swapped(held, axis_bits(step))], axis=0)
    other = across(held)
    return call(
        unpack_kernel,
        (shaped((2048, 128)), shaped((1024, 512)), shaped((512, 1024))),
        place,
        held,
        other,
        scalars=1,
    )


def gelu_parts(values):
    cdf = 0.5 * (1.0 + lax.erf(values * np.float32(np.sqrt(0.5))))
    density = jnp.exp(-0.5 * values * values) * np.float32(1.0 / np.sqrt(2.0 * np.pi))
    return values * cdf, cdf + values * density


def feed_kernel(
    place, m0, m1, m2, m3, c0, c1, c2, c3, up0, up1, down0, down1,
    own_merged, s0, s1, s2, s3, hidden_out, merged, hidden, grad,
):
    th, tl = place[3], place[4]
    for j, source in enumerate((m0, m1, m2, m3)):
        for half in range(2):
            column = ((th ^ half) * 4 + (tl ^ j)) * 128
            column = pl.multiple_of(column, 128)
            for block in range(4):
                merged[ROWS * block : ROWS * block + ROWS, pl.ds(column, 128)] = source[
                    block ^ j, :, 128 * half : 128 * half + 128
                ].astype(F32)
    own_merged[...] = merged[0:ROWS, :].astype(BF16)
    normed = norm_rows(merged[...]).astype(BF16)
    cots = jnp.concatenate([c[...].astype(F32) for c in (c0, c1, c2, c3)], axis=0).astype(BF16)
    for half, (up, down) in enumerate(((up0, down0), (up1, down1))):
        columns = slice(512 * half, 512 * half + 512)
        value, slope = gelu_parts(dot(normed, up[...]))
        hidden[:, columns] = value.astype(BF16)
        grad[:, columns] = (dot_nt(cots, down[...]) * slope).astype(BF16)
    hidden_out[...] = hidden[...]
    partial = dot(hidden[:, 0:512], down0[...]) + dot(hidden[:, 512:1024], down1[...])
    back = dot_nt(grad[:, 0:512], up0[...]) + dot_nt(grad[:, 512:1024], up1[...])
    for j, sent in enumerate((s0, s1, s2, s3)):
        rows = slice(ROWS * j, ROWS * j + ROWS)
        sent[0] = partial[rows].astype(BF16)
        sent[1] = back[rows].astype(BF16)


def finish_kernel(merged, cot, s0, r1, r2, r3, coarse_out, grad_merged):
    merged_f = merged[...].astype(F32)
    summed = s0[0].astype(F32) + r1[0].astype(F32) + r2[0].astype(F32) + r3[0].astype(F32)
    coarse_out[...] = (merged_f + summed).astype(BF16)
    grad_normed = s0[1].astype(F32) + r1[1].astype(F32) + r2[1].astype(F32) + r3[1].astype(F32)
    centred = merged_f - jnp.mean(merged_f, axis=-1, keepdims=True)
    scale_inv = lax.rsqrt(jnp.mean(centred * centred, axis=-1, keepdims=True) + EPS)
    nhat = centred * scale_inv
    grad = cot[...].astype(F32) + scale_inv * (
        grad_normed
        - jnp.mean(grad_normed, axis=-1, keepdims=True)
        - nhat * jnp.mean(grad_normed * nhat, axis=-1, keepdims=True)
    )
    grad_merged[...] = grad.astype(BF16)


def column_kernel(place, c0, c1, c2, c3, near, far):
    cots = jnp.concatenate([c[...].astype(F32) for c in (c0, c1, c2, c3)], axis=0).astype(BF16)
    lat, y, x, zh = place[0], place[1], place[2], place[5]
    source = lax.broadcasted_iota(jnp.int32, (512, 512), 0)
    target = lax.broadcasted_iota(jnp.int32, (512, 512), 1)
    x_part, y_part, z_part = target >> 7, (target >> 5) & 3, (target >> 4) & 1
    x_abs = (x_part ^ (x_part >> 1)) ^ x
    y_abs = (y_part ^ (y_part >> 1)) ^ y
    wanted = (((z_part ^ zh) * 4 + y_abs) * 4 + x_abs) * 16 + (target & 15)
    chosen = jnp.where(source == wanted, 1.0, 0.0).astype(BF16)
    low, high = cots[:, 0:512], cots[:, 512:1024]
    mine = jnp.where(lat == 0, low.astype(F32), high.astype(F32)).astype(BF16)
    theirs = jnp.where(lat == 0, high.astype(F32), low.astype(F32)).astype(BF16)
    near[...] = dot(mine, chosen).astype(BF16)
    far[...] = dot(theirs, chosen).astype(BF16)


def weight_kernel(near, near_hidden, far, far_hidden, kept, sent):
    rows = jnp.concatenate([near[...].astype(F32), far[...].astype(F32)], axis=0).astype(BF16)
    hidden = jnp.concatenate([near_hidden[...].astype(F32), far_hidden[...].astype(F32)], axis=0).astype(BF16)
    total = dot_tn(rows, hidden)
    kept[...] = total[0:256]
    sent[...] = total[256:512].astype(BF16)


def add_kernel(kept, got, left, sent):
    half = left.shape[0]
    total = kept[...] + got[...].astype(F32)
    left[...] = total[0:half]
    sent[...] = total[half:].astype(BF16)


def last_kernel(kept, got, left, sent):
    total = kept[...] + got[...].astype(F32)
    left[...] = total[:, 0:512]
    sent[...] = total[:, 512:1024].astype(BF16)


def token_rows(block):
    return block.transpose(1, 2, 0, 3).reshape(-1, block.shape[-1])


def on_device(fine_tokens, fine_qkv, fine_out, merge_weight, up_weight, down_weight, cotangent):
    lon, tp = lax.axis_index("lon"), lax.axis_index("tp")
    place = jnp.stack(
        [lax.axis_index("lat"), (lon >> 2) & 3, lon & 3, tp >> 2, tp & 3, lon >> 4]
    ).astype(jnp.int32)

    own0 = token_rows(fine_tokens[:, :, :3])
    own1 = token_rows(fine_tokens[:, :, 3:])
    west = moved(own1, lambda s: (s + 1) % COUNT)
    east = moved(own0, lambda s: (s - 1) % COUNT)

    far_merge, far_up, far_down = far_weights(place, merge_weight, up_weight, down_weight)

    cot = jnp.pad(token_rows(cotangent), ((0, ROWS - 36), (0, 0)))
    cots = [cot] + [swapped(cot, z_bits(j)) for j in (1, 2, 3)]

    merged_in = call(
        attend_kernel, shaped((ROWS, 2048)), own0, own1, west, east, fine_qkv, fine_out,
        jnp.asarray(merge_order()), flops=10**9,
    )
    ins = [merged_in] + [swapped(merged_in, z_bits(j)) for j in (1, 2, 3)]
    columns = call(merge_kernel, shaped((4, ROWS, 256)), *ins, merge_weight, far_merge, flops=2 * 10**8)
    held = [columns] + [swapped(columns, z_bits(j)) for j in (1, 2, 3)]

    near_cot, far_cot = call(
        column_kernel, (shaped((4 * ROWS, 512)), shaped((4 * ROWS, 512))), place, *cots, scalars=1, flops=10**8
    )
    other_cot = across(far_cot)

    own_merged, *sent, hidden = call(
        feed_kernel,
        (shaped((ROWS, 1024)),) + tuple(shaped((2, ROWS, 1024)) for _ in range(4)) + (shaped((4 * ROWS, 1024)),),
        place, *held, *cots, up_weight, far_up, down_weight, far_down,
        scalars=1, flops=2 * 10**9,
        scratch_shapes=[
            pltpu.VMEM((4 * ROWS, 1024), F32),
            pltpu.VMEM((4 * ROWS, 1024), BF16),
            pltpu.VMEM((4 * ROWS, 1024), BF16),
        ],
    )
    got = [swapped(sent[j], z_bits(j)) for j in (1, 2, 3)]
    other_hidden = across(hidden)

    kept, out = call(
        weight_kernel, (shaped((256, 1024), F32), shaped((256, 1024))),
        near_cot, hidden, other_cot, other_hidden, flops=3 * 10**8,
    )
    for bits, rows in ((x_bits(3), 128), (x_bits(1), 64), (y_bits(3), 32), (y_bits(1), 16)):
        kept, out = call(
            add_kernel, (shaped((rows, 1024), F32), shaped((rows, 1024))), kept, swapped(out, bits)
        )
    kept, out = call(
        last_kernel, (shaped((16, 512), F32), shaped((16, 512))), kept, swapped(out, Z_HI)
    )
    grad_down = (kept + swapped(out, Z_HALF).astype(F32)).T

    coarse_out, grad_merged = call(
        finish_kernel, (shaped((ROWS, 1024)), shaped((ROWS, 1024))), own_merged, cot, sent[0], *got
    )

    def placed(rows):
        return rows[:36].reshape(6, 3, 2, 1024).transpose(2, 0, 1, 3)

    return placed(coarse_out), placed(grad_merged), grad_down


def solution(mesh):
    tokens = P(None, "lat", ("lon", "tp"), None)
    return jax.shard_map(
        on_device,
        mesh=mesh,
        in_specs=(tokens, P(), P(), P(None, "tp"), P(None, "tp"), P("tp", None), tokens),
        out_specs=(tokens, tokens, P("tp", ("lat", "lon"))),
        check_vma=False,
    )
```

time: 799 us -> 212 us (0.27)
  the two profiles are of different devices: /device:TPU:1 before, /device:TPU:392 now
where the time goes in v1:
time: 212 us; the launch traced here: 211 us
  starting transfers between devices  108 us (51%)
  waiting for transfers between devices  82.8 us (39%)
  Pallas kernels  9.52 us (4%)
  local copies, waits for them, and re-layouts  8.42 us (4%)
    ppermute x25, starting transfers between devices, moved(): return lax.ppermute(value, LINE, [(s, target(s)) for s in range(COUNT)])  102 us
    ppermute x25, waiting for transfers between devices, moved(): return lax.ppermute(value, LINE, [(s, target(s)) for s in range(COUNT)])  81.8 us
    pallas_call x13, Pallas kernels, call(): pl.pallas_call(kernel, out_shape=out_shape, in_specs=specs, out_specs=jax...  9.52 us
    ppermute x3, starting transfers between devices, across(): return lax.ppermute(value, 'lat', [(0, 1), (1, 0)])  6.25 us
    unnamed x24, local copies, waits for them, and re-layouts  5.86 us
  transfers between devices with their start and end apart: 28, of which 15 were waited for; matrix products, arithmetic and copies ran while one was open for 1% of the time, Pallas kernels for 3%

profile of v1, /device:TPU:392, one launch (start us, length us, event | category | flops | bytes accessed | tf_op | source)
XLA Modules:
  0.0 211.0 jit_solution(9419563497653385458)
XLA Ops:
  4.2 5.5 %collective-permute-start.5 = (bf16[80,512]{1,0:T(8,128)(2,1)S(1)}, bf16[80,512]{1,0:T(8,128)(2,1)S(1)}, u32[]{:S(2)}, u32[]{:S(2)}) collective-permute-start(bf16[80,512]{1,0:T(8,128)(2,1)S(1)} %shard_map.104), channel_id=1, source_target_pairs={{0,4},{1,5},{2,6},{3,7},{4,0},{5,1},{6,2},{7,3},{8,12},{9,13},{10,... | collective-permute-start | bytes 245768 | tf_op jit(solution)/shard_map/ppermute | solution.py:33
  9.6 7.0 %collective-permute-done.5 = bf16[80,512]{1,0:T(8,128)(2,1)S(1)} collective-permute-done((bf16[80,512]{1,0:T(8,128)(2,1)S(1)}, bf16[80,512]{1,0:T(8,128)(2,1)S(1)}, u32[]{:S(2)}, u32[]{:S(2)}) %collective-permute-start.5) | collective-permute-done | bytes 81952 | tf_op jit(solution)/shard_map/ppermute | solution.py:33
  16.6 3.4 %collective-permute-start.6 = (bf16[1,80,512]{2,1,0:T(8,128)(2,1)S(1)}, bf16[1,80,512]{2,1,0:T(8,128)(2,1)S(1)}, u32[]{:S(2)}, u32[]{:S(2)}) collective-permute-start(bf16[1,80,512]{2,1,0:T(8,128)(2,1)S(1)} %bitcast.22), channel_id=1, source_target_pairs={{0,8},{1,9},{2,10},{3,11},{4,12},{5,13},{6,14},{7,15},{8,0},{9,1},... | collective-permute-start | bytes 245768 | tf_op jit(solution)/shard_map/ppermute | solution.py:33
  22.9 4.7 %collective-permute-start.7 = (bf16[2,80,512]{2,1,0:T(8,128)(2,1)S(1)}, bf16[2,80,512]{2,1,0:T(8,128)(2,1)S(1)}, u32[]{:S(2)}, u32[]{:S(2)}) collective-permute-start(bf16[2,80,512]{2,1,0:T(8,128)(2,1)S(1)} %pad_maximum_fusion.2), channel_id=1, source_target_pairs={{0,24},{1,25},{2,26},{3,27},{4,28},{5,29},{6,30},{7,31},{8,16},{9,... | collective-permute-start | bytes 491528 | tf_op jit(solution)/shard_map/ppermute | solution.py:33
  27.6 3.7 %collective-permute-done.7 = bf16[2,80,512]{2,1,0:T(8,128)(2,1)S(1)} collective-permute-done((bf16[2,80,512]{2,1,0:T(8,128)(2,1)S(1)}, bf16[2,80,512]{2,1,0:T(8,128)(2,1)S(1)}, u32[]{:S(2)}, u32[]{:S(2)}) %collective-permute-start.7) | collective-permute-done | bytes 163872 | tf_op jit(solution)/shard_map/ppermute | solution.py:33
  33.8 6.6 %collective-permute-done.8 = bf16[4,80,512]{2,1,0:T(8,128)(2,1)S(1)} collective-permute-done((bf16[4,80,512]{2,1,0:T(8,128)(2,1)S(1)}, bf16[4,80,512]{2,1,0:T(8,128)(2,1)S(1)}, u32[]{:S(2)}, u32[]{:S(2)}) %collective-permute-start.8) | collective-permute-done | bytes 327712 | tf_op jit(solution)/shard_map/ppermute | solution.py:33
  40.5 3.6 %collective-permute-start.9 = (bf16[8,80,512]{2,1,0:T(8,128)(2,1)S(1)}, bf16[8,80,512]{2,1,0:T(8,128)(2,1)S(1)}, u32[]{:S(2)}, u32[]{:S(2)}) collective-permute-start(bf16[8,80,512]{2,1,0:T(8,128)(2,1)S(1)} %pad_maximum_fusion), channel_id=1, source_target_pairs={{0,96},{1,97},{2,98},{3,99},{4,100},{5,101},{6,102},{7,103},{8,104... | collective-permute-start | bytes 1966088 | tf_op jit(solution)/shard_map/ppermute | solution.py:33
  44.2 10.9 %collective-permute-done.9 = bf16[8,80,512]{2,1,0:T(8,128)(2,1)S(1)} collective-permute-done((bf16[8,80,512]{2,1,0:T(8,128)(2,1)S(1)}, bf16[8,80,512]{2,1,0:T(8,128)(2,1)S(1)}, u32[]{:S(2)}, u32[]{:S(2)}) %collective-permute-start.9) | collective-permute-done | bytes 655392 | tf_op jit(solution)/shard_map/ppermute | solution.py:33
  59.7 4.6 %collective-permute-start.1 = (bf16[72,512]{1,0:T(8,128)(2,1)S(1)}, bf16[72,512]{1,0:T(8,128)(2,1)S(1)}, u32[]{:S(2)}, u32[]{:S(2)}) collective-permute-start(bf16[72,512]{1,0:T(8,128)(2,1)S(1)} %reshape.24.own0), channel_id=1, source_target_pairs={{0,255},{1,0},{2,1},{3,2},{4,3},{5,4},{6,5},{7,6},{8,7},{9,8},{10,... | collective-permute-start | bytes 221192 | tf_op jit(solution)/shard_map/ppermute | solution.py:33
  72.0 4.6 %collective-permute-start.2 = (bf16[40,2048]{1,0:T(8,128)(2,1)S(1)}, bf16[40,2048]{1,0:T(8,128)(2,1)S(1)}, u32[]{:S(2)}, u32[]{:S(2)}) collective-permute-start(bf16[40,2048]{1,0:T(8,128)(2,1)S(1)} %shard_map.103.b0), channel_id=1, source_target_pairs={{0,1},{1,0},{2,3},{3,2},{4,5},{5,4},{6,7},{7,6},{8,9},{9,8},{10,11... | collective-permute-start | bytes 491528 | tf_op jit(solution)/shard_map/ppermute | solution.py:33
  76.7 15.3 %collective-permute-start.3 = (bf16[40,2048]{1,0:T(8,128)(2,1)S(1)}, bf16[40,2048]{1,0:T(8,128)(2,1)S(1)}, u32[]{:S(2)}, u32[]{:S(2)}) collective-permute-start(bf16[40,2048]{1,0:T(8,128)(2,1)S(1)} %shard_map.103.b0), channel_id=1, source_target_pairs={{0,2},{1,3},{2,0},{3,1},{4,6},{5,7},{6,4},{7,5},{8,10},{9,11},{10,... | collective-permute-start | bytes 491528 | tf_op jit(solution)/shard_map/ppermute | solution.py:33
  97.4 5.9 %collective-permute-start.15 = (bf16[40,1024]{1,0:T(8,128)(2,1)S(1)}, bf16[40,1024]{1,0:T(8,128)(2,1)S(1)}, u32[]{:S(2)}, u32[]{:S(2)}) collective-permute-start(bf16[40,1024]{1,0:T(8,128)(2,1)S(1)} %pad.4.c0.cot), channel_id=1, source_target_pairs={{0,2},{1,3},{2,0},{3,1},{4,6},{5,7},{6,4},{7,5},{8,10},{9,11},{10,... | collective-permute-start | bytes 245768 | tf_op jit(solution)/shard_map/ppermute | solution.py:33
  106.9 5.7 %collective-permute-start.11 = (bf16[4,40,256]{2,1,0:T(8,128)(2,1)S(1)}, bf16[4,40,256]{2,1,0:T(8,128)(2,1)S(1)}, u32[]{:S(2)}, u32[]{:S(2)}) collective-permute-start(bf16[4,40,256]{2,1,0:T(8,128)(2,1)S(1)} %shard_map.106.m0), channel_id=1, source_target_pairs={{0,1},{1,0},{2,3},{3,2},{4,5},{5,4},{6,7},{7,6},{8,9},{9,8},{10,11... | collective-permute-start | bytes 245768 | tf_op jit(solution)/shard_map/ppermute | solution.py:33
  112.5 4.0 %collective-permute-start.12 = (bf16[4,40,256]{2,1,0:T(8,128)(2,1)S(1)}, bf16[4,40,256]{2,1,0:T(8,128)(2,1)S(1)}, u32[]{:S(2)}, u32[]{:S(2)}) collective-permute-start(bf16[4,40,256]{2,1,0:T(8,128)(2,1)S(1)} %shard_map.106.m0), channel_id=1, source_target_pairs={{0,2},{1,3},{2,0},{3,1},{4,6},{5,7},{6,4},{7,5},{8,10},{9,11},{10,... | collective-permute-start | bytes 245768 | tf_op jit(solution)/shard_map/ppermute | solution.py:33
  116.5 3.4 %collective-permute-start.13 = (bf16[4,40,256]{2,1,0:T(8,128)(2,1)S(1)}, bf16[4,40,256]{2,1,0:T(8,128)(2,1)S(1)}, u32[]{:S(2)}, u32[]{:S(2)}) collective-permute-start(bf16[4,40,256]{2,1,0:T(8,128)(2,1)S(1)} %shard_map.106.m0), channel_id=1, source_target_pairs={{0,3},{1,2},{2,1},{3,0},{4,7},{5,6},{6,5},{7,4},{8,11},{9,10},{10,... | collective-permute-start | bytes 245768 | tf_op jit(solution)/shard_map/ppermute | solution.py:33
  121.1 3.7 %collective-permute-done.13.m3 = bf16[4,40,256]{2,1,0:T(8,128)(2,1)S(1)} collective-permute-done((bf16[4,40,256]{2,1,0:T(8,128)(2,1)S(1)}, bf16[4,40,256]{2,1,0:T(8,128)(2,1)S(1)}, u32[]{:S(2)}, u32[]{:S(2)}) %collective-permute-start.13) | collective-permute-done | bytes 81952 | tf_op jit(solution)/shard_map/ppermute | solution.py:33
  135.0 8.0 %collective-permute-start.22 = (bf16[256,1024]{1,0:T(8,128)(2,1)S(1)}, bf16[256,1024]{1,0:T(8,128)(2,1)S(1)}, u32[]{:S(2)}, u32[]{:S(2)}) collective-permute-start(bf16[256,1024]{1,0:T(8,128)(2,1)S(1)} %get-tuple-element.42), channel_id=1, source_target_pairs={{0,24},{1,25},{2,26},{3,27},{4,28},{5,29},{6,30},{7,31},{8,16},{9,... | collective-permute-start | bytes 1572872 | tf_op jit(solution)/shard_map/ppermute | solution.py:33
  143.0 12.4 %collective-permute-done.22.got = bf16[256,1024]{1,0:T(8,128)(2,1)S(1)} collective-permute-done((bf16[256,1024]{1,0:T(8,128)(2,1)S(1)}, bf16[256,1024]{1,0:T(8,128)(2,1)S(1)}, u32[]{:S(2)}, u32[]{:S(2)}) %collective-permute-start.22) | collective-permute-done | bytes 524320 | tf_op jit(solution)/shard_map/ppermute | solution.py:33
  157.5 8.0 %collective-permute-done.23.got = bf16[128,1024]{1,0:T(8,128)(2,1)S(1)} collective-permute-done((bf16[128,1024]{1,0:T(8,128)(2,1)S(1)}, bf16[128,1024]{1,0:T(8,128)(2,1)S(1)}, u32[]{:S(2)}, u32[]{:S(2)}) %collective-permute-start.23) | collective-permute-done | bytes 262176 | tf_op jit(solution)/shard_map/ppermute | solution.py:33
  165.5 4.4 %collective-permute-start.24 = (bf16[64,1024]{1,0:T(8,128)(2,1)S(1)}, bf16[64,1024]{1,0:T(8,128)(2,1)S(1)}, u32[]{:S(2)}, u32[]{:S(2)}) collective-permute-start(bf16[64,1024]{1,0:T(8,128)(2,1)S(1)} %get-tuple-element.46), channel_id=1, source_target_pairs={{0,96},{1,97},{2,98},{3,99},{4,100},{5,101},{6,102},{7,103},{8,104... | collective-permute-start | bytes 393224 | tf_op jit(solution)/shard_map/ppermute | solution.py:33
  175.7 4.4 %collective-permute-start.19 = (bf16[2,40,1024]{2,1,0:T(8,128)(2,1)S(1)}, bf16[2,40,1024]{2,1,0:T(8,128)(2,1)S(1)}, u32[]{:S(2)}, u32[]{:S(2)}) collective-permute-start(bf16[2,40,1024]{2,1,0:T(8,128)(2,1)S(1)} %get-tuple-element.35), channel_id=1, source_target_pairs={{0,3},{1,2},{2,1},{3,0},{4,7},{5,6},{6,5},{7,4},{8,11},{9,10},{10,... | collective-permute-start | bytes 491528 | tf_op jit(solution)/shard_map/ppermute | solution.py:33
  182.0 4.2 %collective-permute-done.25.got = bf16[32,1024]{1,0:T(8,128)(2,1)S(1)} collective-permute-done((bf16[32,1024]{1,0:T(8,128)(2,1)S(1)}, bf16[32,1024]{1,0:T(8,128)(2,1)S(1)}, u32[]{:S(2)}, u32[]{:S(2)}) %collective-permute-start.25) | collective-permute-done | bytes 65568 | tf_op jit(solution)/shard_map/ppermute | solution.py:33
  188.2 12.6 %collective-permute-done.26.got = bf16[16,1024]{1,0:T(8,128)(2,1)S(1)} collective-permute-done((bf16[16,1024]{1,0:T(8,128)(2,1)S(1)}, bf16[16,1024]{1,0:T(8,128)(2,1)S(1)}, u32[]{:S(2)}, u32[]{:S(2)}) %collective-permute-start.26) | collective-permute-done | bytes 32800 | tf_op jit(solution)/shard_map/ppermute | solution.py:33
  204.4 5.9 %collective-permute-done.27 = bf16[16,512]{1,0:T(8,128)(2,1)S(1)} collective-permute-done((bf16[16,512]{1,0:T(8,128)(2,1)S(1)}, bf16[16,512]{1,0:T(8,128)(2,1)S(1)}, u32[]{:S(2)}, u32[]{:S(2)}) %collective-permute-start.27) | collective-permute-done | bytes 16416 | tf_op jit(solution)/shard_map/ppermute | solution.py:33
  (82 shorter events, 57.5 us)
Async XLA Ops:
  4.2 12.4 %collective-permute-start.5 = (bf16[80,512]{1,0:T(8,128)(2,1)S(1)}, bf16[80,512]{1,0:T(8,128)(2,1)S(1)}, u32[]{:S(2)}, u32[]{:S(2)}) collective-permute-start(bf16[80,512]{1,0:T(8,128)(2,1)S(1)} %shard_map.104), channel_id=1, source_target_pairs={{0,4},{1,5},{2,6},{3,7},{4,0},{5,1},{6,2},{7,3},{8,12},{9,13},{10,... | collective-permute-start | bytes 245768 | tf_op jit(solution)/shard_map/ppermute | solution.py:33
  22.9 8.4 %collective-permute-start.7 = (bf16[2,80,512]{2,1,0:T(8,128)(2,1)S(1)}, bf16[2,80,512]{2,1,0:T(8,128)(2,1)S(1)}, u32[]{:S(2)}, u32[]{:S(2)}) collective-permute-start(bf16[2,80,512]{2,1,0:T(8,128)(2,1)S(1)} %pad_maximum_fusion.2), channel_id=1, source_target_pairs={{0,24},{1,25},{2,26},{3,27},{4,28},{5,29},{6,30},{7,31},{8,16},{9,... | collective-permute-start | bytes 491528 | tf_op jit(solution)/shard_map/ppermute | solution.py:33
  31.4 9.0 %collective-permute-start.8 = (bf16[4,80,512]{2,1,0:T(8,128)(2,1)S(1)}, bf16[4,80,512]{2,1,0:T(8,128)(2,1)S(1)}, u32[]{:S(2)}, u32[]{:S(2)}) collective-permute-start(bf16[4,80,512]{2,1,0:T(8,128)(2,1)S(1)} %pad_maximum_fusion.1), channel_id=1, source_target_pairs={{0,32},{1,33},{2,34},{3,35},{4,36},{5,37},{6,38},{7,39},{8,40},{9,... | collective-permute-start | bytes 983048 | tf_op jit(solution)/shard_map/ppermute | solution.py:33
  40.5 14.6 %collective-permute-start.9 = (bf16[8,80,512]{2,1,0:T(8,128)(2,1)S(1)}, bf16[8,80,512]{2,1,0:T(8,128)(2,1)S(1)}, u32[]{:S(2)}, u32[]{:S(2)}) collective-permute-start(bf16[8,80,512]{2,1,0:T(8,128)(2,1)S(1)} %pad_maximum_fusion), channel_id=1, source_target_pairs={{0,96},{1,97},{2,98},{3,99},{4,100},{5,101},{6,102},{7,103},{8,104... | collective-permute-start | bytes 1966088 | tf_op jit(solution)/shard_map/ppermute | solution.py:33
  55.1 42.3 %collective-permute-start.10 = (bf16[16,80,512]{2,1,0:T(8,128)(2,1)S(1)}, bf16[16,80,512]{2,1,0:T(8,128)(2,1)S(1)}, u32[]{:S(2)}, u32[]{:S(2)}) collective-permute-start(bf16[16,80,512]{2,1,0:T(8,128)(2,1)S(1)} %constant_dynamic-update-slice_fusion.near), channel_id=1, source_target_pairs={{0,256},{256,0},{1,257},{257,1},{2,258},{258,2},{3,259},{259,3},{4... | collective-permute-start | bytes 3932168 | tf_op jit(solution)/shard_map/ppermute | solution.py:41
  57.2 7.8 %collective-permute-start = (bf16[72,512]{1,0:T(8,128)(2,1)S(1)}, bf16[72,512]{1,0:T(8,128)(2,1)S(1)}, u32[]{:S(2)}, u32[]{:S(2)}) collective-permute-start(bf16[72,512]{1,0:T(8,128)(2,1)S(1)} %reshape.25.own1), channel_id=1, source_target_pairs={{0,1},{1,2},{2,3},{3,4},{4,5},{5,6},{6,7},{7,8},{8,9},{9,10},{10,1... | collective-permute-start | bytes 221192 | tf_op jit(solution)/shard_map/ppermute | solution.py:33
  59.7 7.3 %collective-permute-start.1 = (bf16[72,512]{1,0:T(8,128)(2,1)S(1)}, bf16[72,512]{1,0:T(8,128)(2,1)S(1)}, u32[]{:S(2)}, u32[]{:S(2)}) collective-permute-start(bf16[72,512]{1,0:T(8,128)(2,1)S(1)} %reshape.24.own0), channel_id=1, source_target_pairs={{0,255},{1,0},{2,1},{3,2},{4,3},{5,4},{6,5},{7,6},{8,7},{9,8},{10,... | collective-permute-start | bytes 221192 | tf_op jit(solution)/shard_map/ppermute | solution.py:33
  72.0 32.3 %collective-permute-start.2 = (bf16[40,2048]{1,0:T(8,128)(2,1)S(1)}, bf16[40,2048]{1,0:T(8,128)(2,1)S(1)}, u32[]{:S(2)}, u32[]{:S(2)}) collective-permute-start(bf16[40,2048]{1,0:T(8,128)(2,1)S(1)} %shard_map.103.b0), channel_id=1, source_target_pairs={{0,1},{1,0},{2,3},{3,2},{4,5},{5,4},{6,7},{7,6},{8,9},{9,8},{10,11... | collective-permute-start | bytes 491528 | tf_op jit(solution)/shard_map/ppermute | solution.py:33
  76.7 29.7 %collective-permute-start.3 = (bf16[40,2048]{1,0:T(8,128)(2,1)S(1)}, bf16[40,2048]{1,0:T(8,128)(2,1)S(1)}, u32[]{:S(2)}, u32[]{:S(2)}) collective-permute-start(bf16[40,2048]{1,0:T(8,128)(2,1)S(1)} %shard_map.103.b0), channel_id=1, source_target_pairs={{0,2},{1,3},{2,0},{3,1},{4,6},{5,7},{6,4},{7,5},{8,10},{9,11},{10,... | collective-permute-start | bytes 491528 | tf_op jit(solution)/shard_map/ppermute | solution.py:33
  92.0 14.4 %collective-permute-start.4 = (bf16[40,2048]{1,0:T(8,128)(2,1)S(1)}, bf16[40,2048]{1,0:T(8,128)(2,1)S(1)}, u32[]{:S(2)}, u32[]{:S(2)}) collective-permute-start(bf16[40,2048]{1,0:T(8,128)(2,1)S(1)} %shard_map.103.b0), channel_id=1, source_target_pairs={{0,3},{1,2},{2,1},{3,0},{4,7},{5,6},{6,5},{7,4},{8,11},{9,10},{10,... | collective-permute-start | bytes 491528 | tf_op jit(solution)/shard_map/ppermute | solution.py:33
  94.9 21.7 %collective-permute-start.14 = (bf16[40,1024]{1,0:T(8,128)(2,1)S(1)}, bf16[40,1024]{1,0:T(8,128)(2,1)S(1)}, u32[]{:S(2)}, u32[]{:S(2)}) collective-permute-start(bf16[40,1024]{1,0:T(8,128)(2,1)S(1)} %pad.4.c0.cot), channel_id=1, source_target_pairs={{0,1},{1,0},{2,3},{3,2},{4,5},{5,4},{6,7},{7,6},{8,9},{9,8},{10,11... | collective-permute-start | bytes 245768 | tf_op jit(solution)/shard_map/ppermute | solution.py:33
  97.4 22.5 %collective-permute-start.15 = (bf16[40,1024]{1,0:T(8,128)(2,1)S(1)}, bf16[40,1024]{1,0:T(8,128)(2,1)S(1)}, u32[]{:S(2)}, u32[]{:S(2)}) collective-permute-start(bf16[40,1024]{1,0:T(8,128)(2,1)S(1)} %pad.4.c0.cot), channel_id=1, source_target_pairs={{0,2},{1,3},{2,0},{3,1},{4,6},{5,7},{6,4},{7,5},{8,10},{9,11},{10,... | collective-permute-start | bytes 245768 | tf_op jit(solution)/shard_map/ppermute | solution.py:33
  104.3 15.6 %collective-permute-start.16 = (bf16[40,1024]{1,0:T(8,128)(2,1)S(1)}, bf16[40,1024]{1,0:T(8,128)(2,1)S(1)}, u32[]{:S(2)}, u32[]{:S(2)}) collective-permute-start(bf16[40,1024]{1,0:T(8,128)(2,1)S(1)} %pad.4.c0.cot), channel_id=1, source_target_pairs={{0,3},{1,2},{2,1},{3,0},{4,7},{5,6},{6,5},{7,4},{8,11},{9,10},{10,... | collective-permute-start | bytes 245768 | tf_op jit(solution)/shard_map/ppermute | solution.py:33
  106.9 13.1 %collective-permute-start.11 = (bf16[4,40,256]{2,1,0:T(8,128)(2,1)S(1)}, bf16[4,40,256]{2,1,0:T(8,128)(2,1)S(1)}, u32[]{:S(2)}, u32[]{:S(2)}) collective-permute-start(bf16[4,40,256]{2,1,0:T(8,128)(2,1)S(1)} %shard_map.106.m0), channel_id=1, source_target_pairs={{0,1},{1,0},{2,3},{3,2},{4,5},{5,4},{6,7},{7,6},{8,9},{9,8},{10,11... | collective-permute-start | bytes 245768 | tf_op jit(solution)/shard_map/ppermute | solution.py:33
  112.5 8.5 %collective-permute-start.12 = (bf16[4,40,256]{2,1,0:T(8,128)(2,1)S(1)}, bf16[4,40,256]{2,1,0:T(8,128)(2,1)S(1)}, u32[]{:S(2)}, u32[]{:S(2)}) collective-permute-start(bf16[4,40,256]{2,1,0:T(8,128)(2,1)S(1)} %shard_map.106.m0), channel_id=1, source_target_pairs={{0,2},{1,3},{2,0},{3,1},{4,6},{5,7},{6,4},{7,5},{8,10},{9,11},{10,... | collective-permute-start | bytes 245768 | tf_op jit(solution)/shard_map/ppermute | solution.py:33
  116.5 8.2 %collective-permute-start.13 = (bf16[4,40,256]{2,1,0:T(8,128)(2,1)S(1)}, bf16[4,40,256]{2,1,0:T(8,128)(2,1)S(1)}, u32[]{:S(2)}, u32[]{:S(2)}) collective-permute-start(bf16[4,40,256]{2,1,0:T(8,128)(2,1)S(1)} %shard_map.106.m0), channel_id=1, source_target_pairs={{0,3},{1,2},{2,1},{3,0},{4,7},{5,6},{6,5},{7,4},{8,11},{9,10},{10,... | collective-permute-start | bytes 245768 | tf_op jit(solution)/shard_map/ppermute | solution.py:33
  135.0 20.4 %collective-permute-start.22 = (bf16[256,1024]{1,0:T(8,128)(2,1)S(1)}, bf16[256,1024]{1,0:T(8,128)(2,1)S(1)}, u32[]{:S(2)}, u32[]{:S(2)}) collective-permute-start(bf16[256,1024]{1,0:T(8,128)(2,1)S(1)} %get-tuple-element.42), channel_id=1, source_target_pairs={{0,24},{1,25},{2,26},{3,27},{4,28},{5,29},{6,30},{7,31},{8,16},{9,... | collective-permute-start | bytes 1572872 | tf_op jit(solution)/shard_map/ppermute | solution.py:33
  155.5 9.9 %collective-permute-start.23 = (bf16[128,1024]{1,0:T(8,128)(2,1)S(1)}, bf16[128,1024]{1,0:T(8,128)(2,1)S(1)}, u32[]{:S(2)}, u32[]{:S(2)}) collective-permute-start(bf16[128,1024]{1,0:T(8,128)(2,1)S(1)} %get-tuple-element.44), channel_id=1, source_target_pairs={{0,8},{1,9},{2,10},{3,11},{4,12},{5,13},{6,14},{7,15},{8,0},{9,1},... | collective-permute-start | bytes 786440 | tf_op jit(solution)/shard_map/ppermute | solution.py:33
  165.5 14.6 %collective-permute-start.24 = (bf16[64,1024]{1,0:T(8,128)(2,1)S(1)}, bf16[64,1024]{1,0:T(8,128)(2,1)S(1)}, u32[]{:S(2)}, u32[]{:S(2)}) collective-permute-start(bf16[64,1024]{1,0:T(8,128)(2,1)S(1)} %get-tuple-element.46), channel_id=1, source_target_pairs={{0,96},{1,97},{2,98},{3,99},{4,100},{5,101},{6,102},{7,103},{8,104... | collective-permute-start | bytes 393224 | tf_op jit(solution)/shard_map/ppermute | solution.py:33
  169.9 32.8 %collective-permute-start.17 = (bf16[2,40,1024]{2,1,0:T(8,128)(2,1)S(1)}, bf16[2,40,1024]{2,1,0:T(8,128)(2,1)S(1)}, u32[]{:S(2)}, u32[]{:S(2)}) collective-permute-start(bf16[2,40,1024]{2,1,0:T(8,128)(2,1)S(1)} %get-tuple-element.33), channel_id=1, source_target_pairs={{0,1},{1,0},{2,3},{3,2},{4,5},{5,4},{6,7},{7,6},{8,9},{9,8},{10,11... | collective-permute-start | bytes 491528 | tf_op jit(solution)/shard_map/ppermute | solution.py:33
  172.8 29.9 %collective-permute-start.18 = (bf16[2,40,1024]{2,1,0:T(8,128)(2,1)S(1)}, bf16[2,40,1024]{2,1,0:T(8,128)(2,1)S(1)}, u32[]{:S(2)}, u32[]{:S(2)}) collective-permute-start(bf16[2,40,1024]{2,1,0:T(8,128)(2,1)S(1)} %get-tuple-element.34), channel_id=1, source_target_pairs={{0,2},{1,3},{2,0},{3,1},{4,6},{5,7},{6,4},{7,5},{8,10},{9,11},{10,... | collective-permute-start | bytes 491528 | tf_op jit(solution)/shard_map/ppermute | solution.py:33
  175.7 27.1 %collective-permute-start.19 = (bf16[2,40,1024]{2,1,0:T(8,128)(2,1)S(1)}, bf16[2,40,1024]{2,1,0:T(8,128)(2,1)S(1)}, u32[]{:S(2)}, u32[]{:S(2)}) collective-permute-start(bf16[2,40,1024]{2,1,0:T(8,128)(2,1)S(1)} %get-tuple-element.35), channel_id=1, source_target_pairs={{0,3},{1,2},{2,1},{3,0},{4,7},{5,6},{6,5},{7,4},{8,11},{9,10},{10,... | collective-permute-start | bytes 491528 | tf_op jit(solution)/shard_map/ppermute | solution.py:33
  186.3 14.5 %collective-permute-start.26 = (bf16[16,1024]{1,0:T(8,128)(2,1)S(1)}, bf16[16,1024]{1,0:T(8,128)(2,1)S(1)}, u32[]{:S(2)}, u32[]{:S(2)}) collective-permute-start(bf16[16,1024]{1,0:T(8,128)(2,1)S(1)} %get-tuple-element.50), channel_id=1, source_target_pairs={{0,128},{1,129},{2,130},{3,131},{4,132},{5,133},{6,134},{7,135},{8... | collective-permute-start | bytes 98312 | tf_op jit(solution)/shard_map/ppermute | solution.py:33
  200.8 9.5 %collective-permute-start.27 = (bf16[16,512]{1,0:T(8,128)(2,1)S(1)}, bf16[16,512]{1,0:T(8,128)(2,1)S(1)}, u32[]{:S(2)}, u32[]{:S(2)}) collective-permute-start(bf16[16,512]{1,0:T(8,128)(2,1)S(1)} %get-tuple-element.52), channel_id=1, source_target_pairs={{0,4},{1,5},{2,6},{3,7},{4,0},{5,1},{6,2},{7,3},{8,12},{9,13},{10,... | collective-permute-start | bytes 49160 | tf_op jit(solution)/shard_map/ppermute | solution.py:33
  (14 other events, 118.4 us)

commit v2 on v1

v2 whole, which is shorter than its diff:
```python
import functools

import jax
import jax.numpy as jnp
import numpy as np
from jax import lax
from jax.experimental import pallas as pl
from jax.experimental.pallas import tpu as pltpu
from jax.sharding import PartitionSpec as P

EPS = 1e-05
F32 = jnp.float32
BF16 = jnp.bfloat16
LINE = ("lon", "tp")
COUNT = 256
RING = (0, 1, 3, 2)
ROWS = 40


def dot(a, b):
    return lax.dot_general(a, b, (((1,), (0,)), ((), ())), preferred_element_type=F32)


def dot_nt(a, b):
    return lax.dot_general(a, b, (((1,), (1,)), ((), ())), preferred_element_type=F32)


def dot_tn(a, b):
    return lax.dot_general(a, b, (((0,), (0,)), ((), ())), preferred_element_type=F32)


def moved(value, target):
    return lax.ppermute(value, LINE, [(s, target(s)) for s in range(COUNT)])


def swapped(value, bits):
    return moved(value, lambda s: s ^ bits)


def across(value):
    return lax.ppermute(value, "lat", [(0, 1), (1, 0)])


def x_bits(index):
    return index << 3


def y_bits(index):
    return index << 5


Z_HALF = 4
Z_HI = 1 << 7


def along_z(value):
    pairs = []
    for lat, steps in ((0, 4), (1, -4)):
        for lon in range(32):
            for tp in range(8):
                z = ((lon >> 4) * 8 + tp + steps) % 16
                target = (z >> 3) * 128 + (lon & 15) * 8 + (z & 7)
                pairs.append((lat * COUNT + lon * 8 + tp, lat * COUNT + target))
    return lax.ppermute(value, ("lat", "lon", "tp"), pairs)


def ring(value, low, steps):
    return moved(value, lambda s: (s & ~(3 << low)) | ((((s >> low) + steps) & 3) << low))


def norm_rows(values):
    centred = values - jnp.mean(values, axis=-1, keepdims=True)
    variance = jnp.mean(centred * centred, axis=-1, keepdims=True)
    return centred * lax.rsqrt(variance + EPS)


def call(kernel, out_shape, *args, flops=0, scalars=0, after=(), **kw):
    specs = [
        pl.BlockSpec(memory_space=pltpu.SMEM if i < scalars else pltpu.VMEM)
        for i in range(len(args))
    ] + [pl.BlockSpec(memory_space=pl.ANY) for _ in after]

    def body(*refs):
        kernel(*refs[: len(args)], *refs[len(args) + len(after) :])

    size = sum(a.size * a.dtype.itemsize for a in args)
    return pl.pallas_call(
        body,
        out_shape=out_shape,
        in_specs=specs,
        out_specs=jax.tree.map(lambda _: pl.BlockSpec(memory_space=pltpu.VMEM), out_shape),
        compiler_params=pltpu.CompilerParams(vmem_limit_bytes=40 * 1024 * 1024),
        cost_estimate=pl.CostEstimate(flops=flops, bytes_accessed=size, transcendentals=0),
        name=kernel.__name__,
        **kw,
    )(*args, *after)


def shaped(shape, dtype=BF16):
    return jax.ShapeDtypeStruct(shape, dtype)


def merge_order():
    order = np.zeros((4 * ROWS, 144), np.float32)
    for quarter in range(4):
        d_lat, d_lon = quarter // 2, quarter % 2
        for token in range(36):
            lat, lon, lev = token // 6, token % 6 // 2, token % 2
            row, column = 2 * lat + d_lat, 2 * lon + d_lon
            source = 72 * (column // 3) + 6 * row + 2 * (column % 3) + lev
            order[ROWS * quarter + token, source] = 1.0
    return order.astype(jnp.bfloat16)


def attend_kernel(own0, own1, west, east, qkv, out_w, order, cot, result):
    tokens = jnp.concatenate(
        [r[...].astype(F32) for r in (own0, own1, west, east)], axis=0
    )
    normed = norm_rows(tokens).astype(BF16)
    packed = dot(normed, qkv[...]).astype(BF16).astype(F32)
    lane = lax.broadcasted_iota(jnp.int32, (1, 128), 1) // 32
    masks = [(lane == h).astype(F32) for h in range(4)]
    scale = 32 ** -0.5
    halves = []
    for window in range(2):
        rows = slice(72 * window, 72 * window + 72)
        other = slice(144 + 72 * window, 216 + 72 * window)
        parts = []
        for group in range(4):
            low = 128 * group
            queries = packed[rows, low : low + 128]
            keys = jnp.concatenate(
                [packed[rows, 512 + low : 640 + low], packed[other, 512 + low : 640 + low]], axis=0
            ).astype(BF16)
            values = jnp.concatenate(
                [packed[rows, 1024 + low : 1152 + low], packed[other, 1024 + low : 1152 + low]], axis=0
            ).astype(BF16)
            stacked = jnp.concatenate([queries * m for m in masks], axis=0).astype(BF16)
            scores = dot_nt(stacked, keys) * scale
            scores = scores - jnp.max(scores, axis=-1, keepdims=True)
            scores = jnp.exp(scores)
            probs = (scores / jnp.sum(scores, axis=-1, keepdims=True)).astype(BF16)
            mixed = dot(probs, values)
            total = mixed[0:72] * masks[0]
            for h in range(1, 4):
                total = total + mixed[72 * h : 72 * h + 72] * masks[h]
            parts.append(total)
        halves.append(jnp.concatenate(parts, axis=1))
    mixed = jnp.concatenate(halves, axis=0).astype(BF16)
    section = (tokens[0:144] + dot(mixed, out_w[...])).astype(BF16)
    spread = dot(order[...], section)
    wide = jnp.concatenate([spread[ROWS * q : ROWS * q + ROWS] for q in range(4)], axis=1)
    result[:, 0:2048] = norm_rows(wide).astype(BF16)
    result[:, 2048:3072] = cot[...]


def stacked_rows(blocks, columns):
    return jnp.concatenate([b[:, columns].astype(F32) for b in blocks], axis=0).astype(BF16)


def merge_kernel(b0, b1, b2, b3, own_w, far_w, result):
    blocks = stacked_rows((b0, b1, b2, b3), slice(0, 2048))
    for half, weight in enumerate((own_w, far_w)):
        part = dot(blocks, weight[...])
        for j in range(4):
            result[j, :, 128 * half : 128 * half + 128] = part[ROWS * j : ROWS * j + ROWS].astype(BF16)


def pack_kernel(place, merge, up, down, packed):
    r = place[0] * 4 + (place[1] & 1) * 2 + (place[2] & 1)
    for half in range(2):
        packed[half, 0:64, :] = up[pl.ds(pl.multiple_of(r * 128 + 64 * half, 64), 64), :]
        packed[half, 64:128, :] = down[pl.ds(pl.multiple_of(r * 64, 64), 64), 512 * half : 512 * half + 512]
        for q in range(4):
            row = pl.multiple_of(512 * q + r * 64 + 32 * half, 32)
            packed[half, 128:160, 128 * q : 128 * q + 128] = merge[pl.ds(row, 32), :]


def split_kernel(both, first, second):
    first[...] = both[0]
    second[...] = both[1]


def pair_kernel(first, other_first, second, other_second, firsts, seconds):
    firsts[0], firsts[1] = first[...], other_first[...]
    seconds[0], seconds[1] = second[...], other_second[...]


def four_kernel(a, b, c, d, result):
    for index, part in enumerate((a, b, c, d)):
        result[2 * index], result[2 * index + 1] = part[0], part[1]


def unpack_kernel(place, a, b, c, d, far, merge, up, down):
    for side in range(2):
        for y in range(2):
            for half in range(2):
                source = (a, b, c, d)[2 * y + half]
                for x in range(2):
                    r = (place[0] ^ side) * 4 + ((place[1] & 1) ^ y) * 2 + ((place[2] & 1) ^ x)
                    piece = far.at[4 * y + 2 * half + x] if side else source.at[x]
                    up[pl.ds(pl.multiple_of(r * 128 + 64 * half, 64), 64), :] = piece[0:64, :]
                    row = pl.multiple_of(r * 64, 64)
                    down[pl.ds(row, 64), 512 * half : 512 * half + 512] = piece[64:128, :]
                    for q in range(4):
                        at = pl.multiple_of(512 * q + r * 64 + 32 * half, 32)
                        merge[pl.ds(at, 32), :] = piece[128:160, 128 * q : 128 * q + 128]


def gelu_parts(values):
    cdf = 0.5 * (1.0 + lax.erf(values * np.float32(np.sqrt(0.5))))
    density = jnp.exp(-0.5 * values * values) * np.float32(1.0 / np.sqrt(2.0 * np.pi))
    return values * cdf, cdf + values * density


def hidden_kernel(
    place, m0, m1, m2, m3, up0, up1, far_cot, own_merged, bundle, slope, merged
):
    th, tl = place[3], place[4]
    for j, source in enumerate((m0, m1, m2, m3)):
        for half in range(2):
            column = ((th ^ half) * 4 + (tl ^ j)) * 128
            column = pl.multiple_of(column, 128)
            for block in range(4):
                merged[ROWS * block : ROWS * block + ROWS, pl.ds(column, 128)] = source[
                    block ^ j, :, 128 * half : 128 * half + 128
                ].astype(F32)
    own_merged[...] = merged[0:ROWS, :].astype(BF16)
    normed = norm_rows(merged[...]).astype(BF16)
    for half, up in enumerate((up0, up1)):
        columns = slice(512 * half, 512 * half + 512)
        value, rate = gelu_parts(dot(normed, up[...]))
        bundle[:, columns] = value.astype(BF16)
        slope[:, columns] = rate
    bundle[:, 1024:1536] = far_cot[...]


def feed_kernel(bundle, slope, b0, b1, b2, b3, up0, up1, down0, down1, s0, s1, s2, s3):
    cots = stacked_rows((b0, b1, b2, b3), slice(2048, 3072))
    partial, back = 0.0, 0.0
    for half, (up, down) in enumerate(((up0, down0), (up1, down1))):
        columns = slice(512 * half, 512 * half + 512)
        grad = (dot_nt(cots, down[...]) * slope[:, columns]).astype(BF16)
        partial = partial + dot(bundle[:, columns], down[...])
        back = back + dot_nt(grad, up[...])
    for j, sent in enumerate((s0, s1, s2, s3)):
        rows = slice(ROWS * j, ROWS * j + ROWS)
        sent[0] = partial[rows].astype(BF16)
        sent[1] = back[rows].astype(BF16)


def finish_kernel(merged, cot, s0, r1, r2, r3, coarse_out, grad_merged):
    merged_f = merged[...].astype(F32)
    summed = s0[0].astype(F32) + r1[0].astype(F32) + r2[0].astype(F32) + r3[0].astype(F32)
    coarse_out[...] = (merged_f + summed).astype(BF16)
    grad_normed = s0[1].astype(F32) + r1[1].astype(F32) + r2[1].astype(F32) + r3[1].astype(F32)
    centred = merged_f - jnp.mean(merged_f, axis=-1, keepdims=True)
    scale_inv = lax.rsqrt(jnp.mean(centred * centred, axis=-1, keepdims=True) + EPS)
    nhat = centred * scale_inv
    grad = cot[...].astype(F32) + scale_inv * (
        grad_normed
        - jnp.mean(grad_normed, axis=-1, keepdims=True)
        - nhat * jnp.mean(grad_normed * nhat, axis=-1, keepdims=True)
    )
    grad_merged[...] = grad.astype(BF16)


def column_kernel(place, b0, b1, b2, b3, near, far):
    cots = stacked_rows((b0, b1, b2, b3), slice(2048, 3072))
    lat, y, x, zh = place[0], place[1], place[2], place[5]
    source = lax.broadcasted_iota(jnp.int32, (512, 512), 0)
    target = lax.broadcasted_iota(jnp.int32, (512, 512), 1)
    x_part, y_part, z_part = target >> 7, (target >> 5) & 3, (target >> 4) & 1
    x_abs = (x_part ^ (x_part >> 1)) ^ x
    y_abs = (y_part ^ (y_part >> 1)) ^ y
    wanted = (((z_part ^ zh) * 4 + y_abs) * 4 + x_abs) * 16 + (target & 15)
    chosen = jnp.where(source == wanted, 1.0, 0.0).astype(BF16)
    low, high = cots[:, 0:512], cots[:, 512:1024]
    mine = jnp.where(lat == 0, low.astype(F32), high.astype(F32)).astype(BF16)
    theirs = jnp.where(lat == 0, high.astype(F32), low.astype(F32)).astype(BF16)
    near[...] = dot(mine, chosen).astype(BF16)
    far[...] = dot(theirs, chosen).astype(BF16)


def weight_kernel(near, near_hidden, far, kept, s1, s2, s3):
    rows = jnp.concatenate([near[...], far[:, 1024:1536]], axis=0)
    hidden = jnp.concatenate([near_hidden[:, 0:1024], far[:, 0:1024]], axis=0)
    total = dot_tn(rows, hidden)
    kept[...] = total[0:128]
    for part, sent in enumerate((s1, s2, s3)):
        sent[...] = total[128 * part + 128 : 128 * part + 256].astype(BF16)


def plus(kept, *got):
    total = kept[...]
    for g in got:
        total = total + g[...].astype(F32)
    return total


def x_sum_kernel(kept, g1, g2, g3, left, s1, s2, s3):
    total = plus(kept, g1, g2, g3)
    left[...] = total[0:32]
    for part, sent in enumerate((s1, s2, s3)):
        sent[...] = total[32 * part + 32 : 32 * part + 64].astype(BF16)


def y_sum_kernel(kept, g1, g2, g3, left, s1, s2, s3):
    total = plus(kept, g1, g2, g3)
    left[...] = total[0:16, 0:512]
    s1[...] = total[0:16, 512:1024].astype(BF16)
    s2[...] = total[16:32, 0:512].astype(BF16)
    s3[...] = total[16:32, 512:1024].astype(BF16)


def z_sum_kernel(kept, g1, g2, g3, result):
    result[...] = plus(kept, g1, g2, g3)


def token_rows(block):
    return block.transpose(1, 2, 0, 3).reshape(-1, block.shape[-1])


def on_device(fine_tokens, fine_qkv, fine_out, merge_weight, up_weight, down_weight, cotangent):
    lon, tp = lax.axis_index("lon"), lax.axis_index("tp")
    place = jnp.stack(
        [lax.axis_index("lat"), (lon >> 2) & 3, lon & 3, tp >> 2, tp & 3, lon >> 4]
    ).astype(jnp.int32)

    half, two = shaped((160, 512)), shaped((2, 160, 512))
    packed = call(pack_kernel, two, place, merge_weight, up_weight, down_weight, scalars=1)
    packed = along_z(packed)

    own0 = token_rows(fine_tokens[:, :, :3])
    own1 = token_rows(fine_tokens[:, :, 3:])
    west = moved(own1, lambda s: (s + 1) % COUNT)
    east = moved(own0, lambda s: (s - 1) % COUNT)
    cot = jnp.pad(token_rows(cotangent), ((0, ROWS - 36), (0, 0)))

    merged_in = call(
        attend_kernel, shaped((ROWS, 3072)), own0, own1, west, east, fine_qkv, fine_out,
        jnp.asarray(merge_order()), cot, flops=10**9,
    )
    p0, p1 = call(split_kernel, (half, half), packed, after=(merged_in,))
    o0, o1 = ring(p0, 3, 1), ring(p1, 3, -1)
    a0, a1 = call(pair_kernel, (two, two), p0, o0, p1, o1)
    ins = [merged_in] + [swapped(merged_in, j) for j in (1, 2, 3)]
    b0, b1 = ring(a0, 5, 1), ring(a1, 5, -1)
    near = call(four_kernel, shaped((8, 160, 512)), a0, a1, b0, b1, after=ins)
    far_merge, far_up, far_down = call(
        unpack_kernel,
        (shaped((2048, 128)), shaped((1024, 512)), shaped((512, 1024))),
        place, a0, a1, b0, b1, across(near), scalars=1,
    )
    near_cot, far_cot = call(
        column_kernel, (shaped((4 * ROWS, 512)), shaped((4 * ROWS, 512))), place, *ins, scalars=1, flops=10**8
    )

    columns = call(merge_kernel, shaped((4, ROWS, 256)), *ins, merge_weight, far_merge, flops=2 * 10**8)
    held = [columns] + [swapped(columns, j) for j in (1, 2, 3)]

    own_merged, bundle, slope = call(
        hidden_kernel,
        (shaped((ROWS, 1024)), shaped((4 * ROWS, 1536)), shaped((4 * ROWS, 1024), F32)),
        place, *held, up_weight, far_up, far_cot, scalars=1, flops=10**9,
        scratch_shapes=[pltpu.VMEM((4 * ROWS, 1024), F32)],
    )
    other = across(bundle)
    sent = call(
        feed_kernel, tuple(shaped((2, ROWS, 1024)) for _ in range(4)),
        bundle, slope, *ins, up_weight, far_up, down_weight, far_down, flops=2 * 10**9,
    )

    part = shaped((128, 1024))
    kept, *out = call(
        weight_kernel, (shaped((128, 1024), F32), part, part, part), near_cot, bundle, other,
        flops=3 * 10**8, after=sent[1:],
    )
    got = [swapped(o, x_bits(bits)) for o, bits in zip(out, RING[1:])]
    back = [swapped(sent[j], j) for j in (1, 2, 3)]
    part = shaped((32, 1024))
    kept, *out = call(
        x_sum_kernel, (shaped((32, 1024), F32), part, part, part), kept, *got, after=back
    )
    coarse_out, grad_merged = call(
        finish_kernel, (shaped((ROWS, 1024)), shaped((ROWS, 1024))), own_merged, cot, sent[0], *back
    )
    got = [swapped(o, y_bits(bits)) for o, bits in zip(out, RING[1:])]
    part = shaped((16, 512))
    kept, *out = call(
        y_sum_kernel, (shaped((16, 512), F32), part, part, part), kept, *got,
        after=(coarse_out, grad_merged),
    )
    got = [swapped(o, bits) for o, bits in zip(out, (Z_HALF, Z_HI, Z_HALF | Z_HI))]
    grad_down = call(z_sum_kernel, shaped((16, 512), F32), kept, *got).T

    def placed(rows):
        return rows[:36].reshape(6, 3, 2, 1024).transpose(2, 0, 1, 3)

    return placed(coarse_out), placed(grad_merged), grad_down


def solution(mesh):
    tokens = P(None, "lat", ("lon", "tp"), None)
    return jax.shard_map(
        on_device,
        mesh=mesh,
        in_specs=(tokens, P(), P(), P(None, "tp"), P(None, "tp"), P("tp", None), tokens),
        out_specs=(tokens, tokens, P("tp", ("lat", "lon"))),
        check_vma=False,
    )
```

time: 212 us -> 183 us (0.86)
  the two profiles are of different devices: /device:TPU:392 before, /device:TPU:32 now
where the time goes in v2:
time: 183 us; the launch traced here: 182 us
  starting transfers between devices  103 us (56%)
  waiting for transfers between devices  61.7 us (34%)
  Pallas kernels  10.9 us (6%)
  local copies, waits for them, and re-layouts  5.16 us (3%)
    ppermute x24, starting transfers between devices, moved(): return lax.ppermute(value, LINE, [(s, target(s)) for s in range(COUNT)])  89.6 us
    ppermute x24, waiting for transfers between devices, moved(): return lax.ppermute(value, LINE, [(s, target(s)) for s in range(COUNT)])  58.7 us
    pallas_call x15, Pallas kernels, call(): pl.pallas_call(body, out_shape=out_shape, in_specs=specs, out_specs=jax.t...  10.9 us
    ppermute x1, starting transfers between devices, along_z(): return lax.ppermute(value, ('lat', 'lon', 'tp'), pairs)  9.23 us
    ppermute x2, starting transfers between devices, across(): return lax.ppermute(value, 'lat', [(0, 1), (1, 0)])  3.98 us
  transfers between devices with their start and end apart: 27, of which 14 were waited for; matrix products, arithmetic and copies ran while one was open for 1% of the time, Pallas kernels for 4%

profile of v2, /device:TPU:32, one launch (start us, length us, event | category | flops | bytes accessed | tf_op | source)
XLA Modules:
  0.0 181.7 jit_solution(17122710557862150271)
XLA Ops:
  4.8 9.2 %collective-permute-start.5 = (bf16[2,160,512]{2,1,0:T(8,128)(2,1)S(1)}, bf16[2,160,512]{2,1,0:T(8,128)(2,1)S(1)}, u32[]{:S(2)}, u32[]{:S(2)}) collective-permute-start(bf16[2,160,512]{2,1,0:T(8,128)(2,1)S(1)} %pack_kernel.1), channel_id=1, source_target_pairs={{0,4},{1,5},{2,6},{3,7},{4,128},{5,129},{6,130},{7,131},{8,12},{9,... | collective-permute-start | bytes 983048 | tf_op jit(solution)/shard_map/ppermute | solution.py:64
  14.2 3.8 %collective-permute-start = (bf16[72,512]{1,0:T(8,128)(2,1)S(1)}, bf16[72,512]{1,0:T(8,128)(2,1)S(1)}, u32[]{:S(2)}, u32[]{:S(2)}) collective-permute-start(bf16[72,512]{1,0:T(8,128)(2,1)S(1)} %reshape.22.refs_1_), channel_id=1, source_target_pairs={{0,1},{1,2},{2,3},{3,4},{4,5},{5,6},{6,7},{7,8},{8,9},{9,10},{10,1... | collective-permute-start | bytes 221192 | tf_op jit(solution)/shard_map/ppermute | solution.py:33
  20.2 7.7 %collective-permute-done.refs_2_ = bf16[72,512]{1,0:T(8,128)(2,1)S(1)} collective-permute-done((bf16[72,512]{1,0:T(8,128)(2,1)S(1)}, bf16[72,512]{1,0:T(8,128)(2,1)S(1)}, u32[]{:S(2)}, u32[]{:S(2)}) %collective-permute-start) | collective-permute-done | bytes 73760 | tf_op jit(solution)/shard_map/ppermute | solution.py:33
  33.4 3.4 %collective-permute-start.6 = (bf16[160,512]{1,0:T(8,128)(2,1)S(1)}, bf16[160,512]{1,0:T(8,128)(2,1)S(1)}, u32[]{:S(2)}, u32[]{:S(2)}) collective-permute-start(bf16[160,512]{1,0:T(8,128)(2,1)S(1)} %get-tuple-element.33.refs_0_), channel_id=1, source_target_pairs={{0,8},{1,9},{2,10},{3,11},{4,12},{5,13},{6,14},{7,15},{8,16},{9,17... | collective-permute-start | bytes 491528 | tf_op jit(solution)/shard_map/ppermute | solution.py:33
  36.8 3.7 %collective-permute-start.7 = (bf16[160,512]{1,0:T(8,128)(2,1)S(1)}, bf16[160,512]{1,0:T(8,128)(2,1)S(1)}, u32[]{:S(2)}, u32[]{:S(2)}) collective-permute-start(bf16[160,512]{1,0:T(8,128)(2,1)S(1)} %get-tuple-element.34.refs_2_), channel_id=1, source_target_pairs={{0,24},{1,25},{2,26},{3,27},{4,28},{5,29},{6,30},{7,31},{8,0},{9,1... | collective-permute-start | bytes 491528 | tf_op jit(solution)/shard_map/ppermute | solution.py:33
  45.5 3.5 %collective-permute-start.8 = (bf16[2,160,512]{2,1,0:T(8,128)(2,1)S(1)}, bf16[2,160,512]{2,1,0:T(8,128)(2,1)S(1)}, u32[]{:S(2)}, u32[]{:S(2)}) collective-permute-start(bf16[2,160,512]{2,1,0:T(8,128)(2,1)S(1)} %get-tuple-element.35.refs_0_.refs_1_), channel_id=1, source_target_pairs={{0,32},{1,33},{2,34},{3,35},{4,36},{5,37},{6,38},{7,39},{8,40},{9,... | collective-permute-start | bytes 983048 | tf_op jit(solution)/shard_map/ppermute | solution.py:33
  49.0 3.6 %collective-permute-start.9 = (bf16[2,160,512]{2,1,0:T(8,128)(2,1)S(1)}, bf16[2,160,512]{2,1,0:T(8,128)(2,1)S(1)}, u32[]{:S(2)}, u32[]{:S(2)}) collective-permute-start(bf16[2,160,512]{2,1,0:T(8,128)(2,1)S(1)} %get-tuple-element.36.refs_1_.refs_2_), channel_id=1, source_target_pairs={{0,96},{1,97},{2,98},{3,99},{4,100},{5,101},{6,102},{7,103},{8,104... | collective-permute-start | bytes 983048 | tf_op jit(solution)/shard_map/ppermute | solution.py:33
  52.6 8.2 %collective-permute-start.2 = (bf16[40,3072]{1,0:T(8,128)(2,1)S(1)}, bf16[40,3072]{1,0:T(8,128)(2,1)S(1)}, u32[]{:S(2)}, u32[]{:S(2)}) collective-permute-start(bf16[40,3072]{1,0:T(8,128)(2,1)S(1)} %attend_kernel.1.refs_1_.refs_4_.refs_0_.refs_2_), channel_id=1, source_target_pairs={{0,1},{1,0},{2,3},{3,2},{4,5},{5,4},{6,7},{7,6},{8,9},{9,8},{10,11... | collective-permute-start | bytes 737288 | tf_op jit(solution)/shard_map/ppermute | solution.py:33
  67.6 12.0 %collective-permute-done.3.refs_6_.refs_2_.refs_3_.refs_4_ = bf16[40,3072]{1,0:T(8,128)(2,1)S(1)} collective-permute-done((bf16[40,3072]{1,0:T(8,128)(2,1)S(1)}, bf16[40,3072]{1,0:T(8,128)(2,1)S(1)}, u32[]{:S(2)}, u32[]{:S(2)}) %collective-permute-start.3) | collective-permute-done | bytes 245792 | tf_op jit(solution)/shard_map/ppermute | solution.py:33
  79.6 5.6 %collective-permute-done.4.refs_7_.refs_3_.refs_4_.refs_5_ = bf16[40,3072]{1,0:T(8,128)(2,1)S(1)} collective-permute-done((bf16[40,3072]{1,0:T(8,128)(2,1)S(1)}, bf16[40,3072]{1,0:T(8,128)(2,1)S(1)}, u32[]{:S(2)}, u32[]{:S(2)}) %collective-permute-start.4) | collective-permute-done | bytes 245792 | tf_op jit(solution)/shard_map/ppermute | solution.py:33
  93.6 3.9 %collective-permute-start.12 = (bf16[4,40,256]{2,1,0:T(8,128)(2,1)S(1)}, bf16[4,40,256]{2,1,0:T(8,128)(2,1)S(1)}, u32[]{:S(2)}, u32[]{:S(2)}) collective-permute-start(bf16[4,40,256]{2,1,0:T(8,128)(2,1)S(1)} %merge_kernel.1.refs_1_), channel_id=1, source_target_pairs={{0,2},{1,3},{2,0},{3,1},{4,6},{5,7},{6,4},{7,5},{8,10},{9,11},{10,... | collective-permute-start | bytes 245768 | tf_op jit(solution)/shard_map/ppermute | solution.py:33
  97.5 3.4 %collective-permute-start.13 = (bf16[4,40,256]{2,1,0:T(8,128)(2,1)S(1)}, bf16[4,40,256]{2,1,0:T(8,128)(2,1)S(1)}, u32[]{:S(2)}, u32[]{:S(2)}) collective-permute-start(bf16[4,40,256]{2,1,0:T(8,128)(2,1)S(1)} %merge_kernel.1.refs_1_), channel_id=1, source_target_pairs={{0,3},{1,2},{2,1},{3,0},{4,7},{5,6},{6,5},{7,4},{8,11},{9,10},{10,... | collective-permute-start | bytes 245768 | tf_op jit(solution)/shard_map/ppermute | solution.py:33
  101.9 4.2 %collective-permute-done.13.refs_4_ = bf16[4,40,256]{2,1,0:T(8,128)(2,1)S(1)} collective-permute-done((bf16[4,40,256]{2,1,0:T(8,128)(2,1)S(1)}, bf16[4,40,256]{2,1,0:T(8,128)(2,1)S(1)}, u32[]{:S(2)}, u32[]{:S(2)}) %collective-permute-start.13) | collective-permute-done | bytes 81952 | tf_op jit(solution)/shard_map/ppermute | solution.py:33
  116.0 5.6 %collective-permute-start.19 = (bf16[128,1024]{1,0:T(8,128)(2,1)S(1)}, bf16[128,1024]{1,0:T(8,128)(2,1)S(1)}, u32[]{:S(2)}, u32[]{:S(2)}) collective-permute-start(bf16[128,1024]{1,0:T(8,128)(2,1)S(1)} %get-tuple-element.53), channel_id=1, source_target_pairs={{0,24},{1,25},{2,26},{3,27},{4,28},{5,29},{6,30},{7,31},{8,16},{9,... | collective-permute-start | bytes 786440 | tf_op jit(solution)/shard_map/ppermute | solution.py:33
  125.0 3.9 %collective-permute-start.15 = (bf16[2,40,1024]{2,1,0:T(8,128)(2,1)S(1)}, bf16[2,40,1024]{2,1,0:T(8,128)(2,1)S(1)}, u32[]{:S(2)}, u32[]{:S(2)}) collective-permute-start(bf16[2,40,1024]{2,1,0:T(8,128)(2,1)S(1)} %get-tuple-element.46.refs_4_), channel_id=1, source_target_pairs={{0,2},{1,3},{2,0},{3,1},{4,6},{5,7},{6,4},{7,5},{8,10},{9,11},{10,... | collective-permute-start | bytes 491528 | tf_op jit(solution)/shard_map/ppermute | solution.py:33
  132.3 6.9 %collective-permute-done.15.refs_4_.refs_5_ = bf16[2,40,1024]{2,1,0:T(8,128)(2,1)S(1)} collective-permute-done((bf16[2,40,1024]{2,1,0:T(8,128)(2,1)S(1)}, bf16[2,40,1024]{2,1,0:T(8,128)(2,1)S(1)}, u32[]{:S(2)}, u32[]{:S(2)}) %collective-permute-start.15) | collective-permute-done | bytes 163872 | tf_op jit(solution)/shard_map/ppermute | solution.py:33
  139.3 5.1 %collective-permute-done.16.refs_5_.refs_6_ = bf16[2,40,1024]{2,1,0:T(8,128)(2,1)S(1)} collective-permute-done((bf16[2,40,1024]{2,1,0:T(8,128)(2,1)S(1)}, bf16[2,40,1024]{2,1,0:T(8,128)(2,1)S(1)}, u32[]{:S(2)}, u32[]{:S(2)}) %collective-permute-start.16) | collective-permute-done | bytes 163872 | tf_op jit(solution)/shard_map/ppermute | solution.py:33
  146.5 4.0 %collective-permute-start.22 = (bf16[32,1024]{1,0:T(8,128)(2,1)S(1)}, bf16[32,1024]{1,0:T(8,128)(2,1)S(1)}, u32[]{:S(2)}, u32[]{:S(2)}) collective-permute-start(bf16[32,1024]{1,0:T(8,128)(2,1)S(1)} %get-tuple-element.57), channel_id=1, source_target_pairs={{0,96},{1,97},{2,98},{3,99},{4,100},{5,101},{6,102},{7,103},{8,104... | collective-permute-start | bytes 196616 | tf_op jit(solution)/shard_map/ppermute | solution.py:33
  150.4 3.9 %collective-permute-start.23 = (bf16[32,1024]{1,0:T(8,128)(2,1)S(1)}, bf16[32,1024]{1,0:T(8,128)(2,1)S(1)}, u32[]{:S(2)}, u32[]{:S(2)}) collective-permute-start(bf16[32,1024]{1,0:T(8,128)(2,1)S(1)} %get-tuple-element.58), channel_id=1, source_target_pairs={{0,64},{1,65},{2,66},{3,67},{4,68},{5,69},{6,70},{7,71},{8,72},{9,... | collective-permute-start | bytes 196616 | tf_op jit(solution)/shard_map/ppermute | solution.py:33
  154.7 3.4 %collective-permute-done.23.refs_3_ = bf16[32,1024]{1,0:T(8,128)(2,1)S(1)} collective-permute-done((bf16[32,1024]{1,0:T(8,128)(2,1)S(1)}, bf16[32,1024]{1,0:T(8,128)(2,1)S(1)}, u32[]{:S(2)}, u32[]{:S(2)}) %collective-permute-start.23) | collective-permute-done | bytes 65568 | tf_op jit(solution)/shard_map/ppermute | solution.py:33
  158.1 4.5 %collective-permute-start.24 = (bf16[16,512]{1,0:T(8,128)(2,1)S(1)}, bf16[16,512]{1,0:T(8,128)(2,1)S(1)}, u32[]{:S(2)}, u32[]{:S(2)}) collective-permute-start(bf16[16,512]{1,0:T(8,128)(2,1)S(1)} %get-tuple-element.60), channel_id=1, source_target_pairs={{0,4},{1,5},{2,6},{3,7},{4,0},{5,1},{6,2},{7,3},{8,12},{9,13},{10,... | collective-permute-start | bytes 49160 | tf_op jit(solution)/shard_map/ppermute | solution.py:33
  162.6 8.8 %collective-permute-start.25 = (bf16[16,512]{1,0:T(8,128)(2,1)S(1)}, bf16[16,512]{1,0:T(8,128)(2,1)S(1)}, u32[]{:S(2)}, u32[]{:S(2)}) collective-permute-start(bf16[16,512]{1,0:T(8,128)(2,1)S(1)} %get-tuple-element.61), channel_id=1, source_target_pairs={{0,128},{1,129},{2,130},{3,131},{4,132},{5,133},{6,134},{7,135},{8... | collective-permute-start | bytes 49160 | tf_op jit(solution)/shard_map/ppermute | solution.py:33
  171.4 3.8 %collective-permute-start.26 = (bf16[16,512]{1,0:T(8,128)(2,1)S(1)}, bf16[16,512]{1,0:T(8,128)(2,1)S(1)}, u32[]{:S(2)}, u32[]{:S(2)}) collective-permute-start(bf16[16,512]{1,0:T(8,128)(2,1)S(1)} %get-tuple-element.62), channel_id=1, source_target_pairs={{0,132},{1,133},{2,134},{3,135},{4,128},{5,129},{6,130},{7,131},{8... | collective-permute-start | bytes 49160 | tf_op jit(solution)/shard_map/ppermute | solution.py:33
  177.0 4.0 %collective-permute-done.26.refs_3_ = bf16[16,512]{1,0:T(8,128)(2,1)S(1)} collective-permute-done((bf16[16,512]{1,0:T(8,128)(2,1)S(1)}, bf16[16,512]{1,0:T(8,128)(2,1)S(1)}, u32[]{:S(2)}, u32[]{:S(2)}) %collective-permute-start.26) | collective-permute-done | bytes 16416 | tf_op jit(solution)/shard_map/ppermute | solution.py:33
  (75 shorter events, 54.5 us)
Async XLA Ops:
  4.8 28.5 %collective-permute-start.5 = (bf16[2,160,512]{2,1,0:T(8,128)(2,1)S(1)}, bf16[2,160,512]{2,1,0:T(8,128)(2,1)S(1)}, u32[]{:S(2)}, u32[]{:S(2)}) collective-permute-start(bf16[2,160,512]{2,1,0:T(8,128)(2,1)S(1)} %pack_kernel.1), channel_id=1, source_target_pairs={{0,4},{1,5},{2,6},{3,7},{4,128},{5,129},{6,130},{7,131},{8,12},{9,... | collective-permute-start | bytes 983048 | tf_op jit(solution)/shard_map/ppermute | solution.py:64
  14.2 13.7 %collective-permute-start = (bf16[72,512]{1,0:T(8,128)(2,1)S(1)}, bf16[72,512]{1,0:T(8,128)(2,1)S(1)}, u32[]{:S(2)}, u32[]{:S(2)}) collective-permute-start(bf16[72,512]{1,0:T(8,128)(2,1)S(1)} %reshape.22.refs_1_), channel_id=1, source_target_pairs={{0,1},{1,2},{2,3},{3,4},{4,5},{5,6},{6,7},{7,8},{8,9},{9,10},{10,1... | collective-permute-start | bytes 221192 | tf_op jit(solution)/shard_map/ppermute | solution.py:33
  18.1 12.5 %collective-permute-start.1 = (bf16[72,512]{1,0:T(8,128)(2,1)S(1)}, bf16[72,512]{1,0:T(8,128)(2,1)S(1)}, u32[]{:S(2)}, u32[]{:S(2)}) collective-permute-start(bf16[72,512]{1,0:T(8,128)(2,1)S(1)} %reshape.21.refs_0_), channel_id=1, source_target_pairs={{0,255},{1,0},{2,1},{3,2},{4,3},{5,4},{6,5},{7,6},{8,7},{9,8},{10,... | collective-permute-start | bytes 221192 | tf_op jit(solution)/shard_map/ppermute | solution.py:33
  33.4 9.7 %collective-permute-start.6 = (bf16[160,512]{1,0:T(8,128)(2,1)S(1)}, bf16[160,512]{1,0:T(8,128)(2,1)S(1)}, u32[]{:S(2)}, u32[]{:S(2)}) collective-permute-start(bf16[160,512]{1,0:T(8,128)(2,1)S(1)} %get-tuple-element.33.refs_0_), channel_id=1, source_target_pairs={{0,8},{1,9},{2,10},{3,11},{4,12},{5,13},{6,14},{7,15},{8,16},{9,17... | collective-permute-start | bytes 491528 | tf_op jit(solution)/shard_map/ppermute | solution.py:33
  36.8 8.7 %collective-permute-start.7 = (bf16[160,512]{1,0:T(8,128)(2,1)S(1)}, bf16[160,512]{1,0:T(8,128)(2,1)S(1)}, u32[]{:S(2)}, u32[]{:S(2)}) collective-permute-start(bf16[160,512]{1,0:T(8,128)(2,1)S(1)} %get-tuple-element.34.refs_2_), channel_id=1, source_target_pairs={{0,24},{1,25},{2,26},{3,27},{4,28},{5,29},{6,30},{7,31},{8,0},{9,1... | collective-permute-start | bytes 491528 | tf_op jit(solution)/shard_map/ppermute | solution.py:33
  45.5 39.7 %collective-permute-start.8 = (bf16[2,160,512]{2,1,0:T(8,128)(2,1)S(1)}, bf16[2,160,512]{2,1,0:T(8,128)(2,1)S(1)}, u32[]{:S(2)}, u32[]{:S(2)}) collective-permute-start(bf16[2,160,512]{2,1,0:T(8,128)(2,1)S(1)} %get-tuple-element.35.refs_0_.refs_1_), channel_id=1, source_target_pairs={{0,32},{1,33},{2,34},{3,35},{4,36},{5,37},{6,38},{7,39},{8,40},{9,... | collective-permute-start | bytes 983048 | tf_op jit(solution)/shard_map/ppermute | solution.py:33
  49.0 36.2 %collective-permute-start.9 = (bf16[2,160,512]{2,1,0:T(8,128)(2,1)S(1)}, bf16[2,160,512]{2,1,0:T(8,128)(2,1)S(1)}, u32[]{:S(2)}, u32[]{:S(2)}) collective-permute-start(bf16[2,160,512]{2,1,0:T(8,128)(2,1)S(1)} %get-tuple-element.36.refs_1_.refs_2_), channel_id=1, source_target_pairs={{0,96},{1,97},{2,98},{3,99},{4,100},{5,101},{6,102},{7,103},{8,104... | collective-permute-start | bytes 983048 | tf_op jit(solution)/shard_map/ppermute | solution.py:33
  52.6 15.0 %collective-permute-start.2 = (bf16[40,3072]{1,0:T(8,128)(2,1)S(1)}, bf16[40,3072]{1,0:T(8,128)(2,1)S(1)}, u32[]{:S(2)}, u32[]{:S(2)}) collective-permute-start(bf16[40,3072]{1,0:T(8,128)(2,1)S(1)} %attend_kernel.1.refs_1_.refs_4_.refs_0_.refs_2_), channel_id=1, source_target_pairs={{0,1},{1,0},{2,3},{3,2},{4,5},{5,4},{6,7},{7,6},{8,9},{9,8},{10,11... | collective-permute-start | bytes 737288 | tf_op jit(solution)/shard_map/ppermute | solution.py:33
  60.8 18.9 %collective-permute-start.3 = (bf16[40,3072]{1,0:T(8,128)(2,1)S(1)}, bf16[40,3072]{1,0:T(8,128)(2,1)S(1)}, u32[]{:S(2)}, u32[]{:S(2)}) collective-permute-start(bf16[40,3072]{1,0:T(8,128)(2,1)S(1)} %attend_kernel.1.refs_1_.refs_4_.refs_0_.refs_2_), channel_id=1, source_target_pairs={{0,2},{1,3},{2,0},{3,1},{4,6},{5,7},{6,4},{7,5},{8,10},{9,11},{10,... | collective-permute-start | bytes 737288 | tf_op jit(solution)/shard_map/ppermute | solution.py:33
  62.7 22.5 %collective-permute-start.4 = (bf16[40,3072]{1,0:T(8,128)(2,1)S(1)}, bf16[40,3072]{1,0:T(8,128)(2,1)S(1)}, u32[]{:S(2)}, u32[]{:S(2)}) collective-permute-start(bf16[40,3072]{1,0:T(8,128)(2,1)S(1)} %attend_kernel.1.refs_1_.refs_4_.refs_0_.refs_2_), channel_id=1, source_target_pairs={{0,3},{1,2},{2,1},{3,0},{4,7},{5,6},{6,5},{7,4},{8,11},{9,10},{10,... | collective-permute-start | bytes 737288 | tf_op jit(solution)/shard_map/ppermute | solution.py:33
  91.7 10.2 %collective-permute-start.11 = (bf16[4,40,256]{2,1,0:T(8,128)(2,1)S(1)}, bf16[4,40,256]{2,1,0:T(8,128)(2,1)S(1)}, u32[]{:S(2)}, u32[]{:S(2)}) collective-permute-start(bf16[4,40,256]{2,1,0:T(8,128)(2,1)S(1)} %merge_kernel.1.refs_1_), channel_id=1, source_target_pairs={{0,1},{1,0},{2,3},{3,2},{4,5},{5,4},{6,7},{7,6},{8,9},{9,8},{10,11... | collective-permute-start | bytes 245768 | tf_op jit(solution)/shard_map/ppermute | solution.py:33
  93.6 8.3 %collective-permute-start.12 = (bf16[4,40,256]{2,1,0:T(8,128)(2,1)S(1)}, bf16[4,40,256]{2,1,0:T(8,128)(2,1)S(1)}, u32[]{:S(2)}, u32[]{:S(2)}) collective-permute-start(bf16[4,40,256]{2,1,0:T(8,128)(2,1)S(1)} %merge_kernel.1.refs_1_), channel_id=1, source_target_pairs={{0,2},{1,3},{2,0},{3,1},{4,6},{5,7},{6,4},{7,5},{8,10},{9,11},{10,... | collective-permute-start | bytes 245768 | tf_op jit(solution)/shard_map/ppermute | solution.py:33
  97.5 8.7 %collective-permute-start.13 = (bf16[4,40,256]{2,1,0:T(8,128)(2,1)S(1)}, bf16[4,40,256]{2,1,0:T(8,128)(2,1)S(1)}, u32[]{:S(2)}, u32[]{:S(2)}) collective-permute-start(bf16[4,40,256]{2,1,0:T(8,128)(2,1)S(1)} %merge_kernel.1.refs_1_), channel_id=1, source_target_pairs={{0,3},{1,2},{2,1},{3,0},{4,7},{5,6},{6,5},{7,4},{8,11},{9,10},{10,... | collective-permute-start | bytes 245768 | tf_op jit(solution)/shard_map/ppermute | solution.py:33
  111.4 17.5 %collective-permute-start.14 = (bf16[2,40,1024]{2,1,0:T(8,128)(2,1)S(1)}, bf16[2,40,1024]{2,1,0:T(8,128)(2,1)S(1)}, u32[]{:S(2)}, u32[]{:S(2)}) collective-permute-start(bf16[2,40,1024]{2,1,0:T(8,128)(2,1)S(1)} %get-tuple-element.45.refs_3_), channel_id=1, source_target_pairs={{0,1},{1,0},{2,3},{3,2},{4,5},{5,4},{6,7},{7,6},{8,9},{9,8},{10,11... | collective-permute-start | bytes 491528 | tf_op jit(solution)/shard_map/ppermute | solution.py:33
  114.1 30.3 %collective-permute-start.18 = (bf16[128,1024]{1,0:T(8,128)(2,1)S(1)}, bf16[128,1024]{1,0:T(8,128)(2,1)S(1)}, u32[]{:S(2)}, u32[]{:S(2)}) collective-permute-start(bf16[128,1024]{1,0:T(8,128)(2,1)S(1)} %get-tuple-element.52), channel_id=1, source_target_pairs={{0,8},{1,9},{2,10},{3,11},{4,12},{5,13},{6,14},{7,15},{8,0},{9,1},... | collective-permute-start | bytes 786440 | tf_op jit(solution)/shard_map/ppermute | solution.py:33
  116.0 28.4 %collective-permute-start.19 = (bf16[128,1024]{1,0:T(8,128)(2,1)S(1)}, bf16[128,1024]{1,0:T(8,128)(2,1)S(1)}, u32[]{:S(2)}, u32[]{:S(2)}) collective-permute-start(bf16[128,1024]{1,0:T(8,128)(2,1)S(1)} %get-tuple-element.53), channel_id=1, source_target_pairs={{0,24},{1,25},{2,26},{3,27},{4,28},{5,29},{6,30},{7,31},{8,16},{9,... | collective-permute-start | bytes 786440 | tf_op jit(solution)/shard_map/ppermute | solution.py:33
  121.7 22.8 %collective-permute-start.20 = (bf16[128,1024]{1,0:T(8,128)(2,1)S(1)}, bf16[128,1024]{1,0:T(8,128)(2,1)S(1)}, u32[]{:S(2)}, u32[]{:S(2)}) collective-permute-start(bf16[128,1024]{1,0:T(8,128)(2,1)S(1)} %get-tuple-element.54), channel_id=1, source_target_pairs={{0,16},{1,17},{2,18},{3,19},{4,20},{5,21},{6,22},{7,23},{8,24},{9,... | collective-permute-start | bytes 786440 | tf_op jit(solution)/shard_map/ppermute | solution.py:33
  125.0 14.2 %collective-permute-start.15 = (bf16[2,40,1024]{2,1,0:T(8,128)(2,1)S(1)}, bf16[2,40,1024]{2,1,0:T(8,128)(2,1)S(1)}, u32[]{:S(2)}, u32[]{:S(2)}) collective-permute-start(bf16[2,40,1024]{2,1,0:T(8,128)(2,1)S(1)} %get-tuple-element.46.refs_4_), channel_id=1, source_target_pairs={{0,2},{1,3},{2,0},{3,1},{4,6},{5,7},{6,4},{7,5},{8,10},{9,11},{10,... | collective-permute-start | bytes 491528 | tf_op jit(solution)/shard_map/ppermute | solution.py:33
  129.0 15.4 %collective-permute-start.16 = (bf16[2,40,1024]{2,1,0:T(8,128)(2,1)S(1)}, bf16[2,40,1024]{2,1,0:T(8,128)(2,1)S(1)}, u32[]{:S(2)}, u32[]{:S(2)}) collective-permute-start(bf16[2,40,1024]{2,1,0:T(8,128)(2,1)S(1)} %get-tuple-element.47.refs_5_), channel_id=1, source_target_pairs={{0,3},{1,2},{2,1},{3,0},{4,7},{5,6},{6,5},{7,4},{8,11},{9,10},{10,... | collective-permute-start | bytes 491528 | tf_op jit(solution)/shard_map/ppermute | solution.py:33
  144.5 10.2 %collective-permute-start.21 = (bf16[32,1024]{1,0:T(8,128)(2,1)S(1)}, bf16[32,1024]{1,0:T(8,128)(2,1)S(1)}, u32[]{:S(2)}, u32[]{:S(2)}) collective-permute-start(bf16[32,1024]{1,0:T(8,128)(2,1)S(1)} %get-tuple-element.56), channel_id=1, source_target_pairs={{0,32},{1,33},{2,34},{3,35},{4,36},{5,37},{6,38},{7,39},{8,40},{9,... | collective-permute-start | bytes 196616 | tf_op jit(solution)/shard_map/ppermute | solution.py:33
  146.5 8.3 %collective-permute-start.22 = (bf16[32,1024]{1,0:T(8,128)(2,1)S(1)}, bf16[32,1024]{1,0:T(8,128)(2,1)S(1)}, u32[]{:S(2)}, u32[]{:S(2)}) collective-permute-start(bf16[32,1024]{1,0:T(8,128)(2,1)S(1)} %get-tuple-element.57), channel_id=1, source_target_pairs={{0,96},{1,97},{2,98},{3,99},{4,100},{5,101},{6,102},{7,103},{8,104... | collective-permute-start | bytes 196616 | tf_op jit(solution)/shard_map/ppermute | solution.py:33
  158.1 18.4 %collective-permute-start.24 = (bf16[16,512]{1,0:T(8,128)(2,1)S(1)}, bf16[16,512]{1,0:T(8,128)(2,1)S(1)}, u32[]{:S(2)}, u32[]{:S(2)}) collective-permute-start(bf16[16,512]{1,0:T(8,128)(2,1)S(1)} %get-tuple-element.60), channel_id=1, source_target_pairs={{0,4},{1,5},{2,6},{3,7},{4,0},{5,1},{6,2},{7,3},{8,12},{9,13},{10,... | collective-permute-start | bytes 49160 | tf_op jit(solution)/shard_map/ppermute | solution.py:33
  162.6 14.4 %collective-permute-start.25 = (bf16[16,512]{1,0:T(8,128)(2,1)S(1)}, bf16[16,512]{1,0:T(8,128)(2,1)S(1)}, u32[]{:S(2)}, u32[]{:S(2)}) collective-permute-start(bf16[16,512]{1,0:T(8,128)(2,1)S(1)} %get-tuple-element.61), channel_id=1, source_target_pairs={{0,128},{1,129},{2,130},{3,131},{4,132},{5,133},{6,134},{7,135},{8... | collective-permute-start | bytes 49160 | tf_op jit(solution)/shard_map/ppermute | solution.py:33
  171.4 9.6 %collective-permute-start.26 = (bf16[16,512]{1,0:T(8,128)(2,1)S(1)}, bf16[16,512]{1,0:T(8,128)(2,1)S(1)}, u32[]{:S(2)}, u32[]{:S(2)}) collective-permute-start(bf16[16,512]{1,0:T(8,128)(2,1)S(1)} %get-tuple-element.62), channel_id=1, source_target_pairs={{0,132},{1,133},{2,134},{3,135},{4,128},{5,129},{6,130},{7,131},{8... | collective-permute-start | bytes 49160 | tf_op jit(solution)/shard_map/ppermute | solution.py:33
  (14 other events, 151.1 us)

commit v3 on v2

v3 whole, which is shorter than its diff:
```python
import jax
import jax.numpy as jnp
import numpy as np
from jax import lax
from jax.experimental import pallas as pl
from jax.experimental.pallas import tpu as pltpu
from jax.sharding import Mesh, PartitionSpec as P

EPS = 1e-05
F32 = jnp.float32
BF16 = jnp.bfloat16
AXES = ("lat", "z_hi", "y", "x", "z_half", "z_near")
LINE = AXES[1:]
COUNT = 256
ROWS = 40


def dot(a, b):
    return lax.dot_general(a, b, (((1,), (0,)), ((), ())), preferred_element_type=F32)


def dot_nt(a, b):
    return lax.dot_general(a, b, (((1,), (1,)), ((), ())), preferred_element_type=F32)


def dot_tn(a, b):
    return lax.dot_general(a, b, (((0,), (0,)), ((), ())), preferred_element_type=F32)


def moved(value, target):
    return lax.ppermute(value, LINE, [(s, target(s)) for s in range(COUNT)])


def swapped(value, bits):
    return moved(value, lambda s: s ^ bits)


def across(value):
    return lax.ppermute(value, "lat", [(0, 1), (1, 0)])


def along_z(value):
    pairs = []
    for lat, steps in ((0, 4), (1, -4)):
        for lon in range(32):
            for tp in range(8):
                z = ((lon >> 4) * 8 + tp + steps) % 16
                target = (z >> 3) * 128 + (lon & 15) * 8 + (z & 7)
                pairs.append((lat * COUNT + lon * 8 + tp, lat * COUNT + target))
    return lax.ppermute(value, AXES, pairs)


def exchanged(value, axes):
    return lax.all_to_all(value, axes, 0, 0)


def norm_rows(values):
    centred = values - jnp.mean(values, axis=-1, keepdims=True)
    variance = jnp.mean(centred * centred, axis=-1, keepdims=True)
    return centred * lax.rsqrt(variance + EPS)


def call(kernel, out_shape, *args, flops=0, scalars=0, after=(), **kw):
    specs = [
        pl.BlockSpec(memory_space=pltpu.SMEM if i < scalars else pltpu.VMEM)
        for i in range(len(args))
    ] + [pl.BlockSpec(memory_space=pl.ANY) for _ in after]

    def body(*refs):
        kernel(*refs[: len(args)], *refs[len(args) + len(after) :])

    size = sum(a.size * a.dtype.itemsize for a in args)
    return pl.pallas_call(
        body,
        out_shape=out_shape,
        in_specs=specs,
        out_specs=jax.tree.map(lambda _: pl.BlockSpec(memory_space=pltpu.VMEM), out_shape),
        compiler_params=pltpu.CompilerParams(vmem_limit_bytes=40 * 1024 * 1024),
        cost_estimate=pl.CostEstimate(flops=flops, bytes_accessed=size, transcendentals=0),
        name=kernel.__name__,
        **kw,
    )(*args, *after)


def shaped(shape, dtype=BF16):
    return jax.ShapeDtypeStruct(shape, dtype)


def merge_order():
    order = np.zeros((4 * ROWS, 144), np.float32)
    for quarter in range(4):
        d_lat, d_lon = quarter // 2, quarter % 2
        for token in range(36):
            lat, lon, lev = token // 6, token % 6 // 2, token % 2
            row, column = 2 * lat + d_lat, 2 * lon + d_lon
            source = 72 * (column // 3) + 6 * row + 2 * (column % 3) + lev
            order[ROWS * quarter + token, source] = 1.0
    return order.astype(jnp.bfloat16)


def attend_kernel(own0, own1, west, east, qkv, out_w, order, cot, result):
    tokens = jnp.concatenate(
        [r[...].astype(F32) for r in (own0, own1, west, east)], axis=0
    )
    normed = norm_rows(tokens).astype(BF16)
    packed = dot(normed, qkv[...]).astype(BF16).astype(F32)
    lane = lax.broadcasted_iota(jnp.int32, (1, 128), 1) // 32
    masks = [(lane == h).astype(F32) for h in range(4)]
    scale = 32 ** -0.5
    halves = []
    for window in range(2):
        rows = slice(72 * window, 72 * window + 72)
        other = slice(144 + 72 * window, 216 + 72 * window)
        parts = []
        for group in range(4):
            low = 128 * group
            queries = packed[rows, low : low + 128]
            keys = jnp.concatenate(
                [packed[rows, 512 + low : 640 + low], packed[other, 512 + low : 640 + low]], axis=0
            ).astype(BF16)
            values = jnp.concatenate(
                [packed[rows, 1024 + low : 1152 + low], packed[other, 1024 + low : 1152 + low]], axis=0
            ).astype(BF16)
            stacked = jnp.concatenate([queries * m for m in masks], axis=0).astype(BF16)
            scores = dot_nt(stacked, keys) * scale
            scores = scores - jnp.max(scores, axis=-1, keepdims=True)
            scores = jnp.exp(scores)
            probs = (scores / jnp.sum(scores, axis=-1, keepdims=True)).astype(BF16)
            mixed = dot(probs, values)
            total = mixed[0:72] * masks[0]
            for h in range(1, 4):
                total = total + mixed[72 * h : 72 * h + 72] * masks[h]
            parts.append(total)
        halves.append(jnp.concatenate(parts, axis=1))
    mixed = jnp.concatenate(halves, axis=0).astype(BF16)
    section = (tokens[0:144] + dot(mixed, out_w[...])).astype(BF16)
    spread = dot(order[...], section)
    wide = jnp.concatenate([spread[ROWS * q : ROWS * q + ROWS] for q in range(4)], axis=1)
    merged_in = norm_rows(wide).astype(BF16)
    for copy in range(4):
        result[copy, :, 0:2048] = merged_in
        result[copy, :, 2048:3072] = cot[...]


def stacked_rows(blocks, columns):
    return jnp.concatenate([blocks[j, :, columns].astype(F32) for j in range(4)], axis=0).astype(BF16)


def merge_kernel(ins, own_w, far_w, result):
    blocks = stacked_rows(ins, slice(0, 2048))
    for half, weight in enumerate((own_w, far_w)):
        part = dot(blocks, weight[...]).astype(BF16).astype(F32)
        for j in range(4):
            rows = part[ROWS * j : ROWS * j + ROWS].astype(BF16)
            for copy in range(4):
                result[copy, j, :, 128 * half : 128 * half + 128] = rows


def pack_kernel(place, merge, up, down, packed, done):
    r = place[0] * 16 + place[1] * 4 + place[2]
    row = pl.multiple_of((place[0] * 8 + place[1] * 2 + place[2] // 2) * 32, 32)
    column = pl.multiple_of(lax.rem(place[2], 2) * 512, 512)
    pairs = [
        (up.at[pl.ds(pl.multiple_of(r * 32, 32), 32), :], packed.at[0:32, :]),
        (down.at[pl.ds(row, 32), pl.ds(column, 512)], packed.at[32:64, :]),
    ]
    for q in range(4):
        at = pl.ds(pl.multiple_of(512 * q + r * 16, 16), 16)
        pairs.append((merge.at[at, :], packed.at[64:80, 128 * q : 128 * q + 128]))
    copies = [pltpu.make_async_copy(a, b, done.at[i]) for i, (a, b) in enumerate(pairs)]
    for copy in copies:
        copy.start()
    for copy in copies:
        copy.wait()


def pack(place, merge, up, down):
    hbm = pl.BlockSpec(memory_space=pltpu.HBM)
    return pl.pallas_call(
        pack_kernel,
        out_shape=shaped((80, 512)),
        in_specs=[pl.BlockSpec(memory_space=pltpu.SMEM), hbm, hbm, hbm],
        out_specs=pl.BlockSpec(memory_space=pltpu.VMEM),
        scratch_shapes=[pltpu.SemaphoreType.DMA((6,))],
        name="pack_kernel",
    )(place, merge, up, down)


def spread_kernel(piece, result):
    for copy in range(16):
        result[copy] = piece[...]


def unpack_kernel(place, near, far, merge, up, down):
    for side, source in enumerate((near, far)):
        first = (place[0] ^ side) * 16
        for index in range(16):
            r = first + index
            up[pl.ds(pl.multiple_of(r * 32, 32), 32), :] = source[index, 0:32, :]
            row = pl.multiple_of((first + index - index % 2) * 16, 32)
            column = 512 * (index % 2)
            down[pl.ds(row, 32), column : column + 512] = source[index, 32:64, :]
            for q in range(4):
                at = pl.multiple_of(512 * q + r * 16, 16)
                merge[pl.ds(at, 16), :] = source[index, 64:80, 128 * q : 128 * q + 128]


def gelu_parts(values):
    cdf = 0.5 * (1.0 + lax.erf(values * np.float32(np.sqrt(0.5))))
    density = jnp.exp(-0.5 * values * values) * np.float32(1.0 / np.sqrt(2.0 * np.pi))
    return values * cdf, cdf + values * density


def hidden_kernel(place, columns, ins, up0, up1, own_merged, bundle, slope, merged):
    lat, half_index, near = place[0], place[3], place[4]
    for j in range(4):
        for half in range(2):
            column = pl.multiple_of(((half_index ^ half) * 4 + j) * 128, 128)
            for block in range(4):
                merged[ROWS * block : ROWS * block + ROWS, pl.ds(column, 128)] = columns[
                    j, block, :, 128 * half : 128 * half + 128
                ].astype(F32)
    own_merged[...] = merged[pl.ds(pl.multiple_of(near * ROWS, 8), ROWS), :].astype(BF16)
    normed = norm_rows(merged[...]).astype(BF16)
    for half, up in enumerate((up0, up1)):
        at = slice(512 * half, 512 * half + 512)
        value, rate = gelu_parts(dot(normed, up[...]))
        bundle[:, at] = value.astype(BF16)
        slope[:, at] = rate
    at = pl.ds(pl.multiple_of(2048 + (1 - lat) * 512, 512), 512)
    bundle[:, 1024:1536] = stacked_rows(ins, at)


def feed_kernel(place, bundle, slope, ins, up0, up1, down0, down1, kept, sent, partial, back):
    cots = stacked_rows(ins, slice(2048, 3072))
    values, grads = 0.0, 0.0
    for half, (up, down) in enumerate(((up0, down0), (up1, down1))):
        at = slice(512 * half, 512 * half + 512)
        grad = (dot_nt(cots, down[...]) * slope[:, at]).astype(BF16)
        values = values + dot(bundle[:, at], down[...])
        grads = grads + dot_nt(grad, up[...])
    partial[...] = values
    back[...] = grads
    for j in range(4):
        rows = pl.ds(pl.multiple_of((place[4] ^ j) * ROWS, 8), ROWS)
        for index, source in enumerate((partial, back)):
            if j < 2:
                kept[j, index] = source[rows, :]
            else:
                sent[j - 2, index] = source[rows, :].astype(BF16)


def halve_kernel(kept, got, left, sent):
    left[...] = kept[0] + got[0].astype(F32)
    sent[...] = (kept[1] + got[1].astype(F32)).astype(BF16)


def finish_kernel(merged, cot, left, got, coarse_out, grad_merged):
    merged_f = merged[...].astype(F32)
    coarse_out[...] = (merged_f + left[0] + got[0].astype(F32)).astype(BF16)
    grad_normed = left[1] + got[1].astype(F32)
    centred = merged_f - jnp.mean(merged_f, axis=-1, keepdims=True)
    scale_inv = lax.rsqrt(jnp.mean(centred * centred, axis=-1, keepdims=True) + EPS)
    nhat = centred * scale_inv
    grad = cot[...].astype(F32) + scale_inv * (
        grad_normed
        - jnp.mean(grad_normed, axis=-1, keepdims=True)
        - nhat * jnp.mean(grad_normed * nhat, axis=-1, keepdims=True)
    )
    grad_merged[...] = grad.astype(BF16)


def weight_kernel(place, ins, bundle, other, result):
    at = pl.ds(pl.multiple_of(2048 + place[0] * 512, 512), 512)
    rows = jnp.concatenate([stacked_rows(ins, at), other[:, 1024:1536]], axis=0)
    hidden = jnp.concatenate([bundle[:, 0:1024], other[:, 0:1024]], axis=0)
    total = dot_tn(rows, hidden)
    for z_hi in range(2):
        for index in range(16):
            low = 256 * z_hi + 16 * index
            result[index, 16 * z_hi : 16 * z_hi + 16, :] = total[low : low + 16].astype(BF16)


def plane_sum_kernel(place, parts, result, total):
    summed = parts[0].astype(F32)
    for index in range(1, 16):
        summed = summed + parts[index].astype(F32)
    total[...] = summed
    for z_hi in range(2):
        for half in range(2):
            at = pl.ds(pl.multiple_of((place[3] ^ half) * 512, 512), 512)
            result[2 * z_hi + half] = total[16 * z_hi : 16 * z_hi + 16, at].astype(BF16)


def line_sum_kernel(parts, result):
    summed = parts[0].astype(F32)
    for index in range(1, 4):
        summed = summed + parts[index].astype(F32)
    result[...] = summed


def token_rows(block):
    return block.transpose(1, 2, 0, 3).reshape(-1, block.shape[-1])


def on_device(fine_tokens, fine_qkv, fine_out, merge_weight, up_weight, down_weight, cotangent):
    place = jnp.stack([lax.axis_index(a) for a in ("lat", "y", "x", "z_half", "z_near")]).astype(jnp.int32)

    own0 = token_rows(fine_tokens[:, :, :3])
    own1 = token_rows(fine_tokens[:, :, 3:])
    west = moved(own1, lambda s: (s + 1) % COUNT)
    east = moved(own0, lambda s: (s - 1) % COUNT)
    cot = jnp.pad(token_rows(cotangent), ((0, ROWS - 36), (0, 0)))

    piece = along_z(pack(place, merge_weight, up_weight, down_weight))
    near = exchanged(call(spread_kernel, shaped((16, 80, 512)), piece), ("y", "x"))
    far = across(near)

    merged_in = call(
        attend_kernel, shaped((4, ROWS, 3072)), own0, own1, west, east, fine_qkv, fine_out,
        jnp.asarray(merge_order()), cot, flops=10**9, after=(near,),
    )
    ins = exchanged(merged_in, "z_near")
    far_merge, far_up, far_down = call(
        unpack_kernel,
        (shaped((2048, 128)), shaped((1024, 512)), shaped((512, 1024))),
        place, near, far, scalars=1, after=(ins,),
    )
    columns = call(merge_kernel, shaped((4, 4, ROWS, 256)), ins, merge_weight, far_merge, flops=2 * 10**8)
    columns = exchanged(columns, "z_near")
    own_merged, bundle, slope = call(
        hidden_kernel,
        (shaped((ROWS, 1024)), shaped((4 * ROWS, 1536)), shaped((4 * ROWS, 1024), F32)),
        place, columns, ins, up_weight, far_up, scalars=1, flops=10**9,
        scratch_shapes=[pltpu.VMEM((4 * ROWS, 1024), F32)],
    )
    other = across(bundle)
    kept, sent = call(
        feed_kernel, (shaped((2, 2, ROWS, 1024), F32), shaped((2, 2, ROWS, 1024))),
        place, bundle, slope, ins, up_weight, far_up, down_weight, far_down, scalars=1, flops=2 * 10**9,
        scratch_shapes=[pltpu.VMEM((4 * ROWS, 1024), F32)] * 2,
    )
    got = swapped(sent, 2)

    parts = call(
        weight_kernel, shaped((16, 32, 1024)), place, ins, bundle, other, scalars=1,
        flops=3 * 10**8, after=(sent,),
    )
    parts = exchanged(parts, ("y", "x"))
    left, sent = call(
        halve_kernel, (shaped((2, ROWS, 1024), F32), shaped((2, ROWS, 1024))), kept, got, after=(parts,)
    )
    got = swapped(sent, 1)
    parts = call(
        plane_sum_kernel, shaped((4, 16, 512)), place, parts, scalars=1,
        scratch_shapes=[pltpu.VMEM((32, 1024), F32)], after=(sent,),
    )
    parts = exchanged(parts, ("z_hi", "z_half"))
    coarse_out, grad_merged = call(
        finish_kernel, (shaped((ROWS, 1024)), shaped((ROWS, 1024))), own_merged, cot, left, got,
        after=(parts,),
    )
    grad_down = call(line_sum_kernel, shaped((16, 512), F32), parts).T

    def placed(rows):
        return rows[:36].reshape(6, 3, 2, 1024).transpose(2, 0, 1, 3)

    return placed(coarse_out), placed(grad_merged), grad_down


def solution(mesh):
    lon, tp = ("z_hi", "y", "x"), ("z_half", "z_near")
    parts = Mesh(mesh.devices.reshape(2, 2, 4, 4, 2, 4), AXES)
    tokens = P(None, "lat", lon + tp, None)
    return jax.shard_map(
        on_device,
        mesh=parts,
        in_specs=(tokens, P(), P(), P(None, tp), P(None, tp), P(tp, None), tokens),
        out_specs=(tokens, tokens, P(tp, ("lat",) + lon)),
        check_vma=False,
    )
```

time: 183 us -> 161 us (0.88)
  the two profiles are of different devices: /device:TPU:32 before, /device:TPU:1 now
where the time goes in v3:
time: 161 us; the launch traced here: 159 us
  starting transfers between devices  66.6 us (41%)
  waiting for transfers between devices  51.6 us (32%)
  Pallas kernels  17.9 us (11%)
  local copies, waits for them, and re-layouts  12.4 us (8%)
  blocking collectives  9.47 us (6%)
    ppermute x4, waiting for transfers between devices, moved(): return lax.ppermute(value, LINE, [(s, target(s)) for s in range(COUNT)])  29.5 us
    all_to_all x4, starting transfers between devices, exchanged(): return lax.all_to_all(value, axes, 0, 0)  25 us
    pallas_call x11, Pallas kernels, call(): pl.pallas_call(body, out_shape=out_shape, in_specs=specs, out_specs=jax.t...  15.8 us
    all_to_all x4, waiting for transfers between devices, exchanged(): return lax.all_to_all(value, axes, 0, 0)  15.1 us
    ppermute x4, starting transfers between devices, moved(): return lax.ppermute(value, LINE, [(s, target(s)) for s in range(COUNT)])  14.3 us
    ppermute x2, starting transfers between devices, across(): return lax.ppermute(value, 'lat', [(0, 1), (1, 0)])  14 us
    ppermute x1, starting transfers between devices, along_z(): return lax.ppermute(value, AXES, pairs)  13.3 us
    all_to_all x1, blocking collectives, exchanged(): return lax.all_to_all(value, axes, 0, 0)  9.47 us
  transfers between devices with their start and end apart: 11, of which 8 were waited for; matrix products, arithmetic and copies ran while one was open for 4% of the time, Pallas kernels for 2%

profile of v3, /device:TPU:1, one launch (start us, length us, event | category | flops | bytes accessed | tf_op | source)
XLA Modules:
  0.0 158.9 jit_solution(12783065125582839872)
XLA Ops:
  1.2 2.1 %pack_kernel.1 = bf16[80,512]{1,0:T(8,128)(2,1)} custom-call(s32[5]{0:T(128)} %stack.23.place.refs_0_, bf16[2048,128]{1,0:T(8,128)(2,1)} %refs_1_.1, bf16[1024,512]{1,0:T(8,128)(2,1)} %refs_4_.3, bf16[512,1024]{1,0:T(8,128)(2,1)} %refs_6_.2), custom_call_target="tpu_custom_call" | custom-call | tf_op jit(solution)/shard_map/pack_kernel/pallas_call | solution.py:179
  3.4 13.3 %collective-permute-start.2 = (bf16[80,512]{1,0:T(8,128)(2,1)}, bf16[80,512]{1,0:T(8,128)(2,1)S(1)}, u32[]{:S(2)}, u32[]{:S(2)}) collective-permute-start(bf16[80,512]{1,0:T(8,128)(2,1)} %pack_kernel.1), channel_id=1, source_target_pairs={{0,4},{1,5},{2,6},{3,7},{4,128},{5,129},{6,130},{7,131},{8,12},{9,... | collective-permute-start | bytes 245768 | tf_op jit(solution)/shard_map/ppermute | solution.py:50
  16.6 4.3 %collective-permute-done.2.refs_0_ = bf16[80,512]{1,0:T(8,128)(2,1)S(1)} collective-permute-done((bf16[80,512]{1,0:T(8,128)(2,1)}, bf16[80,512]{1,0:T(8,128)(2,1)S(1)}, u32[]{:S(2)}, u32[]{:S(2)}) %collective-permute-start.2) | collective-permute-done | bytes 81952 | tf_op jit(solution)/shard_map/ppermute | solution.py:50
  22.2 6.9 %all-to-all-start = ((bf16[16,80,512]{2,1,0:T(8,128)(2,1)}), bf16[16,80,512]{2,1,0:T(8,128)(2,1)S(1)}, u32[]{:S(2)}, u32[]{:S(2)}) async-start(bf16[16,80,512]{2,1,0:T(8,128)(2,1)} %spread_kernel.1), calls=%async_computation | async-start | bytes 2621440 | tf_op jit(solution)/shard_map/all_to_all | solution.py:54
  29.1 1.7 %slice_bitcast_fusion = (bf16[12,3,2,512]{3,2,1,0:T(2,128)(2,1)S(1)}, bf16[12,3,2,512]{3,2,1,0:T(2,128)(2,1)}) fusion(bf16[2,12,6,512]{3,0,2,1:T(2,128)(2,1)} %param.8), kind=kLoop, calls=%fused_computation | loop fusion | bytes 294912 | tf_op jit(solution)/shard_map/transpose | solution.py:303
  32.3 8.3 %collective-permute-start.1 = (bf16[72,512]{1,0:T(8,128)(2,1)}, bf16[72,512]{1,0:T(8,128)(2,1)}, u32[]{:S(2)}, u32[]{:S(2)}) collective-permute-start(bf16[72,512]{1,0:T(8,128)(2,1)} %reshape.21.refs_0_), channel_id=1, source_target_pairs={{0,255},{1,0},{2,1},{3,2},{4,3},{5,4},{6,5},{7,6},{8,7},{9,8},{10,... | collective-permute-start | bytes 221192 | tf_op jit(solution)/shard_map/ppermute | solution.py:31
  41.3 1.9 %collective-permute-start = (bf16[72,512]{1,0:T(8,128)(2,1)}, bf16[72,512]{1,0:T(8,128)(2,1)}, u32[]{:S(2)}, u32[]{:S(2)}) collective-permute-start(bf16[72,512]{1,0:T(8,128)(2,1)} %reshape.22.refs_1_), channel_id=1, source_target_pairs={{0,1},{1,2},{2,3},{3,4},{4,5},{5,6},{6,7},{7,8},{8,9},{9,10},{10,1... | collective-permute-start | bytes 221192 | tf_op jit(solution)/shard_map/ppermute | solution.py:31
  45.6 7.3 %collective-permute-done.refs_2_ = bf16[72,512]{1,0:T(8,128)(2,1)} collective-permute-done((bf16[72,512]{1,0:T(8,128)(2,1)}, bf16[72,512]{1,0:T(8,128)(2,1)}, u32[]{:S(2)}, u32[]{:S(2)}) %collective-permute-start) | collective-permute-done | bytes 73760 | tf_op jit(solution)/shard_map/ppermute | solution.py:31
  53.8 4.7 %attend_kernel.1 = bf16[4,40,3072]{2,1,0:T(8,128)(2,1)} custom-call(bf16[72,512]{1,0:T(8,128)(2,1)} %reshape.21.refs_0_, bf16[72,512]{1,0:T(8,128)(2,1)} %reshape.22.refs_1_, bf16[72,512]{1,0:T(8,128)(2,1)} %collective-permute-done.refs_2_, bf16[72,512]{1,0:T(8,128)(2,1)} %collective-permute-done.1.refs_3_, bf16[512,1536]{1,0:T(8,128)(2,1)S(1)} %copy-done.1, ...), custom_call_target="tpu_custom_call" | custom-call | flops 1000000000 | bytes 2520064 | tf_op jit(solution)/shard_map/attend_kernel/pallas_call | solution.py:73
  58.5 3.6 %all-to-all-start.1 = ((bf16[4,40,3072]{2,1,0:T(8,128)(2,1)}), bf16[4,40,3072]{2,1,0:T(8,128)(2,1)S(1)}, u32[]{:S(2)}, u32[]{:S(2)}) async-start(bf16[4,40,3072]{2,1,0:T(8,128)(2,1)} %attend_kernel.1), calls=%async_computation.1 | async-start | bytes 1966080 | tf_op jit(solution)/shard_map/all_to_all | solution.py:54
  62.2 7.2 %collective-permute-start.3 = (bf16[16,80,512]{2,1,0:T(8,128)(2,1)S(1)}, bf16[16,80,512]{2,1,0:T(8,128)(2,1)S(1)}, u32[]{:S(2)}, u32[]{:S(2)}) collective-permute-start(bf16[16,80,512]{2,1,0:T(8,128)(2,1)S(1)} %all-to-all-done.refs_8_.refs_1_), channel_id=1, source_target_pairs={{0,256},{256,0},{1,257},{257,1},{2,258},{258,2},{3,259},{259,3},{4... | collective-permute-start | bytes 3932168 | tf_op jit(solution)/shard_map/ppermute | solution.py:39
  69.4 2.6 %collective-permute-done.3.refs_2_ = bf16[16,80,512]{2,1,0:T(8,128)(2,1)S(1)} collective-permute-done((bf16[16,80,512]{2,1,0:T(8,128)(2,1)S(1)}, bf16[16,80,512]{2,1,0:T(8,128)(2,1)S(1)}, u32[]{:S(2)}, u32[]{:S(2)}) %collective-permute-start.3) | collective-permute-done | bytes 1310752 | tf_op jit(solution)/shard_map/ppermute | solution.py:39
  73.1 10.5 %all-to-all-done.1.refs_3_.refs_0_.refs_2_.refs_1_ = bf16[4,40,3072]{2,1,0:T(8,128)(2,1)S(1)} async-done(((bf16[4,40,3072]{2,1,0:T(8,128)(2,1)}), bf16[4,40,3072]{2,1,0:T(8,128)(2,1)S(1)}, u32[]{:S(2)}, u32[]{:S(2)}) %all-to-all-start.1) | async-done | bytes 983072 | tf_op jit(solution)/shard_map/all_to_all | solution.py:54
  86.4 9.5 %all_to_all.25.refs_1_ = bf16[4,4,40,256]{3,2,1,0:T(8,128)(2,1)S(1)} all-to-all(bf16[4,4,40,256]{3,2,1,0:T(8,128)(2,1)S(1)} %merge_kernel.1), channel_id=1, replica_groups=mesh['lat'=2,'z_hi'=2,'y'=4,'x'=4,'z_half'=2,'z_near'=4] {'z_near'}, dimensions={0} | all-to-all | bytes 655360 | tf_op jit(solution)/shard_map/all_to_all | solution.py:54
  97.3 6.7 %collective-permute-start.5 = (bf16[160,1536]{1,0:T(8,128)(2,1)S(1)}, bf16[160,1536]{1,0:T(8,128)(2,1)S(1)}, u32[]{:S(2)}, u32[]{:S(2)}) collective-permute-start(bf16[160,1536]{1,0:T(8,128)(2,1)S(1)} %get-tuple-element.18.refs_1_.refs_2_), channel_id=1, source_target_pairs={{0,256},{256,0},{1,257},{257,1},{2,258},{258,2},{3,259},{259,3},{4... | collective-permute-start | bytes 1474568 | tf_op jit(solution)/shard_map/ppermute | solution.py:39
  104.1 2.5 %feed_kernel.1 = (f32[2,2,40,1024]{3,2,1,0:T(8,128)S(1)}, bf16[2,2,40,1024]{3,2,1,0:T(8,128)(2,1)S(1)}) custom-call(s32[5]{0:T(128)S(1)} %copy-done.10, bf16[160,1536]{1,0:T(8,128)(2,1)S(1)} %get-tuple-element.18.refs_1_.refs_2_, f32[160,1024]{1,0:T(8,128)S(1)} %get-tuple-element.19.refs_2_, ...), custom_call_target="tpu_custom_call" | custom-call | flops 2000000000 | bytes 6324244 | tf_op jit(solution)/shard_map/feed_kernel/pallas_call | solution.py:73
  107.4 2.3 %weight_kernel.1 = bf16[16,32,1024]{2,1,0:T(8,128)(2,1)} custom-call(s32[5]{0:T(128)S(1)} %copy-done.10, bf16[4,40,3072]{2,1,0:T(8,128)(2,1)S(1)} %all-to-all-done.1.refs_3_.refs_0_.refs_2_.refs_1_, bf16[160,1536]{1,0:T(8,128)(2,1)S(1)} %get-tuple-element.18.refs_1_.refs_2_, bf16[160,1536]{1,0:T(8,128)(2,1)S(1)} %collective-permute-done.5.refs_3_, ...), custom_call_target="tpu_custom_call" | custom-call | flops 300000000 | bytes 1966100 | tf_op jit(solution)/shard_map/weight_kernel/pallas_call | solution.py:73
  109.7 6.9 %all-to-all-start.3 = ((bf16[16,32,1024]{2,1,0:T(8,128)(2,1)}), bf16[16,32,1024]{2,1,0:T(8,128)(2,1)S(1)}, u32[]{:S(2)}, u32[]{:S(2)}) async-start(bf16[16,32,1024]{2,1,0:T(8,128)(2,1)} %weight_kernel.1), calls=%async_computation.3 | async-start | bytes 2097152 | tf_op jit(solution)/shard_map/all_to_all | solution.py:54
  116.6 2.2 %collective-permute-start.4 = (bf16[2,2,40,1024]{3,2,1,0:T(8,128)(2,1)S(1)}, bf16[2,2,40,1024]{3,2,1,0:T(8,128)(2,1)S(1)}, u32[]{:S(2)}, u32[]{:S(2)}) collective-permute-start(bf16[2,2,40,1024]{3,2,1,0:T(8,128)(2,1)S(1)} %get-tuple-element.22.refs_4_), channel_id=1, source_target_pairs={{0,2},{1,3},{2,0},{3,1},{4,6},{5,7},{6,4},{7,5},{8,10},{9,11},{10,... | collective-permute-start | bytes 983048 | tf_op jit(solution)/shard_map/ppermute | solution.py:31
  118.8 17.0 %collective-permute-done.4.refs_1_ = bf16[2,2,40,1024]{3,2,1,0:T(8,128)(2,1)S(1)} collective-permute-done((bf16[2,2,40,1024]{3,2,1,0:T(8,128)(2,1)S(1)}, bf16[2,2,40,1024]{3,2,1,0:T(8,128)(2,1)S(1)}, u32[]{:S(2)}, u32[]{:S(2)}) %collective-permute-start.4) | collective-permute-done | bytes 327712 | tf_op jit(solution)/shard_map/ppermute | solution.py:31
  137.3 7.6 %all-to-all-start.4 = ((bf16[4,16,512]{2,1,0:T(8,128)(2,1)}), bf16[4,16,512]{2,1,0:T(8,128)(2,1)S(1)}, u32[]{:S(2)}, u32[]{:S(2)}) async-start(bf16[4,16,512]{2,1,0:T(8,128)(2,1)} %plane_sum_kernel.1), calls=%async_computation.4 | async-start | bytes 131072 | tf_op jit(solution)/shard_map/all_to_all | solution.py:54
  144.9 1.9 %collective-permute-start.6 = (bf16[2,40,1024]{2,1,0:T(8,128)(2,1)S(1)}, bf16[2,40,1024]{2,1,0:T(8,128)(2,1)S(1)}, u32[]{:S(2)}, u32[]{:S(2)}) collective-permute-start(bf16[2,40,1024]{2,1,0:T(8,128)(2,1)S(1)} %get-tuple-element.24.refs_2_), channel_id=1, source_target_pairs={{0,1},{1,0},{2,3},{3,2},{4,5},{5,4},{6,7},{7,6},{8,9},{9,8},{10,11... | collective-permute-start | bytes 491528 | tf_op jit(solution)/shard_map/ppermute | solution.py:31
  146.8 5.2 %collective-permute-done.6.refs_3_ = bf16[2,40,1024]{2,1,0:T(8,128)(2,1)S(1)} collective-permute-done((bf16[2,40,1024]{2,1,0:T(8,128)(2,1)S(1)}, bf16[2,40,1024]{2,1,0:T(8,128)(2,1)S(1)}, u32[]{:S(2)}, u32[]{:S(2)}) %collective-permute-start.6) | collective-permute-done | bytes 163872 | tf_op jit(solution)/shard_map/ppermute | solution.py:31
  152.0 4.6 %all-to-all-done.4.refs_4_.refs_0_ = bf16[4,16,512]{2,1,0:T(8,128)(2,1)S(1)} async-done(((bf16[4,16,512]{2,1,0:T(8,128)(2,1)}), bf16[4,16,512]{2,1,0:T(8,128)(2,1)S(1)}, u32[]{:S(2)}, u32[]{:S(2)}) %all-to-all-start.4) | async-done | bytes 65568 | tf_op jit(solution)/shard_map/all_to_all | solution.py:54
  (41 shorter events, 17.1 us)
Async XLA Ops:
  3.4 17.6 %collective-permute-start.2 = (bf16[80,512]{1,0:T(8,128)(2,1)}, bf16[80,512]{1,0:T(8,128)(2,1)S(1)}, u32[]{:S(2)}, u32[]{:S(2)}) collective-permute-start(bf16[80,512]{1,0:T(8,128)(2,1)} %pack_kernel.1), channel_id=1, source_target_pairs={{0,4},{1,5},{2,6},{3,7},{4,128},{5,129},{6,130},{7,131},{8,12},{9,... | collective-permute-start | bytes 245768 | tf_op jit(solution)/shard_map/ppermute | solution.py:50
  22.2 30.8 %copy-start.1 = (bf16[512,1536]{1,0:T(8,128)(2,1)S(1)}, bf16[512,1536]{1,0:T(8,128)(2,1)}, u32[]{:S(2)}) copy-start(bf16[512,1536]{1,0:T(8,128)(2,1)} %refs_4_.2) | copy-start | bytes 4718596
  22.2 30.8 %copy-start.8 = (bf16[512,512]{1,0:T(8,128)(2,1)S(1)}, bf16[512,512]{1,0:T(8,128)(2,1)}, u32[]{:S(2)}) copy-start(bf16[512,512]{1,0:T(8,128)(2,1)} %refs_5_.1) | copy-start | bytes 1572868
  22.2 30.8 %all-to-all-start = ((bf16[16,80,512]{2,1,0:T(8,128)(2,1)}), bf16[16,80,512]{2,1,0:T(8,128)(2,1)S(1)}, u32[]{:S(2)}, u32[]{:S(2)}) async-start(bf16[16,80,512]{2,1,0:T(8,128)(2,1)} %spread_kernel.1), calls=%async_computation | async-start | bytes 2621440 | tf_op jit(solution)/shard_map/all_to_all | solution.py:54
  32.3 13.3 %collective-permute-start.1 = (bf16[72,512]{1,0:T(8,128)(2,1)}, bf16[72,512]{1,0:T(8,128)(2,1)}, u32[]{:S(2)}, u32[]{:S(2)}) collective-permute-start(bf16[72,512]{1,0:T(8,128)(2,1)} %reshape.21.refs_0_), channel_id=1, source_target_pairs={{0,255},{1,0},{2,1},{3,2},{4,3},{5,4},{6,5},{7,6},{8,7},{9,8},{10,... | collective-permute-start | bytes 221192 | tf_op jit(solution)/shard_map/ppermute | solution.py:31
  41.3 11.6 %collective-permute-start = (bf16[72,512]{1,0:T(8,128)(2,1)}, bf16[72,512]{1,0:T(8,128)(2,1)}, u32[]{:S(2)}, u32[]{:S(2)}) collective-permute-start(bf16[72,512]{1,0:T(8,128)(2,1)} %reshape.22.refs_1_), channel_id=1, source_target_pairs={{0,1},{1,2},{2,3},{3,4},{4,5},{5,6},{6,7},{7,8},{8,9},{9,10},{10,1... | collective-permute-start | bytes 221192 | tf_op jit(solution)/shard_map/ppermute | solution.py:31
  52.9 0.9 copy-start.9
  58.5 25.1 %copy-start.10 = (s32[5]{0:T(128)S(1)}, s32[5]{0:T(128)}, u32[]{:S(2)}) copy-start(s32[5]{0:T(128)} %stack.23.place.refs_0_) | copy-start | bytes 64
  58.5 25.1 %all-to-all-start.1 = ((bf16[4,40,3072]{2,1,0:T(8,128)(2,1)}), bf16[4,40,3072]{2,1,0:T(8,128)(2,1)S(1)}, u32[]{:S(2)}, u32[]{:S(2)}) async-start(bf16[4,40,3072]{2,1,0:T(8,128)(2,1)} %attend_kernel.1), calls=%async_computation.1 | async-start | bytes 1966080 | tf_op jit(solution)/shard_map/all_to_all | solution.py:54
  62.2 23.7 %copy-start = (bf16[2048,128]{1,0:T(8,128)(2,1)S(1)}, bf16[2048,128]{1,0:T(8,128)(2,1)}, u32[]{:S(2)}) copy-start(bf16[2048,128]{1,0:T(8,128)(2,1)} %refs_1_.1) | copy-start | bytes 1572868
  62.2 9.9 %collective-permute-start.3 = (bf16[16,80,512]{2,1,0:T(8,128)(2,1)S(1)}, bf16[16,80,512]{2,1,0:T(8,128)(2,1)S(1)}, u32[]{:S(2)}, u32[]{:S(2)}) collective-permute-start(bf16[16,80,512]{2,1,0:T(8,128)(2,1)S(1)} %all-to-all-done.refs_8_.refs_1_), channel_id=1, source_target_pairs={{0,256},{256,0},{1,257},{257,1},{2,258},{258,2},{3,259},{259,3},{4... | collective-permute-start | bytes 3932168 | tf_op jit(solution)/shard_map/ppermute | solution.py:39
  72.0 1.1 copy-start.2
  83.6 1.3 copy-start.3
  85.9 10.0 %copy-start.4 = (bf16[1024,512]{1,0:T(8,128)(2,1)S(1)}, bf16[1024,512]{1,0:T(8,128)(2,1)}, u32[]{:S(2)}) copy-start(bf16[1024,512]{1,0:T(8,128)(2,1)} %refs_4_.3) | copy-start | bytes 3145732
  95.8 8.2 %copy-start.5 = (bf16[512,1024]{1,0:T(8,128)(2,1)S(1)}, bf16[512,1024]{1,0:T(8,128)(2,1)}, u32[]{:S(2)}) copy-start(bf16[512,1024]{1,0:T(8,128)(2,1)} %refs_6_.2) | copy-start | bytes 3145732
  97.3 10.1 %collective-permute-start.5 = (bf16[160,1536]{1,0:T(8,128)(2,1)S(1)}, bf16[160,1536]{1,0:T(8,128)(2,1)S(1)}, u32[]{:S(2)}, u32[]{:S(2)}) collective-permute-start(bf16[160,1536]{1,0:T(8,128)(2,1)S(1)} %get-tuple-element.18.refs_1_.refs_2_), channel_id=1, source_target_pairs={{0,256},{256,0},{1,257},{257,1},{2,258},{258,2},{3,259},{259,3},{4... | collective-permute-start | bytes 1474568 | tf_op jit(solution)/shard_map/ppermute | solution.py:39
  106.6 0.8 copy-start.6
  109.7 26.2 %copy-start.7 = (f32[2,2,40,1024]{3,2,1,0:T(8,128)S(1)}, f32[2,2,40,1024]{3,2,1,0:T(8,128)}, u32[]{:S(2)}) copy-start(f32[2,2,40,1024]{3,2,1,0:T(8,128)} %copy-done.6) | copy-start | bytes 1966084
  109.7 26.2 %all-to-all-start.3 = ((bf16[16,32,1024]{2,1,0:T(8,128)(2,1)}), bf16[16,32,1024]{2,1,0:T(8,128)(2,1)S(1)}, u32[]{:S(2)}, u32[]{:S(2)}) async-start(bf16[16,32,1024]{2,1,0:T(8,128)(2,1)} %weight_kernel.1), calls=%async_computation.3 | async-start | bytes 2097152 | tf_op jit(solution)/shard_map/all_to_all | solution.py:54
  116.6 19.2 %collective-permute-start.4 = (bf16[2,2,40,1024]{3,2,1,0:T(8,128)(2,1)S(1)}, bf16[2,2,40,1024]{3,2,1,0:T(8,128)(2,1)S(1)}, u32[]{:S(2)}, u32[]{:S(2)}) collective-permute-start(bf16[2,2,40,1024]{3,2,1,0:T(8,128)(2,1)S(1)} %get-tuple-element.22.refs_4_), channel_id=1, source_target_pairs={{0,2},{1,3},{2,0},{3,1},{4,6},{5,7},{6,4},{7,5},{8,10},{9,11},{10,... | collective-permute-start | bytes 983048 | tf_op jit(solution)/shard_map/ppermute | solution.py:31
  137.3 19.3 %all-to-all-start.4 = ((bf16[4,16,512]{2,1,0:T(8,128)(2,1)}), bf16[4,16,512]{2,1,0:T(8,128)(2,1)S(1)}, u32[]{:S(2)}, u32[]{:S(2)}) async-start(bf16[4,16,512]{2,1,0:T(8,128)(2,1)} %plane_sum_kernel.1), calls=%async_computation.4 | async-start | bytes 131072 | tf_op jit(solution)/shard_map/all_to_all | solution.py:54
  144.9 7.1 %collective-permute-start.6 = (bf16[2,40,1024]{2,1,0:T(8,128)(2,1)S(1)}, bf16[2,40,1024]{2,1,0:T(8,128)(2,1)S(1)}, u32[]{:S(2)}, u32[]{:S(2)}) collective-permute-start(bf16[2,40,1024]{2,1,0:T(8,128)(2,1)S(1)} %get-tuple-element.24.refs_2_), channel_id=1, source_target_pairs={{0,1},{1,0},{2,3},{3,2},{4,5},{5,4},{6,7},{7,6},{8,9},{9,8},{10,11... | collective-permute-start | bytes 491528 | tf_op jit(solution)/shard_map/ppermute | solution.py:31

commit v4 on v3

--- a/solution.py
+++ b/solution.py
@@ -75,7 +75,7 @@
         out_shape=out_shape,
         in_specs=specs,
         out_specs=jax.tree.map(lambda _: pl.BlockSpec(memory_space=pltpu.VMEM), out_shape),
-        compiler_params=pltpu.CompilerParams(vmem_limit_bytes=40 * 1024 * 1024),
+        compiler_params=pltpu.CompilerParams(vmem_limit_bytes=16 * 1024 * 1024),
         cost_estimate=pl.CostEstimate(flops=flops, bytes_accessed=size, transcendentals=0),
         name=kernel.__name__,
         **kw,
@@ -98,7 +98,7 @@
     return order.astype(jnp.bfloat16)
 
 
-def attend_kernel(own0, own1, west, east, qkv, out_w, order, cot, result):
+def attend_kernel(own0, own1, west, east, qkv, out_w, order, result):
     tokens = jnp.concatenate(
         [r[...].astype(F32) for r in (own0, own1, west, east)], axis=0
     )
@@ -138,8 +138,7 @@
     wide = jnp.concatenate([spread[ROWS * q : ROWS * q + ROWS] for q in range(4)], axis=1)
     merged_in = norm_rows(wide).astype(BF16)
     for copy in range(4):
-        result[copy, :, 0:2048] = merged_in
-        result[copy, :, 2048:3072] = cot[...]
+        result[copy] = merged_in
 
 
 def stacked_rows(blocks, columns):
@@ -156,11 +155,15 @@
                 result[copy, j, :, 128 * half : 128 * half + 128] = rows
 
 
-def pack_kernel(place, merge, up, down, packed, done):
+def prepare_kernel(
+    place, tokens, cotangent, merge, up, down, west_side, east_side, packed, cot, tokens_in, cot_in, done
+):
     r = place[0] * 16 + place[1] * 4 + place[2]
     row = pl.multiple_of((place[0] * 8 + place[1] * 2 + place[2] // 2) * 32, 32)
     column = pl.multiple_of(lax.rem(place[2], 2) * 512, 512)
     pairs = [
+        (tokens, tokens_in),
+        (cotangent, cot_in),
         (up.at[pl.ds(pl.multiple_of(r * 32, 32), 32), :], packed.at[0:32, :]),
         (down.at[pl.ds(row, 32), pl.ds(column, 512)], packed.at[32:64, :]),
     ]
@@ -170,20 +173,37 @@
     copies = [pltpu.make_async_copy(a, b, done.at[i]) for i, (a, b) in enumerate(pairs)]
     for copy in copies:
         copy.start()
-    for copy in copies:
+    copies[0].wait()
+    for lat in range(12):
+        for lon in range(3):
+            rows = slice(6 * lat + 2 * lon, 6 * lat + 2 * lon + 2)
+            west_side[rows, :] = tokens_in[lat, lon]
+            east_side[rows, :] = tokens_in[lat, lon + 3]
+    copies[1].wait()
+    for copy in range(4):
+        for lat in range(6):
+            for lon in range(3):
+                cot[copy, 6 * lat + 2 * lon : 6 * lat + 2 * lon + 2, :] = cot_in[lat, lon]
+        cot[copy, 36:40, :] = jnp.zeros((4, 1024), BF16)
+    for copy in copies[2:]:
         copy.wait()
 
 
-def pack(place, merge, up, down):
+def prepare(place, tokens, cotangent, merge, up, down):
     hbm = pl.BlockSpec(memory_space=pltpu.HBM)
+    vmem = pl.BlockSpec(memory_space=pltpu.VMEM)
     return pl.pallas_call(
-        pack_kernel,
-        out_shape=shaped((80, 512)),
-        in_specs=[pl.BlockSpec(memory_space=pltpu.SMEM), hbm, hbm, hbm],
-        out_specs=pl.BlockSpec(memory_space=pltpu.VMEM),
-        scratch_shapes=[pltpu.SemaphoreType.DMA((6,))],
-        name="pack_kernel",
-    )(place, merge, up, down)
+        prepare_kernel,
+        out_shape=(shaped((72, 512)), shaped((72, 512)), shaped((80, 512)), shaped((4, ROWS, 1024))),
+        in_specs=[pl.BlockSpec(memory_space=pltpu.SMEM), hbm, hbm, hbm, hbm, hbm],
+        out_specs=(vmem,) * 4,
+        scratch_shapes=[
+            pltpu.VMEM((12, 6, 2, 512), BF16),
+            pltpu.VMEM((6, 3, 2, 1024), BF16),
+            pltpu.SemaphoreType.DMA((8,)),
+        ],
+        name="prepare_kernel",
+    )(place, tokens.transpose(1, 2, 0, 3), cotangent.transpose(1, 2, 0, 3), merge, up, down)
 
 
 def spread_kernel(piece, result):
@@ -211,7 +231,7 @@
     return values * cdf, cdf + values * density
 
 
-def hidden_kernel(place, columns, ins, up0, up1, own_merged, bundle, slope, merged):
+def hidden_kernel(place, columns, cots, up0, up1, own_merged, bundle, slope, merged):
     lat, half_index, near = place[0], place[3], place[4]
     for j in range(4):
         for half in range(2):
@@ -227,52 +247,50 @@
         value, rate = gelu_parts(dot(normed, up[...]))
         bundle[:, at] = value.astype(BF16)
         slope[:, at] = rate
-    at = pl.ds(pl.multiple_of(2048 + (1 - lat) * 512, 512), 512)
-    bundle[:, 1024:1536] = stacked_rows(ins, at)
-
-
-def feed_kernel(place, bundle, slope, ins, up0, up1, down0, down1, kept, sent, partial, back):
-    cots = stacked_rows(ins, slice(2048, 3072))
+    at = pl.ds(pl.multiple_of((1 - lat) * 512, 512), 512)
+    bundle[:, 1024:1536] = stacked_rows(cots, at)
+
+
+def feed_kernel(bundle, slope, cots, up0, up1, down0, down1, sent):
+    cots = stacked_rows(cots, slice(0, 1024))
     values, grads = 0.0, 0.0
     for half, (up, down) in enumerate(((up0, down0), (up1, down1))):
         at = slice(512 * half, 512 * half + 512)
         grad = (dot_nt(cots, down[...]) * slope[:, at]).astype(BF16)
         values = values + dot(bundle[:, at], down[...])
         grads = grads + dot_nt(grad, up[...])
-    partial[...] = values
-    back[...] = grads
     for j in range(4):
-        rows = pl.ds(pl.multiple_of((place[4] ^ j) * ROWS, 8), ROWS)
-        for index, source in enumerate((partial, back)):
-            if j < 2:
-                kept[j, index] = source[rows, :]
-            else:
-                sent[j - 2, index] = source[rows, :].astype(BF16)
-
-
-def halve_kernel(kept, got, left, sent):
-    left[...] = kept[0] + got[0].astype(F32)
-    sent[...] = (kept[1] + got[1].astype(F32)).astype(BF16)
-
-
-def finish_kernel(merged, cot, left, got, coarse_out, grad_merged):
+        rows = slice(ROWS * j, ROWS * j + ROWS)
+        sent[j, 0] = values[rows].astype(BF16)
+        sent[j, 1] = grads[rows].astype(BF16)
+
+
+def finish_kernel(merged, cot, got, coarse_out, grad_merged):
     merged_f = merged[...].astype(F32)
-    coarse_out[...] = (merged_f + left[0] + got[0].astype(F32)).astype(BF16)
-    grad_normed = left[1] + got[1].astype(F32)
+    summed = got[0].astype(F32)
+    for j in range(1, 4):
+        summed = summed + got[j].astype(F32)
+    value = (merged_f + summed[0]).astype(BF16)
+    grad_normed = summed[1]
     centred = merged_f - jnp.mean(merged_f, axis=-1, keepdims=True)
     scale_inv = lax.rsqrt(jnp.mean(centred * centred, axis=-1, keepdims=True) + EPS)
     nhat = centred * scale_inv
-    grad = cot[...].astype(F32) + scale_inv * (
+    grad = cot[0].astype(F32) + scale_inv * (
         grad_normed
         - jnp.mean(grad_normed, axis=-1, keepdims=True)
         - nhat * jnp.mean(grad_normed * nhat, axis=-1, keepdims=True)
     )
-    grad_merged[...] = grad.astype(BF16)
-
-
-def weight_kernel(place, ins, bundle, other, result):
-    at = pl.ds(pl.multiple_of(2048 + place[0] * 512, 512), 512)
-    rows = jnp.concatenate([stacked_rows(ins, at), other[:, 1024:1536]], axis=0)
+    grad = grad.astype(BF16)
+    for lat in range(6):
+        for lon in range(3):
+            rows = slice(6 * lat + 2 * lon, 6 * lat + 2 * lon + 2)
+            coarse_out[lat, lon] = value[rows]
+            grad_merged[lat, lon] = grad[rows]
+
+
+def weight_kernel(place, cots, bundle, other, result):
+    at = pl.ds(pl.multiple_of(place[0] * 512, 512), 512)
+    rows = jnp.concatenate([stacked_rows(cots, at), other[:, 1024:1536]], axis=0)
     hidden = jnp.concatenate([bundle[:, 0:1024], other[:, 0:1024]], axis=0)
     total = dot_tn(rows, hidden)
     for z_hi in range(2):
@@ -299,26 +317,21 @@
     result[...] = summed
 
 
-def token_rows(block):
-    return block.transpose(1, 2, 0, 3).reshape(-1, block.shape[-1])
-
-
 def on_device(fine_tokens, fine_qkv, fine_out, merge_weight, up_weight, down_weight, cotangent):
     place = jnp.stack([lax.axis_index(a) for a in ("lat", "y", "x", "z_half", "z_near")]).astype(jnp.int32)
-
-    own0 = token_rows(fine_tokens[:, :, :3])
-    own1 = token_rows(fine_tokens[:, :, 3:])
+    own0, own1, piece, cot = prepare(place, fine_tokens, cotangent, merge_weight, up_weight, down_weight)
+
     west = moved(own1, lambda s: (s + 1) % COUNT)
     east = moved(own0, lambda s: (s - 1) % COUNT)
-    cot = jnp.pad(token_rows(cotangent), ((0, ROWS - 36), (0, 0)))
-
-    piece = along_z(pack(place, merge_weight, up_weight, down_weight))
-    near = exchanged(call(spread_kernel, shaped((16, 80, 512)), piece), ("y", "x"))
+    piece = along_z(piece)
+    cots = exchanged(cot, "z_near")
+
+    pieces = call(spread_kernel, shaped((16, 80, 512)), piece, after=(west, east, cots))
+    near = exchanged(pieces, ("y", "x"))
     far = across(near)
-
     merged_in = call(
-        attend_kernel, shaped((4, ROWS, 3072)), own0, own1, west, east, fine_qkv, fine_out,
-        jnp.asarray(merge_order()), cot, flops=10**9, after=(near,),
+        attend_kernel, shaped((4, ROWS, 2048)), own0, own1, west, east, fine_qkv, fine_out,
+        jnp.asarray(merge_order()), flops=10**9, after=(pieces,),
     )
     ins = exchanged(merged_in, "z_near")
     far_merge, far_up, far_down = call(
@@ -331,41 +344,31 @@
     own_merged, bundle, slope = call(
         hidden_kernel,
         (shaped((ROWS, 1024)), shaped((4 * ROWS, 1536)), shaped((4 * ROWS, 1024), F32)),
-        place, columns, ins, up_weight, far_up, scalars=1, flops=10**9,
+        place, columns, cots, up_weight, far_up, scalars=1, flops=10**9,
         scratch_shapes=[pltpu.VMEM((4 * ROWS, 1024), F32)],
     )
     other = across(bundle)
-    kept, sent = call(
-        feed_kernel, (shaped((2, 2, ROWS, 1024), F32), shaped((2, 2, ROWS, 1024))),
-        place, bundle, slope, ins, up_weight, far_up, down_weight, far_down, scalars=1, flops=2 * 10**9,
-        scratch_shapes=[pltpu.VMEM((4 * ROWS, 1024), F32)] * 2,
-    )
-    got = swapped(sent, 2)
-
+    partials = call(
+        feed_kernel, shaped((4, 2, ROWS, 1024)),
+        bundle, slope, cots, up_weight, far_up, down_weight, far_down, flops=2 * 10**9,
+    )
     parts = call(
-        weight_kernel, shaped((16, 32, 1024)), place, ins, bundle, other, scalars=1,
-        flops=3 * 10**8, after=(sent,),
+        weight_kernel, shaped((16, 32, 1024)), place, cots, bundle, other, scalars=1,
+        flops=3 * 10**8, after=(partials,),
     )
     parts = exchanged(parts, ("y", "x"))
-    left, sent = call(
-        halve_kernel, (shaped((2, ROWS, 1024), F32), shaped((2, ROWS, 1024))), kept, got, after=(parts,)
-    )
-    got = swapped(sent, 1)
+    got = exchanged(partials, "z_near")
     parts = call(
         plane_sum_kernel, shaped((4, 16, 512)), place, parts, scalars=1,
-        scratch_shapes=[pltpu.VMEM((32, 1024), F32)], after=(sent,),
+        scratch_shapes=[pltpu.VMEM((32, 1024), F32)],
     )
     parts = exchanged(parts, ("z_hi", "z_half"))
-    coarse_out, grad_merged = call(
-        finish_kernel, (shaped((ROWS, 1024)), shaped((ROWS, 1024))), own_merged, cot, left, got,
-        after=(parts,),
-    )
-    grad_down = call(line_sum_kernel, shaped((16, 512), F32), parts).T
-
-    def placed(rows):
-        return rows[:36].reshape(6, 3, 2, 1024).transpose(2, 0, 1, 3)
-
-    return placed(coarse_out), placed(grad_merged), grad_down
+    tokens = shaped((6, 3, 2, 1024))
+    coarse_out, grad_merged = call(finish_kernel, (tokens, tokens), own_merged, cot, got)
+    grad_down = call(
+        line_sum_kernel, shaped((16, 512), F32), parts, after=(coarse_out, grad_merged)
+    ).T
+    return coarse_out.transpose(2, 0, 1, 3), grad_merged.transpose(2, 0, 1, 3), grad_down
 
 
 def solution(mesh):

time: 161 us -> 180 us (1.12)
  blocking collectives: 9.47 us -> 31.1 us
  starting transfers between devices: 66.6 us -> 78.1 us
  local copies, waits for them, and re-layouts: 12.4 us -> 3.82 us
  waiting for transfers between devices: 51.6 us -> 47 us
    all_to_all x1 -> x2, blocking collectives: 9.47 us -> 31.1 us  [exchanged(): return lax.all_to_all(value, axes, 0, 0)]
    ppermute x4 -> x2, waiting for transfers between devices: 29.5 us -> 8.8 us  [moved(): return lax.ppermute(value, LINE, [(s, target(s)) for s in range(COUNT)])]
    all_to_all x4 -> x5, waiting for transfers between devices: 15.1 us -> 35.5 us  [exchanged(): return lax.all_to_all(value, axes, 0, 0)]
    all_to_all x4 -> x5, starting transfers between devices: 25 us -> 37.5 us  [exchanged(): return lax.all_to_all(value, axes, 0, 0)]
    reshape x5 -> x0, local copies, waits for them, and re-layouts: 5.09 us -> none  [the longest x3 3.75 us: token_rows(): return block.transpose(1, 2, 0, 3).reshape(-1, block.shape[-1])]
    ppermute x2, starting transfers between devices: 14 us -> 18.4 us  [across(): return lax.ppermute(value, 'lat', [(0, 1), (1, 0)])]
    ppermute x1, waiting for transfers between devices: 4.35 us -> 0.01 us  [along_z(): return lax.ppermute(value, AXES, pairs)]
    ppermute x1, starting transfers between devices: 13.3 us -> 10.3 us  [along_z(): return lax.ppermute(value, AXES, pairs)]
  transfers between devices with their start and end apart: 11 -> 10, of which waited for: 8 -> 5; matrix products, arithmetic and copies ran while one was open for 4% -> 0% of each run, Pallas kernels for 2% -> 5%
where the time goes in v4:
time: 180 us; the launch traced here: 179 us
  starting transfers between devices  78.1 us (43%)
  waiting for transfers between devices  47 us (26%)
  blocking collectives  31.1 us (17%)
  Pallas kernels  18 us (10%)
  local copies, waits for them, and re-layouts  3.82 us (2%)
    all_to_all x5, starting transfers between devices, exchanged(): return lax.all_to_all(value, axes, 0, 0)  37.5 us
    all_to_all x5, waiting for transfers between devices, exchanged(): return lax.all_to_all(value, axes, 0, 0)  35.5 us
    all_to_all x2, blocking collectives, exchanged(): return lax.all_to_all(value, axes, 0, 0)  31.1 us
    ppermute x2, starting transfers between devices, across(): return lax.ppermute(value, 'lat', [(0, 1), (1, 0)])  18.4 us
    pallas_call x10, Pallas kernels, call(): pl.pallas_call(body, out_shape=out_shape, in_specs=specs, out_specs=jax.t...  15.3 us
    ppermute x2, starting transfers between devices, moved(): return lax.ppermute(value, LINE, [(s, target(s)) for s in range(COUNT)])  12 us
    ppermute x1, starting transfers between devices, along_z(): return lax.ppermute(value, AXES, pairs)  10.3 us
    ppermute x2, waiting for transfers between devices, moved(): return lax.ppermute(value, LINE, [(s, target(s)) for s in range(COUNT)])  8.8 us
  transfers between devices with their start and end apart: 10, of which 5 were waited for; matrix products, arithmetic and copies ran while one was open for 0% of the time, Pallas kernels for 5%

profile of v4, /device:TPU:1, one launch (start us, length us, event | category | flops | bytes accessed | tf_op | source)
XLA Modules:
  0.0 178.9 jit_solution(1732360042454989019)
XLA Ops:
  1.2 2.7 %prepare_kernel.1 = (bf16[72,512]{1,0:T(8,128)(2,1)}, bf16[72,512]{1,0:T(8,128)(2,1)}, bf16[80,512]{1,0:T(8,128)(2,1)}, bf16[4,40,1024]{2,1,0:T(8,128)(2,1)}) custom-call(s32[5]{0:T(128)} %stack.23.place.refs_0_, bf16[12,6,2,512]{3,2,1,0:T(2,128)(2,1)} %bitcast.12, bf16[6,3,2,1024]{3,2,1,0:T(2,128)(2,1)} %bitcast.13, bf16[2048,128]{1,0:T(8,128)(2,1)} %refs_1_.1, ...), custom_call_target="tpu_custom_call" | custom-call | tf_op jit(solution)/shard_map/prepare_kernel/pallas_call | solution.py:195
  4.0 6.5 %all-to-all-start = ((bf16[4,40,1024]{2,1,0:T(8,128)(2,1)}), bf16[4,40,1024]{2,1,0:T(8,128)(2,1)S(1)}, u32[]{:S(2)}, u32[]{:S(2)}) async-start(bf16[4,40,1024]{2,1,0:T(8,128)(2,1)} %get-tuple-element.18.refs_1_), calls=%async_computation | async-start | bytes 655360 | tf_op jit(solution)/shard_map/all_to_all | solution.py:54
  10.4 10.3 %collective-permute-start.2 = (bf16[80,512]{1,0:T(8,128)(2,1)}, bf16[80,512]{1,0:T(8,128)(2,1)S(1)}, u32[]{:S(2)}, u32[]{:S(2)}) collective-permute-start(bf16[80,512]{1,0:T(8,128)(2,1)} %get-tuple-element.17), channel_id=1, source_target_pairs={{0,4},{1,5},{2,6},{3,7},{4,128},{5,129},{6,130},{7,131},{8,12},{9,... | collective-permute-start | bytes 245768 | tf_op jit(solution)/shard_map/ppermute | solution.py:50
  20.7 10.1 %collective-permute-start.1 = (bf16[72,512]{1,0:T(8,128)(2,1)}, bf16[72,512]{1,0:T(8,128)(2,1)S(1)}, u32[]{:S(2)}, u32[]{:S(2)}) collective-permute-start(bf16[72,512]{1,0:T(8,128)(2,1)} %get-tuple-element.15.refs_0_), channel_id=1, source_target_pairs={{0,255},{1,0},{2,1},{3,2},{4,3},{5,4},{6,5},{7,6},{8,7},{9,8},{10,... | collective-permute-start | bytes 221192 | tf_op jit(solution)/shard_map/ppermute | solution.py:31
  30.8 1.9 %collective-permute-start = (bf16[72,512]{1,0:T(8,128)(2,1)}, bf16[72,512]{1,0:T(8,128)(2,1)S(1)}, u32[]{:S(2)}, u32[]{:S(2)}) collective-permute-start(bf16[72,512]{1,0:T(8,128)(2,1)} %get-tuple-element.16.refs_1_), channel_id=1, source_target_pairs={{0,1},{1,2},{2,3},{3,4},{4,5},{5,6},{6,7},{7,8},{8,9},{9,10},{10,1... | collective-permute-start | bytes 221192 | tf_op jit(solution)/shard_map/ppermute | solution.py:31
  32.7 8.8 %collective-permute-done.refs_1_.refs_2_ = bf16[72,512]{1,0:T(8,128)(2,1)S(1)} collective-permute-done((bf16[72,512]{1,0:T(8,128)(2,1)}, bf16[72,512]{1,0:T(8,128)(2,1)S(1)}, u32[]{:S(2)}, u32[]{:S(2)}) %collective-permute-start) | collective-permute-done | bytes 73760 | tf_op jit(solution)/shard_map/ppermute | solution.py:31
  42.7 4.2 %all-to-all-start.2 = ((bf16[16,80,512]{2,1,0:T(8,128)(2,1)}), bf16[16,80,512]{2,1,0:T(8,128)(2,1)S(1)}, u32[]{:S(2)}, u32[]{:S(2)}) async-start(bf16[16,80,512]{2,1,0:T(8,128)(2,1)} %spread_kernel.1.refs_7_), calls=%async_computation.2 | async-start | bytes 2621440 | tf_op jit(solution)/shard_map/all_to_all | solution.py:54
  46.9 1.4 copy-done.1
  48.3 3.6 %attend_kernel.1 = bf16[4,40,2048]{2,1,0:T(8,128)(2,1)} custom-call(bf16[72,512]{1,0:T(8,128)(2,1)S(1)} %copy-done.9, bf16[72,512]{1,0:T(8,128)(2,1)S(1)} %copy-done.10, bf16[72,512]{1,0:T(8,128)(2,1)S(1)} %collective-permute-done.refs_1_.refs_2_, bf16[72,512]{1,0:T(8,128)(2,1)S(1)} %collective-permute-done.1.refs_2_.refs_3_, ...), custom_call_target="tpu_custom_call" | custom-call | flops 1000000000 | bytes 2438144 | tf_op jit(solution)/shard_map/attend_kernel/pallas_call | solution.py:73
  51.9 9.3 %all-to-all-done.2.refs_1_ = bf16[16,80,512]{2,1,0:T(8,128)(2,1)S(1)} async-done(((bf16[16,80,512]{2,1,0:T(8,128)(2,1)}), bf16[16,80,512]{2,1,0:T(8,128)(2,1)S(1)}, u32[]{:S(2)}, u32[]{:S(2)}) %all-to-all-start.2) | async-done | bytes 1310752 | tf_op jit(solution)/shard_map/all_to_all | solution.py:54
  61.2 3.5 %all-to-all-start.1 = ((bf16[4,40,2048]{2,1,0:T(8,128)(2,1)}), bf16[4,40,2048]{2,1,0:T(8,128)(2,1)S(1)}, u32[]{:S(2)}, u32[]{:S(2)}) async-start(bf16[4,40,2048]{2,1,0:T(8,128)(2,1)} %attend_kernel.1), calls=%async_computation.1 | async-start | bytes 1310720 | tf_op jit(solution)/shard_map/all_to_all | solution.py:54
  64.7 10.5 %collective-permute-start.3 = (bf16[16,80,512]{2,1,0:T(8,128)(2,1)S(1)}, bf16[16,80,512]{2,1,0:T(8,128)(2,1)}, u32[]{:S(2)}, u32[]{:S(2)}) collective-permute-start(bf16[16,80,512]{2,1,0:T(8,128)(2,1)S(1)} %all-to-all-done.2.refs_1_), channel_id=1, source_target_pairs={{0,256},{256,0},{1,257},{257,1},{2,258},{258,2},{3,259},{259,3},{4... | collective-permute-start | bytes 3932168 | tf_op jit(solution)/shard_map/ppermute | solution.py:39
  75.3 2.8 %collective-permute-done.3.refs_2_ = bf16[16,80,512]{2,1,0:T(8,128)(2,1)} collective-permute-done((bf16[16,80,512]{2,1,0:T(8,128)(2,1)S(1)}, bf16[16,80,512]{2,1,0:T(8,128)(2,1)}, u32[]{:S(2)}, u32[]{:S(2)}) %collective-permute-start.3) | collective-permute-done | bytes 1310752 | tf_op jit(solution)/shard_map/ppermute | solution.py:39
  78.1 1.7 unpack_kernel.1
  80.3 11.4 %all_to_all.35.refs_1_ = bf16[4,4,40,256]{3,2,1,0:T(8,128)(2,1)S(1)} all-to-all(bf16[4,4,40,256]{3,2,1,0:T(8,128)(2,1)S(1)} %merge_kernel.1), channel_id=1, replica_groups=mesh['lat'=2,'z_hi'=2,'y'=4,'x'=4,'z_half'=2,'z_near'=4] {'z_near'}, dimensions={0} | all-to-all | bytes 655360 | tf_op jit(solution)/shard_map/all_to_all | solution.py:54
  91.7 1.4 hidden_kernel.1
  93.1 7.9 %collective-permute-start.4 = (bf16[160,1536]{1,0:T(8,128)(2,1)S(1)}, bf16[160,1536]{1,0:T(8,128)(2,1)S(1)}, u32[]{:S(2)}, u32[]{:S(2)}) collective-permute-start(bf16[160,1536]{1,0:T(8,128)(2,1)S(1)} %get-tuple-element.22.refs_0_.refs_2_), channel_id=1, source_target_pairs={{0,256},{256,0},{1,257},{257,1},{2,258},{258,2},{3,259},{259,3},{4... | collective-permute-start | bytes 1474568 | tf_op jit(solution)/shard_map/ppermute | solution.py:39
  101.0 2.7 %feed_kernel.1.refs_4_ = bf16[4,2,40,1024]{3,2,1,0:T(8,128)(2,1)} custom-call(bf16[160,1536]{1,0:T(8,128)(2,1)S(1)} %get-tuple-element.22.refs_0_.refs_2_, f32[160,1024]{1,0:T(8,128)S(1)} %get-tuple-element.23.refs_1_, bf16[4,40,1024]{2,1,0:T(8,128)(2,1)S(1)} %all-to-all-done.refs_3_.refs_2_.refs_1_, bf16[1024,512]{1,0:T(8,128)(2,1)S(1)} %copy-done.3, ...), custom_call_target="tpu_custom_call" | custom-call | flops 2000000000 | bytes 5668864 | tf_op jit(solution)/shard_map/feed_kernel/pallas_call | solution.py:73
  105.0 19.7 %all_to_all.36.refs_1_ = bf16[16,32,1024]{2,1,0:T(8,128)(2,1)S(1)} all-to-all(bf16[16,32,1024]{2,1,0:T(8,128)(2,1)S(1)} %weight_kernel.1), channel_id=1, replica_groups=mesh['lat'=2,'z_hi'=2,'y'=4,'x'=4,'z_half'=2,'z_near'=4] {'y','x'}, dimensions={0} | all-to-all | bytes 2097152 | tf_op jit(solution)/shard_map/all_to_all | solution.py:54
  124.7 3.6 %all-to-all-start.4 = ((bf16[4,2,40,1024]{3,2,1,0:T(8,128)(2,1)}), bf16[4,2,40,1024]{3,2,1,0:T(8,128)(2,1)S(1)}, u32[]{:S(2)}, u32[]{:S(2)}) async-start(bf16[4,2,40,1024]{3,2,1,0:T(8,128)(2,1)} %feed_kernel.1.refs_4_), calls=%async_computation.4 | async-start | bytes 1310720 | tf_op jit(solution)/shard_map/all_to_all | solution.py:54
  128.3 1.3 plane_sum_kernel.1
  129.7 15.4 %all-to-all-done.4.refs_2_ = bf16[4,2,40,1024]{3,2,1,0:T(8,128)(2,1)S(1)} async-done(((bf16[4,2,40,1024]{3,2,1,0:T(8,128)(2,1)}), bf16[4,2,40,1024]{3,2,1,0:T(8,128)(2,1)S(1)}, u32[]{:S(2)}, u32[]{:S(2)}) %all-to-all-start.4) | async-done | bytes 655392 | tf_op jit(solution)/shard_map/all_to_all | solution.py:54
  145.1 19.7 %all-to-all-start.6 = ((bf16[4,16,512]{2,1,0:T(8,128)(2,1)}), bf16[4,16,512]{2,1,0:T(8,128)(2,1)S(1)}, u32[]{:S(2)}, u32[]{:S(2)}) async-start(bf16[4,16,512]{2,1,0:T(8,128)(2,1)} %plane_sum_kernel.1), calls=%async_computation.6 | async-start | bytes 131072 | tf_op jit(solution)/shard_map/all_to_all | solution.py:54
  165.8 10.7 %all-to-all-done.6.refs_0_ = bf16[4,16,512]{2,1,0:T(8,128)(2,1)S(1)} async-done(((bf16[4,16,512]{2,1,0:T(8,128)(2,1)}), bf16[4,16,512]{2,1,0:T(8,128)(2,1)S(1)}, u32[]{:S(2)}, u32[]{:S(2)}) %all-to-all-start.6) | async-done | bytes 65568 | tf_op jit(solution)/shard_map/all_to_all | solution.py:54
  (34 shorter events, 7.0 us)
Async XLA Ops:
  4.0 37.6 %all-to-all-start = ((bf16[4,40,1024]{2,1,0:T(8,128)(2,1)}), bf16[4,40,1024]{2,1,0:T(8,128)(2,1)S(1)}, u32[]{:S(2)}, u32[]{:S(2)}) async-start(bf16[4,40,1024]{2,1,0:T(8,128)(2,1)} %get-tuple-element.18.refs_1_), calls=%async_computation | async-start | bytes 655360 | tf_op jit(solution)/shard_map/all_to_all | solution.py:54
  10.4 31.1 %collective-permute-start.2 = (bf16[80,512]{1,0:T(8,128)(2,1)}, bf16[80,512]{1,0:T(8,128)(2,1)S(1)}, u32[]{:S(2)}, u32[]{:S(2)}) collective-permute-start(bf16[80,512]{1,0:T(8,128)(2,1)} %get-tuple-element.17), channel_id=1, source_target_pairs={{0,4},{1,5},{2,6},{3,7},{4,128},{5,129},{6,130},{7,131},{8,12},{9,... | collective-permute-start | bytes 245768 | tf_op jit(solution)/shard_map/ppermute | solution.py:50
  20.7 12.0 %collective-permute-start.1 = (bf16[72,512]{1,0:T(8,128)(2,1)}, bf16[72,512]{1,0:T(8,128)(2,1)S(1)}, u32[]{:S(2)}, u32[]{:S(2)}) collective-permute-start(bf16[72,512]{1,0:T(8,128)(2,1)} %get-tuple-element.15.refs_0_), channel_id=1, source_target_pairs={{0,255},{1,0},{2,1},{3,2},{4,3},{5,4},{6,5},{7,6},{8,7},{9,8},{10,... | collective-permute-start | bytes 221192 | tf_op jit(solution)/shard_map/ppermute | solution.py:31
  30.8 10.7 %collective-permute-start = (bf16[72,512]{1,0:T(8,128)(2,1)}, bf16[72,512]{1,0:T(8,128)(2,1)S(1)}, u32[]{:S(2)}, u32[]{:S(2)}) collective-permute-start(bf16[72,512]{1,0:T(8,128)(2,1)} %get-tuple-element.16.refs_1_), channel_id=1, source_target_pairs={{0,1},{1,2},{2,3},{3,4},{4,5},{5,6},{6,7},{7,8},{8,9},{9,10},{10,1... | collective-permute-start | bytes 221192 | tf_op jit(solution)/shard_map/ppermute | solution.py:31
  42.7 4.2 %copy-start.5 = (bf16[512,512]{1,0:T(8,128)(2,1)S(1)}, bf16[512,512]{1,0:T(8,128)(2,1)}, u32[]{:S(2)}) copy-start(bf16[512,512]{1,0:T(8,128)(2,1)} %refs_5_.2) | copy-start | bytes 1572868
  42.7 4.2 %copy-start.6 = (bf16[160,144]{1,0:T(8,128)(2,1)S(1)}, bf16[160,144]{1,0:T(8,128)(2,1)}, u32[]{:S(2)}) copy-start(bf16[160,144]{1,0:T(8,128)(2,1)} %constant.22.clone.refs_6_) | copy-start | bytes 138244
  42.7 4.2 %copy-start.9 = (bf16[72,512]{1,0:T(8,128)(2,1)S(1)}, bf16[72,512]{1,0:T(8,128)(2,1)}, u32[]{:S(2)}) copy-start(bf16[72,512]{1,0:T(8,128)(2,1)} %get-tuple-element.15.refs_0_) | copy-start | bytes 221188
  42.7 4.2 %copy-start.10 = (bf16[72,512]{1,0:T(8,128)(2,1)S(1)}, bf16[72,512]{1,0:T(8,128)(2,1)}, u32[]{:S(2)}) copy-start(bf16[72,512]{1,0:T(8,128)(2,1)} %get-tuple-element.16.refs_1_) | copy-start | bytes 221188
  42.7 18.5 %all-to-all-start.2 = ((bf16[16,80,512]{2,1,0:T(8,128)(2,1)}), bf16[16,80,512]{2,1,0:T(8,128)(2,1)S(1)}, u32[]{:S(2)}, u32[]{:S(2)}) async-start(bf16[16,80,512]{2,1,0:T(8,128)(2,1)} %spread_kernel.1.refs_7_), calls=%async_computation.2 | async-start | bytes 2621440 | tf_op jit(solution)/shard_map/all_to_all | solution.py:54
  46.9 1.4 copy-start.1
  51.9 26.1 %copy-start.11 = (s32[5]{0:T(128)S(1)}, s32[5]{0:T(128)}, u32[]{:S(2)}) copy-start(s32[5]{0:T(128)} %stack.23.place.refs_0_) | copy-start | bytes 64
  61.2 14.0 %all-to-all-start.1 = ((bf16[4,40,2048]{2,1,0:T(8,128)(2,1)}), bf16[4,40,2048]{2,1,0:T(8,128)(2,1)S(1)}, u32[]{:S(2)}, u32[]{:S(2)}) async-start(bf16[4,40,2048]{2,1,0:T(8,128)(2,1)} %attend_kernel.1), calls=%async_computation.1 | async-start | bytes 1310720 | tf_op jit(solution)/shard_map/all_to_all | solution.py:54
  64.7 15.0 %copy-start = (bf16[2048,128]{1,0:T(8,128)(2,1)S(1)}, bf16[2048,128]{1,0:T(8,128)(2,1)}, u32[]{:S(2)}) copy-start(bf16[2048,128]{1,0:T(8,128)(2,1)} %refs_1_.1) | copy-start | bytes 1572868
  64.7 13.3 %collective-permute-start.3 = (bf16[16,80,512]{2,1,0:T(8,128)(2,1)S(1)}, bf16[16,80,512]{2,1,0:T(8,128)(2,1)}, u32[]{:S(2)}, u32[]{:S(2)}) collective-permute-start(bf16[16,80,512]{2,1,0:T(8,128)(2,1)S(1)} %all-to-all-done.2.refs_1_), channel_id=1, source_target_pairs={{0,256},{256,0},{1,257},{257,1},{2,258},{258,2},{3,259},{259,3},{4... | collective-permute-start | bytes 3932168 | tf_op jit(solution)/shard_map/ppermute | solution.py:39
  79.7 11.9 %copy-start.3 = (bf16[1024,512]{1,0:T(8,128)(2,1)S(1)}, bf16[1024,512]{1,0:T(8,128)(2,1)}, u32[]{:S(2)}) copy-start(bf16[1024,512]{1,0:T(8,128)(2,1)} %refs_3_.3) | copy-start | bytes 3145732
  91.7 9.3 %copy-start.4 = (bf16[512,1024]{1,0:T(8,128)(2,1)S(1)}, bf16[512,1024]{1,0:T(8,128)(2,1)}, u32[]{:S(2)}) copy-start(bf16[512,1024]{1,0:T(8,128)(2,1)} %refs_5_.3) | copy-start | bytes 3145732
  93.1 10.6 %collective-permute-start.4 = (bf16[160,1536]{1,0:T(8,128)(2,1)S(1)}, bf16[160,1536]{1,0:T(8,128)(2,1)S(1)}, u32[]{:S(2)}, u32[]{:S(2)}) collective-permute-start(bf16[160,1536]{1,0:T(8,128)(2,1)S(1)} %get-tuple-element.22.refs_0_.refs_2_), channel_id=1, source_target_pairs={{0,256},{256,0},{1,257},{257,1},{2,258},{258,2},{3,259},{259,3},{4... | collective-permute-start | bytes 1474568 | tf_op jit(solution)/shard_map/ppermute | solution.py:39
  124.7 40.1 %copy-start.2 = (bf16[4,40,1024]{2,1,0:T(8,128)(2,1)S(1)}, bf16[4,40,1024]{2,1,0:T(8,128)(2,1)}, u32[]{:S(2)}) copy-start(bf16[4,40,1024]{2,1,0:T(8,128)(2,1)} %get-tuple-element.18.refs_1_) | copy-start | bytes 983044
  124.7 20.4 %all-to-all-start.4 = ((bf16[4,2,40,1024]{3,2,1,0:T(8,128)(2,1)}), bf16[4,2,40,1024]{3,2,1,0:T(8,128)(2,1)S(1)}, u32[]{:S(2)}, u32[]{:S(2)}) async-start(bf16[4,2,40,1024]{3,2,1,0:T(8,128)(2,1)} %feed_kernel.1.refs_4_), calls=%async_computation.4 | async-start | bytes 1310720 | tf_op jit(solution)/shard_map/all_to_all | solution.py:54
  145.1 31.4 %all-to-all-start.6 = ((bf16[4,16,512]{2,1,0:T(8,128)(2,1)}), bf16[4,16,512]{2,1,0:T(8,128)(2,1)S(1)}, u32[]{:S(2)}, u32[]{:S(2)}) async-start(bf16[4,16,512]{2,1,0:T(8,128)(2,1)} %plane_sum_kernel.1), calls=%async_computation.6 | async-start | bytes 131072 | tf_op jit(solution)/shard_map/all_to_all | solution.py:54
  176.5 0.9 copy-start.7
  177.4 0.9 copy-start.8

commit v5 on v4

v5 whole, which is shorter than its diff:
```python
import jax
import jax.numpy as jnp
import numpy as np
from jax import lax
from jax.experimental import pallas as pl
from jax.experimental.pallas import tpu as pltpu
from jax.sharding import Mesh, PartitionSpec as P

EPS = 1e-05
F32 = jnp.float32
BF16 = jnp.bfloat16
AXES = ("lat", "z_hi", "y", "x", "z_half", "z_near")
LINE = AXES[1:]
COUNT = 256
ROWS = 40


def dot(a, b):
    return lax.dot_general(a, b, (((1,), (0,)), ((), ())), preferred_element_type=F32)


def dot_nt(a, b):
    return lax.dot_general(a, b, (((1,), (1,)), ((), ())), preferred_element_type=F32)


def dot_tn(a, b):
    return lax.dot_general(a, b, (((0,), (0,)), ((), ())), preferred_element_type=F32)


def moved(value, target):
    return lax.ppermute(value, LINE, [(s, target(s)) for s in range(COUNT)])


def swapped(value, bits):
    return moved(value, lambda s: s ^ bits)


def across(value):
    return lax.ppermute(value, "lat", [(0, 1), (1, 0)])


def along_z(value):
    pairs = []
    for lat, steps in ((0, 4), (1, -4)):
        for lon in range(32):
            for tp in range(8):
                z = ((lon >> 4) * 8 + tp + steps) % 16
                target = (z >> 3) * 128 + (lon & 15) * 8 + (z & 7)
                pairs.append((lat * COUNT + lon * 8 + tp, lat * COUNT + target))
    return lax.ppermute(value, AXES, pairs)


def exchanged(value, axes):
    return lax.all_to_all(value, axes, 0, 0)


def norm_rows(values):
    centred = values - jnp.mean(values, axis=-1, keepdims=True)
    variance = jnp.mean(centred * centred, axis=-1, keepdims=True)
    return centred * lax.rsqrt(variance + EPS)


def in_hbm(value):
    return pltpu.with_memory_space_constraint(value, pltpu.HBM)


def call(kernel, out_shape, *args, flops=0, scalars=0, hbm=(), hbm_out=0, after=(), through=(), limit=16, **kw):
    outs = out_shape if isinstance(out_shape, tuple) else (out_shape,)
    here, far = pl.BlockSpec(memory_space=pltpu.VMEM), pl.BlockSpec(memory_space=pltpu.HBM)
    scalar = pl.BlockSpec(memory_space=pltpu.SMEM)
    specs = [scalar if i < scalars else far if i in hbm else here for i in range(len(args))]
    first, last = len(args) + len(after), len(args) + len(after) + len(through)

    def body(*refs):
        kernel(*refs[: len(args)], *refs[last : last + len(outs)], *refs[last + len(outs) + len(through) :])

    size = sum(a.size * a.dtype.itemsize for a in args)
    result = pl.pallas_call(
        body,
        out_shape=tuple(pltpu.HBM(o.shape, o.dtype) if i < hbm_out else o for i, o in enumerate(outs))
        + tuple(pltpu.HBM(t.shape, t.dtype) for t in through),
        in_specs=specs + [far] * (len(after) + len(through)),
        out_specs=(far,) * hbm_out + (here,) * (len(outs) - hbm_out) + (far,) * len(through),
        input_output_aliases={first + i: len(outs) + i for i in range(len(through))},
        compiler_params=pltpu.CompilerParams(vmem_limit_bytes=limit * 1024 * 1024) if limit else None,
        cost_estimate=pl.CostEstimate(flops=flops, bytes_accessed=size, transcendentals=0),
        name=kernel.__name__,
        **kw,
    )(*(in_hbm(a) if i in hbm else a for i, a in enumerate(args)), *(in_hbm(a) for a in (*after, *through)))
    return result if len(result) > 1 else result[0]


def shaped(shape, dtype=BF16):
    return jax.ShapeDtypeStruct(shape, dtype)


def merge_order():
    order = np.zeros((2, 4 * ROWS, 144), np.float32)
    for odd in range(2):
        for quarter in range(4):
            d_lat, d_lon = quarter // 2, quarter % 2
            for token in range(36):
                lat, lon, lev = token // 6, token % 6 // 2, token % 2
                row, column = 2 * lat + d_lat, 2 * lon + d_lon
                side = column // 3 if odd else 1 - column // 3
                order[odd, ROWS * quarter + token, 72 * side + 6 * row + 2 * (column % 3) + lev] = 1.0
    return order.astype(jnp.bfloat16)


def started(copies):
    copies = [pltpu.make_async_copy(*c) for c in copies]
    for copy in copies:
        copy.start()
    return copies


def project_kernel(side0, side1, qkv, packed):
    tokens = jnp.concatenate([side0[...].astype(F32), side1[0:72].astype(F32)], axis=0)
    packed[...] = dot(norm_rows(tokens).astype(BF16), qkv[...]).astype(BF16)


def attend_kernel(place, side0, side1, own, got0, got1, qkv, out_w, order, result, merged_in, done):
    tokens = jnp.concatenate([side0[...].astype(F32), side1[0:72].astype(F32)], axis=0)
    others = jnp.concatenate([got0[...].astype(F32), got1[0:72].astype(F32)], axis=0)
    other_packed = dot(norm_rows(others).astype(BF16), qkv[:, 512:1536]).astype(BF16).astype(F32)
    packed = own[...].astype(F32)
    lane = lax.broadcasted_iota(jnp.int32, (1, 128), 1) // 32
    masks = [(lane == h).astype(F32) for h in range(4)]
    scale = 32 ** -0.5
    halves = []
    for window in range(2):
        rows = slice(72 * window, 72 * window + 72)
        parts = []
        for group in range(4):
            low = 128 * group
            queries = packed[rows, low : low + 128]
            keys = jnp.concatenate(
                [packed[rows, 512 + low : 640 + low], other_packed[rows, low : low + 128]], axis=0
            ).astype(BF16)
            values = jnp.concatenate(
                [packed[rows, 1024 + low : 1152 + low], other_packed[rows, 512 + low : 640 + low]], axis=0
            ).astype(BF16)
            stacked = jnp.concatenate([queries * m for m in masks], axis=0).astype(BF16)
            scores = dot_nt(stacked, keys) * scale
            scores = scores - jnp.max(scores, axis=-1, keepdims=True)
            scores = jnp.exp(scores)
            probs = (scores / jnp.sum(scores, axis=-1, keepdims=True)).astype(BF16)
            mixed = dot(probs, values)
            total = mixed[0:72] * masks[0]
            for h in range(1, 4):
                total = total + mixed[72 * h : 72 * h + 72] * masks[h]
            parts.append(total)
        halves.append(jnp.concatenate(parts, axis=1))
    mixed = jnp.concatenate(halves, axis=0).astype(BF16)
    section = (tokens + dot(mixed, out_w[...])).astype(BF16)
    spread = dot(order[place[4] & 1], section)
    wide = jnp.concatenate([spread[ROWS * q : ROWS * q + ROWS] for q in range(4)], axis=1)
    merged_in[...] = norm_rows(wide).astype(BF16)
    for copy in started([(merged_in, result, done)]):
        copy.wait()


def stacked_rows(blocks, columns):
    return jnp.concatenate([blocks[j, :, columns].astype(F32) for j in range(4)], axis=0).astype(BF16)


def merge_half(place, source, side, weight):
    for index in range(16):
        for q in range(4):
            weight[64 * index + 16 * q : 64 * index + 16 * q + 16, :] = source[index, 64:80, 128 * q : 128 * q + 128]
    return pl.ds(pl.multiple_of((place[0] ^ side) * 1024, 1024), 1024)


def merge_near_kernel(place, b0, b1, b2, b3, own_w, near, rows, own, part, blocks, weight, done):
    copies = started([(block, blocks.at[j], done.at[j]) for j, block in enumerate((b0, b1, b2, b3))])
    at = merge_half(place, near, 0, weight)
    for copy in copies:
        copy.wait()
    rows[...] = jnp.concatenate([blocks[j].astype(F32) for j in range(4)], axis=0).astype(BF16)
    own[...] = dot(rows[...], own_w[...])
    part[...] = dot(rows[:, at], weight[...])


def merge_kernel(place, rows, own, part, far, result, weight):
    at = merge_half(place, far, 1, weight)
    for half, part in enumerate((own[...], part[...] + dot(rows[:, at], weight[...]))):
        for j in range(4):
            piece = part[ROWS * j : ROWS * j + ROWS].astype(BF16)
            for copy in range(4):
                result[copy, place[4] ^ j, :, 128 * half : 128 * half + 128] = piece


def prepare_kernel(
    tokens, cotangent, merge, up, down, side0, side1, packed, cot, tokens_in, cot_in, done
):
    r = lax.axis_index("lat") * 16 + lax.axis_index("y") * 4 + lax.axis_index("x")
    east = 1 - (lax.axis_index("z_near") & 1)
    pairs = [
        (tokens, tokens_in),
        (cotangent, cot_in),
        (up.at[pl.ds(pl.multiple_of(r * 32, 32), 32), :], packed.at[0:32, :]),
    ]
    row = pl.ds(pl.multiple_of(r * 16, 16), 16)
    for half in range(2):
        pairs.append((down.at[row, 512 * half : 512 * half + 512], packed.at[32 + 16 * half : 48 + 16 * half, :]))
    for q in range(4):
        at = pl.ds(pl.multiple_of(r * 64 + 16 * q, 16), 16)
        pairs.append((merge.at[at, :], packed.at[64:80, 128 * q : 128 * q + 128]))
    copies = started([(a, b, done.at[i]) for i, (a, b) in enumerate(pairs)])
    copies[0].wait()
    for lat in range(12):
        for lon in range(3):
            rows = slice(6 * lat + 2 * lon, 6 * lat + 2 * lon + 2)
            side0[rows, :] = tokens_in[lat, 3 * east + lon]
            side1[rows, :] = tokens_in[lat, 3 * (1 - east) + lon]
    side1[72:96, :] = jnp.zeros((24, 512), BF16)
    copies[1].wait()
    for copy in range(4):
        for lat in range(6):
            for lon in range(3):
                cot[copy, 6 * lat + 2 * lon : 6 * lat + 2 * lon + 2, :] = cot_in[lat, lon]
        cot[copy, 36:40, :] = jnp.zeros((4, 1024), BF16)
    for copy in copies[2:]:
        copy.wait()


def prepare(tokens, cotangent, merge, up, down):
    hbm = pl.BlockSpec(memory_space=pltpu.HBM)
    vmem = pl.BlockSpec(memory_space=pltpu.VMEM)
    return pl.pallas_call(
        prepare_kernel,
        out_shape=(shaped((72, 512)), shaped((96, 512)), shaped((80, 512)), shaped((4, ROWS, 1024))),
        in_specs=[hbm] * 5,
        out_specs=(vmem,) * 4,
        scratch_shapes=[
            pltpu.VMEM((12, 6, 2, 512), BF16),
            pltpu.VMEM((6, 3, 2, 1024), BF16),
            pltpu.SemaphoreType.DMA((9,)),
        ],
        name="prepare_kernel",
    )(tokens.transpose(1, 2, 0, 3), cotangent.transpose(1, 2, 0, 3), merge, up, down)


def spread_kernel(piece, result, held, done):
    for copy in started([(piece, held, done.at[0])]):
        copy.wait()
    for copy in started([(held, result.at[i], done.at[i]) for i in range(16)]):
        copy.wait()


def after_kernel(result):
    result[...] = jnp.zeros(result.shape, F32)


def copy_kernel(source, result):
    result[...] = source[...]


def up_half(source):
    return source[:, 0:32, :].reshape(512, 512)


def down_half(source, columns):
    return source[:, 32 + 16 * columns : 48 + 16 * columns, :].reshape(256, 512)


def gelu_parts(values):
    cdf = 0.5 * (1.0 + lax.erf(values * np.float32(np.sqrt(0.5))))
    density = jnp.exp(-0.5 * values * values) * np.float32(1.0 / np.sqrt(2.0 * np.pi))
    return values * cdf, cdf + values * density


def hidden_kernel(
    place, up_hbm, columns, cots, near, far, own_merged, bundle, slope, merged, own, normed, up, done
):
    (fetch,) = started([(up_hbm, up, done.at[1])])
    lat, half_index, near_index = place[0], place[3], place[4]
    for j in range(4):
        for half in range(2):
            column = pl.multiple_of(((half_index ^ half) * 4 + j) * 128, 128)
            for block in range(4):
                merged[ROWS * block : ROWS * block + ROWS, pl.ds(column, 128)] = columns[
                    j, block, :, 128 * half : 128 * half + 128
                ].astype(F32)
    own[...] = merged[pl.ds(pl.multiple_of(near_index * ROWS, 8), ROWS), :].astype(BF16)
    (copy,) = started([(own, own_merged, done.at[0])])
    normed[...] = norm_rows(merged[...]).astype(BF16)
    fetch.wait()
    value, slope[:, 0:512] = gelu_parts(dot(normed[...], up[...]))
    bundle[:, 0:512] = value.astype(BF16)
    preact = 0.0
    for side, source in enumerate((near, far)):
        at = pl.ds(pl.multiple_of((lat ^ side) * 512, 512), 512)
        preact = preact + dot(normed[:, at], up_half(source))
    value, slope[:, 512:1024] = gelu_parts(preact)
    bundle[:, 512:1024] = value.astype(BF16)
    bundle[:, 1024:1536] = stacked_rows(cots, pl.ds(pl.multiple_of((1 - lat) * 512, 512), 512))
    copy.wait()


def feed_kernel(place, bundle, slope, cots, up, down, near, far, values, grads):
    cots = stacked_rows(cots, slice(0, 1024))
    grad = (dot_nt(cots, down[...]) * slope[:, 0:512]).astype(BF16)
    values[...] = dot(bundle[:, 0:512], down[...])
    grads[...] = dot_nt(grad, up[...])
    far_grads = []
    for side, source in enumerate((near, far)):
        at = pl.ds(pl.multiple_of(512 + (place[0] ^ side) * 256, 256), 256)
        grad = 0.0
        for half in range(2):
            columns = slice(512 * half, 512 * half + 512)
            part = down_half(source, half)
            values[:, columns] = values[:, columns] + dot(bundle[:, at], part)
            grad = grad + dot_nt(cots[:, columns], part)
        far_grads.append((grad * slope[:, at]).astype(BF16))
    first = jnp.where(place[0] == 0, far_grads[0].astype(F32), far_grads[1].astype(F32)).astype(BF16)
    second = jnp.where(place[0] == 0, far_grads[1].astype(F32), far_grads[0].astype(F32)).astype(BF16)
    grad = jnp.concatenate([first, second], axis=1)
    for side, source in enumerate((near, far)):
        at = pl.ds(pl.multiple_of((place[0] ^ side) * 512, 512), 512)
        grads[:, at] = grads[:, at] + dot_nt(grad, up_half(source))


def sum_of(parts):
    summed = parts[0].astype(F32)
    for index in range(1, parts.shape[0]):
        summed = summed + parts[index].astype(F32)
    return summed


def finish_kernel(
    merged_hbm, cot_hbm, p0, p1, p2, p3, coarse_out, grad_merged, merged, cot, parts, first, second, done
):
    copies = started(
        [(merged_hbm, merged, done.at[0]), (cot_hbm.at[0], cot, done.at[1])]
        + [(p, parts.at[j], done.at[2 + j]) for j, p in enumerate((p0, p1, p2, p3))]
    )
    for copy in copies:
        copy.wait()
    merged_f = merged[...].astype(F32)
    value, grad_normed = merged_f, 0.0
    for j in range(4):
        value = value + parts[j, 0].astype(F32)
        grad_normed = grad_normed + parts[j, 1].astype(F32)
    value = value.astype(BF16)
    centred = merged_f - jnp.mean(merged_f, axis=-1, keepdims=True)
    scale_inv = lax.rsqrt(jnp.mean(centred * centred, axis=-1, keepdims=True) + EPS)
    nhat = centred * scale_inv
    grad = cot[...].astype(F32) + scale_inv * (
        grad_normed
        - jnp.mean(grad_normed, axis=-1, keepdims=True)
        - nhat * jnp.mean(grad_normed * nhat, axis=-1, keepdims=True)
    )
    grad = grad.astype(BF16)
    for lat in range(6):
        for lon in range(3):
            rows = slice(6 * lat + 2 * lon, 6 * lat + 2 * lon + 2)
            first[lat, lon] = value[rows]
            second[lat, lon] = grad[rows]
    copies = started([(first, coarse_out, done.at[0]), (second, grad_merged, done.at[1])])
    for copy in copies:
        copy.wait()


def finish(*args):
    tokens = shaped((6, 3, 2, 1024))
    return call(
        finish_kernel, (tokens, tokens), *args, hbm=range(6), hbm_out=2,
        scratch_shapes=[
            pltpu.VMEM((ROWS, 1024), BF16),
            pltpu.VMEM((ROWS, 1024), BF16),
            pltpu.VMEM((4, 2, ROWS, 1024), BF16),
            pltpu.VMEM(tokens.shape, BF16),
            pltpu.VMEM(tokens.shape, BF16),
            pltpu.SemaphoreType.DMA((6,)),
        ],
    )


def weight_kernel(
    place, cots, bundle, other, values, grads, s0, s1, s2, s3, result, parts, held, done
):
    at = pl.ds(pl.multiple_of(place[0] * 512, 512), 512)
    rows = jnp.concatenate([stacked_rows(cots, at), other[:, 1024:1536]], axis=0)
    hidden = jnp.concatenate([bundle[:, 0:1024], other[:, 0:1024]], axis=0)
    copies = []
    for z_hi in range(2):
        total = dot_tn(rows[:, 256 * z_hi : 256 * z_hi + 256], hidden).astype(BF16)
        held[z_hi] = total.reshape(16, 16, 1024)
        copies += started([(held.at[z_hi], result.at[:, 16 * z_hi : 16 * z_hi + 16, :], done.at[4 + z_hi])])
    for j, sent in enumerate((s0, s1, s2, s3)):
        at = pl.ds(pl.multiple_of((place[4] ^ j) * ROWS, 8), ROWS)
        parts[j, 0] = values[at, :].astype(BF16)
        parts[j, 1] = grads[at, :].astype(BF16)
        copies += started([(parts.at[j], sent, done.at[j])])
    for copy in copies:
        copy.wait()


def plane_sum_kernel(place, parts, result, total):
    total[...] = sum_of(parts)
    for z_hi in range(2):
        for half in range(2):
            at = pl.ds(pl.multiple_of((place[3] ^ half) * 512, 512), 512)
            result[2 * z_hi + half] = total[16 * z_hi : 16 * z_hi + 16, at].astype(BF16)


def line_sum_kernel(parts, result):
    result[...] = sum_of(parts)


def on_device(fine_tokens, fine_qkv, fine_out, merge_weight, up_weight, down_weight, cotangent):
    place = jnp.stack([lax.axis_index(a) for a in ("lat", "y", "x", "z_half", "z_near")]).astype(jnp.int32)
    side0, side1, piece, cot = prepare(fine_tokens, cotangent, merge_weight, up_weight, down_weight)

    got0 = swapped(side0, 1)
    got1 = moved(side1, lambda s: (s + 1 if s % 2 else s - 1) % COUNT)
    piece = along_z(piece)
    cots = exchanged(cot, "z_near")

    own = call(project_kernel, shaped((144, 1536)), side0, side1, fine_qkv, flops=2 * 10**8)
    merged_in = call(
        attend_kernel, shaped((ROWS, 2048)), place, side0, side1, own, got0, got1, fine_qkv, fine_out,
        jnp.asarray(merge_order()), scalars=1, hbm_out=1, flops=10**9, after=(cots,),
        scratch_shapes=[pltpu.VMEM((ROWS, 2048), BF16), pltpu.SemaphoreType.DMA],
    )
    pieces = call(
        spread_kernel, shaped((16, 80, 512)), piece, hbm=(0,), hbm_out=1, after=(merged_in,),
        scratch_shapes=[pltpu.VMEM((80, 512), BF16), pltpu.SemaphoreType.DMA((16,))],
    )
    near = exchanged(pieces, ("y", "x"))
    ins = [merged_in] + [swapped(merged_in, j) for j in (3, 2, 1)][::-1]
    near = call(copy_kernel, shaped((16, 80, 512)), near, after=ins[1:])
    far = across(near)
    narrow = shaped((4 * ROWS, 128), F32)
    rows, own, part = call(
        merge_near_kernel, (shaped((4 * ROWS, 2048)), narrow, narrow), place, *ins, merge_weight, near,
        scalars=1, hbm=range(1, 5), flops=2 * 10**8,
        scratch_shapes=[
            pltpu.VMEM((4, ROWS, 2048), BF16),
            pltpu.VMEM((1024, 128), BF16),
            pltpu.SemaphoreType.DMA((4,)),
        ],
    )
    columns = call(
        merge_kernel, shaped((4, 4, ROWS, 256)), place, rows, own, part, far, scalars=1, flops=10**8,
        scratch_shapes=[pltpu.VMEM((1024, 128), BF16)],
    )
    columns = exchanged(columns, "z_near")
    own_merged, bundle, slope = call(
        hidden_kernel,
        (shaped((ROWS, 1024)), shaped((4 * ROWS, 1536)), shaped((4 * ROWS, 1024), F32)),
        place, up_weight, columns, cots, near, far, scalars=1, hbm=(1,), hbm_out=1, flops=10**9,
        scratch_shapes=[
            pltpu.VMEM((4 * ROWS, 1024), F32),
            pltpu.VMEM((ROWS, 1024), BF16),
            pltpu.VMEM((4 * ROWS, 1024), BF16),
            pltpu.VMEM((1024, 512), BF16),
            pltpu.SemaphoreType.DMA((2,)),
        ],
    )
    other = across(bundle)
    wide = shaped((4 * ROWS, 1024), F32)
    values, grads = call(
        feed_kernel, (wide, wide), place, bundle, slope, cots, up_weight, down_weight, near, far, scalars=1,
        flops=2 * 10**9,
    )
    partial = shaped((2, ROWS, 1024))
    *partials, parts = call(
        weight_kernel, (partial,) * 4 + (shaped((16, 32, 1024)),), place, cots, bundle, other, values, grads,
        scalars=1, hbm_out=5, flops=3 * 10**8,
        scratch_shapes=[
            pltpu.VMEM((4, 2, ROWS, 1024), BF16),
            pltpu.VMEM((2, 16, 16, 1024), BF16),
            pltpu.SemaphoreType.DMA((6,)),
        ],
    )
    parts = exchanged(parts, ("y", "x"))
    partials = [partials[0]] + [swapped(partials[j], j) for j in (3, 2, 1)][::-1]
    parts = call(
        plane_sum_kernel, shaped((4, 16, 512)), place, parts, scalars=1, after=partials[1:],
        scratch_shapes=[pltpu.VMEM((32, 1024), F32)],
    )
    parts = exchanged(parts, ("z_hi", "z_half"))
    coarse_out, grad_merged = finish(own_merged, cot, *partials)
    grad_down, coarse_out, grad_merged = call(
        line_sum_kernel, shaped((16, 512), F32), parts, through=(coarse_out, grad_merged)
    )
    grad_down = grad_down.T
    return coarse_out.transpose(2, 0, 1, 3), grad_merged.transpose(2, 0, 1, 3), grad_down


def solution(mesh):
    lon, tp = ("z_hi", "y", "x"), ("z_half", "z_near")
    parts = Mesh(mesh.devices.reshape(2, 2, 4, 4, 2, 4), AXES)
    tokens = P(None, "lat", lon + tp, None)
    return jax.shard_map(
        on_device,
        mesh=parts,
        in_specs=(tokens, P(), P(), P(None, tp), P(None, tp), P(tp, None), tokens),
        out_specs=(tokens, tokens, P(tp, ("lat",) + lon)),
        check_vma=False,
    )
```

time: 180 us -> 145 us (0.81)
  the two profiles are of different devices: /device:TPU:1 before, /device:TPU:34 now
where the time goes in v5:
time: 145 us; the launch traced here: 144 us
  starting transfers between devices  67.3 us (46%)
  waiting for transfers between devices  34.1 us (24%)
  Pallas kernels  23.3 us (16%)
  blocking collectives  14.5 us (10%)
  local copies, waits for them, and re-layouts  3.93 us (3%)
    ppermute x8, starting transfers between devices, moved(): return lax.ppermute(value, LINE, [(s, target(s)) for s in range(COUNT)])  32.8 us
    all_to_all x4, starting transfers between devices, exchanged(): return lax.all_to_all(value, axes, 0, 0)  28.8 us
    pallas_call x12, Pallas kernels, call(): pl.pallas_call(body, out_shape=tuple((pltpu.HBM(o.shape, o.dtype) if i <...  21.1 us
    ppermute x8, waiting for transfers between devices, moved(): return lax.ppermute(value, LINE, [(s, target(s)) for s in range(COUNT)])  19.2 us
    all_to_all x1, blocking collectives, exchanged(): return lax.all_to_all(value, axes, 0, 0)  14.5 us
    all_to_all x4, waiting for transfers between devices, exchanged(): return lax.all_to_all(value, axes, 0, 0)  12 us
    unnamed x42, local copies, waits for them, and re-layouts  3.84 us
    ppermute x2, starting transfers between devices, across(): return lax.ppermute(value, 'lat', [(0, 1), (1, 0)])  3.84 us
  transfers between devices with their start and end apart: 15, of which 8 were waited for; matrix products, arithmetic and copies ran while one was open for 0% of the time, Pallas kernels for 8%

profile of v5, /device:TPU:34, one launch (start us, length us, event | category | flops | bytes accessed | tf_op | source)
XLA Modules:
  0.0 144.1 jit_solution(6790610242527215841)
XLA Ops:
  0.6 2.2 %prepare_kernel.1 = (bf16[72,512]{1,0:T(8,128)(2,1)}, bf16[96,512]{1,0:T(8,128)(2,1)}, bf16[80,512]{1,0:T(8,128)(2,1)}, bf16[4,40,1024]{2,1,0:T(8,128)(2,1)}) custom-call(bf16[12,6,2,512]{3,2,1,0:T(2,128)(2,1)} %bitcast.10, bf16[6,3,2,1024]{3,2,1,0:T(2,128)(2,1)} %bitcast.11, bf16[2048,128]{1,0:T(8,128)(2,1)} %refs_5_.2, bf16[1024,512]{1,0:T(8,128)(2,1)} %refs_4_.1, ...), custom_call_target="tpu_custom_call" | custom-call | tf_op jit(solution)/shard_map/prepare_kernel/pallas_call | solution.py:230
  2.9 6.1 %all-to-all-start = ((bf16[4,40,1024]{2,1,0:T(8,128)(2,1)}), bf16[4,40,1024]{2,1,0:T(8,128)(2,1)S(1)}, u32[]{:S(2)}, u32[]{:S(2)}) async-start(bf16[4,40,1024]{2,1,0:T(8,128)(2,1)} %get-tuple-element.25.refs_1_), calls=%async_computation | async-start | bytes 655360 | tf_op jit(solution)/shard_map/all_to_all | solution.py:54
  9.0 3.4 %collective-permute-start.1 = (bf16[96,512]{1,0:T(8,128)(2,1)}, bf16[96,512]{1,0:T(8,128)(2,1)S(1)}, u32[]{:S(2)}, u32[]{:S(2)}) collective-permute-start(bf16[96,512]{1,0:T(8,128)(2,1)} %get-tuple-element.27.refs_1_.refs_2_), channel_id=1, source_target_pairs={{0,255},{1,2},{2,1},{3,4},{4,3},{5,6},{6,5},{7,8},{8,7},{9,10},{10... | collective-permute-start | bytes 294920 | tf_op jit(solution)/shard_map/ppermute | solution.py:31
  12.4 10.9 %collective-permute-start = (bf16[72,512]{1,0:T(8,128)(2,1)}, bf16[72,512]{1,0:T(8,128)(2,1)S(1)}, u32[]{:S(2)}, u32[]{:S(2)}) collective-permute-start(bf16[72,512]{1,0:T(8,128)(2,1)} %get-tuple-element.26.refs_0_.refs_1_), channel_id=1, source_target_pairs={{0,1},{1,0},{2,3},{3,2},{4,5},{5,4},{6,7},{7,6},{8,9},{9,8},{10,11... | collective-permute-start | bytes 221192 | tf_op jit(solution)/shard_map/ppermute | solution.py:31
  28.4 3.6 %attend_kernel.1.refs_1_ = bf16[40,2048]{1,0:T(8,128)(2,1)} custom-call(s32[5]{0:T(128)S(1)} %stack.23.refs_0_, bf16[72,512]{1,0:T(8,128)(2,1)S(1)} %copy-done.7, bf16[96,512]{1,0:T(8,128)(2,1)S(1)} %copy-done.6, bf16[144,1536]{1,0:T(8,128)(2,1)S(1)} %project_kernel.1.refs_3_, bf16[72,512]{1,0:T(8,128)(2,1)S(1)} %collective-permute-done.refs_4_, ...), custom_call_target="tpu_custom_call" | custom-call | flops 1000000000 | bytes 2975764 | tf_op jit(solution)/shard_map/attend_kernel/pallas_call | solution.py:78
  34.7 2.1 %spread_kernel.1 = bf16[16,80,512]{2,1,0:T(8,128)(2,1)} custom-call(bf16[80,512]{1,0:T(8,128)(2,1)} %copy-done.17, bf16[40,2048]{1,0:T(8,128)(2,1)} %attend_kernel.1.refs_1_), custom_call_target="tpu_custom_call" | custom-call | bytes 81920 | tf_op jit(solution)/shard_map/spread_kernel/pallas_call | solution.py:78
  36.8 8.5 %all-to-all-start.1 = ((bf16[16,80,512]{2,1,0:T(8,128)(2,1)}), bf16[16,80,512]{2,1,0:T(8,128)(2,1)S(1)}, u32[]{:S(2)}, u32[]{:S(2)}) async-start(bf16[16,80,512]{2,1,0:T(8,128)(2,1)} %spread_kernel.1), calls=%async_computation.1 | async-start | bytes 2621440 | tf_op jit(solution)/shard_map/all_to_all | solution.py:54
  47.5 4.5 %collective-permute-start.3 = (bf16[40,2048]{1,0:T(8,128)(2,1)S(1)}, bf16[40,2048]{1,0:T(8,128)(2,1)S(1)}, u32[]{:S(2)}, u32[]{:S(2)}) collective-permute-start(bf16[40,2048]{1,0:T(8,128)(2,1)S(1)} %copy-done.13), channel_id=1, source_target_pairs={{0,2},{1,3},{2,0},{3,1},{4,6},{5,7},{6,4},{7,5},{8,10},{9,11},{10,... | collective-permute-start | bytes 491528 | tf_op jit(solution)/shard_map/ppermute | solution.py:31
  51.9 2.8 %collective-permute-start.2 = (bf16[40,2048]{1,0:T(8,128)(2,1)S(1)}, bf16[40,2048]{1,0:T(8,128)(2,1)S(1)}, u32[]{:S(2)}, u32[]{:S(2)}) collective-permute-start(bf16[40,2048]{1,0:T(8,128)(2,1)S(1)} %copy-done.13), channel_id=1, source_target_pairs={{0,1},{1,0},{2,3},{3,2},{4,5},{5,4},{6,7},{7,6},{8,9},{9,8},{10,11... | collective-permute-start | bytes 491528 | tf_op jit(solution)/shard_map/ppermute | solution.py:31
  54.8 5.1 %collective-permute-done.4.refs_3_.refs_4_ = bf16[40,2048]{1,0:T(8,128)(2,1)S(1)} collective-permute-done((bf16[40,2048]{1,0:T(8,128)(2,1)S(1)}, bf16[40,2048]{1,0:T(8,128)(2,1)S(1)}, u32[]{:S(2)}, u32[]{:S(2)}) %collective-permute-start.4) | collective-permute-done | bytes 163872 | tf_op jit(solution)/shard_map/ppermute | solution.py:31
  64.8 2.1 %merge_near_kernel.1 = (bf16[160,2048]{1,0:T(8,128)(2,1)S(1)}, f32[160,128]{1,0:T(8,128)S(1)}, f32[160,128]{1,0:T(8,128)S(1)}) custom-call(s32[5]{0:T(128)S(1)} %stack.23.refs_0_, bf16[40,2048]{1,0:T(8,128)(2,1)} %attend_kernel.1.refs_1_, bf16[40,2048]{1,0:T(8,128)(2,1)} %copy-done.12, bf16[40,2048]{1,0:T(8,128)(2,1)} %copy-done.11, ...), custom_call_target="tpu_custom_call" | custom-call | flops 200000000 | bytes 2490388 | tf_op jit(solution)/shard_map/merge_near_kernel/pallas_call | solution.py:78
  68.6 14.5 %all_to_all.25.refs_2_ = bf16[4,4,40,256]{3,2,1,0:T(8,128)(2,1)S(1)} all-to-all(bf16[4,4,40,256]{3,2,1,0:T(8,128)(2,1)S(1)} %merge_kernel.1), channel_id=1, replica_groups=mesh['lat'=2,'z_hi'=2,'y'=4,'x'=4,'z_half'=2,'z_near'=4] {'z_near'}, dimensions={0} | all-to-all | bytes 655360 | tf_op jit(solution)/shard_map/all_to_all | solution.py:54
  83.0 2.6 %hidden_kernel.1 = (bf16[40,1024]{1,0:T(8,128)(2,1)}, bf16[160,1536]{1,0:T(8,128)(2,1)S(1)}, f32[160,1024]{1,0:T(8,128)S(1)}) custom-call(s32[5]{0:T(128)S(1)} %stack.23.refs_0_, bf16[1024,512]{1,0:T(8,128)(2,1)} %refs_4_.1, bf16[4,4,40,256]{3,2,1,0:T(8,128)(2,1)S(1)} %all_to_all.25.refs_2_, bf16[4,40,1024]{2,1,0:T(8,128)(2,1)S(1)} %copy-done.2, ...), custom_call_target="tpu_custom_call" | custom-call | flops 1000000000 | bytes 4325396 | tf_op jit(solution)/shard_map/hidden_kernel/pallas_call | solution.py:78
  87.6 2.4 %feed_kernel.1 = (f32[160,1024]{1,0:T(8,128)S(1)}, f32[160,1024]{1,0:T(8,128)S(1)}) custom-call(s32[5]{0:T(128)S(1)} %stack.23.refs_0_, bf16[160,1536]{1,0:T(8,128)(2,1)S(1)} %get-tuple-element.32.refs_1_.refs_2_, f32[160,1024]{1,0:T(8,128)S(1)} %get-tuple-element.33.refs_2_, bf16[4,40,1024]{2,1,0:T(8,128)(2,1)S(1)} %copy-done.2, ...), custom_call_target="tpu_custom_call" | custom-call | flops 2000000000 | bytes 6193172 | tf_op jit(solution)/shard_map/feed_kernel/pallas_call | solution.py:78
  90.1 2.4 %weight_kernel.1 = (bf16[2,40,1024]{2,1,0:T(8,128)(2,1)}, bf16[2,40,1024]{2,1,0:T(8,128)(2,1)}, bf16[2,40,1024]{2,1,0:T(8,128)(2,1)}, bf16[2,40,1024]{2,1,0:T(8,128)(2,1)}, bf16[16,32,1024]{2,1,0:T(8,128)(2,1)}) custom-call(s32[5]{0:T(128)S(1)} %stack.23.refs_0_, bf16[4,40,1024]{2,1,0:T(8,128)(2,1)S(1)} %copy-done.2, ...), custom_call_target="tpu_custom_call" | custom-call | flops 300000000 | bytes 2621460 | tf_op jit(solution)/shard_map/weight_kernel/pallas_call | solution.py:78
  92.5 7.4 %all-to-all-start.3 = ((bf16[16,32,1024]{2,1,0:T(8,128)(2,1)}), bf16[16,32,1024]{2,1,0:T(8,128)(2,1)S(1)}, u32[]{:S(2)}, u32[]{:S(2)}) async-start(bf16[16,32,1024]{2,1,0:T(8,128)(2,1)} %get-tuple-element.36), calls=%async_computation.3 | async-start | bytes 2097152 | tf_op jit(solution)/shard_map/all_to_all | solution.py:54
  99.9 3.5 %collective-permute-start.8 = (bf16[2,40,1024]{2,1,0:T(8,128)(2,1)S(1)}, bf16[2,40,1024]{2,1,0:T(8,128)(2,1)S(1)}, u32[]{:S(2)}, u32[]{:S(2)}) collective-permute-start(bf16[2,40,1024]{2,1,0:T(8,128)(2,1)S(1)} %copy-done.20), channel_id=1, source_target_pairs={{0,1},{1,0},{2,3},{3,2},{4,5},{5,4},{6,7},{7,6},{8,9},{9,8},{10,11... | collective-permute-start | bytes 491528 | tf_op jit(solution)/shard_map/ppermute | solution.py:31
  103.5 2.3 %collective-permute-start.9 = (bf16[2,40,1024]{2,1,0:T(8,128)(2,1)S(1)}, bf16[2,40,1024]{2,1,0:T(8,128)(2,1)S(1)}, u32[]{:S(2)}, u32[]{:S(2)}) collective-permute-start(bf16[2,40,1024]{2,1,0:T(8,128)(2,1)S(1)} %copy-done.19), channel_id=1, source_target_pairs={{0,2},{1,3},{2,0},{3,1},{4,6},{5,7},{6,4},{7,5},{8,10},{9,11},{10,... | collective-permute-start | bytes 491528 | tf_op jit(solution)/shard_map/ppermute | solution.py:31
  105.8 3.4 %collective-permute-start.10 = (bf16[2,40,1024]{2,1,0:T(8,128)(2,1)S(1)}, bf16[2,40,1024]{2,1,0:T(8,128)(2,1)S(1)}, u32[]{:S(2)}, u32[]{:S(2)}) collective-permute-start(bf16[2,40,1024]{2,1,0:T(8,128)(2,1)S(1)} %copy-done.18), channel_id=1, source_target_pairs={{0,3},{1,2},{2,1},{3,0},{4,7},{5,6},{6,5},{7,4},{8,11},{9,10},{10,... | collective-permute-start | bytes 491528 | tf_op jit(solution)/shard_map/ppermute | solution.py:31
  109.2 8.1 %collective-permute-done.9.refs_3_.refs_4_ = bf16[2,40,1024]{2,1,0:T(8,128)(2,1)S(1)} collective-permute-done((bf16[2,40,1024]{2,1,0:T(8,128)(2,1)S(1)}, bf16[2,40,1024]{2,1,0:T(8,128)(2,1)S(1)}, u32[]{:S(2)}, u32[]{:S(2)}) %collective-permute-start.9) | collective-permute-done | bytes 163872 | tf_op jit(solution)/shard_map/ppermute | solution.py:31
  117.3 4.2 %collective-permute-done.10.refs_4_.refs_5_ = bf16[2,40,1024]{2,1,0:T(8,128)(2,1)S(1)} collective-permute-done((bf16[2,40,1024]{2,1,0:T(8,128)(2,1)S(1)}, bf16[2,40,1024]{2,1,0:T(8,128)(2,1)S(1)}, u32[]{:S(2)}, u32[]{:S(2)}) %collective-permute-start.10) | collective-permute-done | bytes 163872 | tf_op jit(solution)/shard_map/ppermute | solution.py:31
  123.6 6.7 %all-to-all-start.4 = ((bf16[4,16,512]{2,1,0:T(8,128)(2,1)}), bf16[4,16,512]{2,1,0:T(8,128)(2,1)S(1)}, u32[]{:S(2)}, u32[]{:S(2)}) async-start(bf16[4,16,512]{2,1,0:T(8,128)(2,1)} %plane_sum_kernel.1), calls=%async_computation.4 | async-start | bytes 131072 | tf_op jit(solution)/shard_map/all_to_all | solution.py:54
  130.3 2.2 %finish_kernel.1 = (bf16[6,3,2,1024]{3,2,1,0:T(2,128)(2,1)}, bf16[6,3,2,1024]{3,2,1,0:T(2,128)(2,1)}) custom-call(bf16[40,1024]{1,0:T(8,128)(2,1)} %get-tuple-element.40.refs_0_, bf16[4,40,1024]{2,1,0:T(8,128)(2,1)} %get-tuple-element.25.refs_1_, bf16[2,40,1024]{2,1,0:T(8,128)(2,1)} %get-tuple-element.41.refs_2_, bf16[2,40,1024]{2,1,0:T(8,128)(2,1)} %copy-done.14, ...), custom_call_target="tpu_custom_call" | custom-call | bytes 1064960 | tf_op jit(solution)/shard_map/finish_kernel/pallas_call | solution.py:78
  132.5 10.9 %all-to-all-done.4.refs_0_ = bf16[4,16,512]{2,1,0:T(8,128)(2,1)S(1)} async-done(((bf16[4,16,512]{2,1,0:T(8,128)(2,1)}), bf16[4,16,512]{2,1,0:T(8,128)(2,1)S(1)}, u32[]{:S(2)}, u32[]{:S(2)}) %all-to-all-start.4) | async-done | bytes 65568 | tf_op jit(solution)/shard_map/all_to_all | solution.py:54
  (63 shorter events, 20.9 us)
Async XLA Ops:
  0.6 24.7 %copy-start.4 = (bf16[512,1536]{1,0:T(8,128)(2,1)S(1)}, bf16[512,1536]{1,0:T(8,128)(2,1)}, u32[]{:S(2)}) copy-start(bf16[512,1536]{1,0:T(8,128)(2,1)} %refs_6_.1) | copy-start | bytes 4718596
  2.9 25.5 %copy-start.8 = (bf16[512,512]{1,0:T(8,128)(2,1)S(1)}, bf16[512,512]{1,0:T(8,128)(2,1)}, u32[]{:S(2)}) copy-start(bf16[512,512]{1,0:T(8,128)(2,1)} %refs_7_.1) | copy-start | bytes 1572868
  2.9 25.5 %copy-start.9 = (bf16[2,160,144]{2,1,0:T(8,128)(2,1)S(1)}, bf16[2,160,144]{2,1,0:T(8,128)(2,1)}, u32[]{:S(2)}) copy-start(bf16[2,160,144]{2,1,0:T(8,128)(2,1)} %constant.22.clone.refs_8_) | copy-start | bytes 276484
  2.9 24.8 %all-to-all-start = ((bf16[4,40,1024]{2,1,0:T(8,128)(2,1)}), bf16[4,40,1024]{2,1,0:T(8,128)(2,1)S(1)}, u32[]{:S(2)}, u32[]{:S(2)}) async-start(bf16[4,40,1024]{2,1,0:T(8,128)(2,1)} %get-tuple-element.25.refs_1_), calls=%async_computation | async-start | bytes 655360 | tf_op jit(solution)/shard_map/all_to_all | solution.py:54
  9.0 18.6 %collective-permute-start.1 = (bf16[96,512]{1,0:T(8,128)(2,1)}, bf16[96,512]{1,0:T(8,128)(2,1)S(1)}, u32[]{:S(2)}, u32[]{:S(2)}) collective-permute-start(bf16[96,512]{1,0:T(8,128)(2,1)} %get-tuple-element.27.refs_1_.refs_2_), channel_id=1, source_target_pairs={{0,255},{1,2},{2,1},{3,4},{4,3},{5,6},{6,5},{7,8},{8,7},{9,10},{10... | collective-permute-start | bytes 294920 | tf_op jit(solution)/shard_map/ppermute | solution.py:31
  12.4 15.2 %collective-permute-start = (bf16[72,512]{1,0:T(8,128)(2,1)}, bf16[72,512]{1,0:T(8,128)(2,1)S(1)}, u32[]{:S(2)}, u32[]{:S(2)}) collective-permute-start(bf16[72,512]{1,0:T(8,128)(2,1)} %get-tuple-element.26.refs_0_.refs_1_), channel_id=1, source_target_pairs={{0,1},{1,0},{2,3},{3,2},{4,5},{5,4},{6,7},{7,6},{8,9},{9,8},{10,11... | collective-permute-start | bytes 221192 | tf_op jit(solution)/shard_map/ppermute | solution.py:31
  23.3 10.8 %collective-permute-start.5 = (bf16[80,512]{1,0:T(8,128)(2,1)}, bf16[80,512]{1,0:T(8,128)(2,1)S(1)}, u32[]{:S(2)}, u32[]{:S(2)}) collective-permute-start(bf16[80,512]{1,0:T(8,128)(2,1)} %get-tuple-element.28), channel_id=1, source_target_pairs={{0,4},{1,5},{2,6},{3,7},{4,128},{5,129},{6,130},{7,131},{8,12},{9,... | collective-permute-start | bytes 245768 | tf_op jit(solution)/shard_map/ppermute | solution.py:50
  36.8 8.6 %copy-start.13 = (bf16[40,2048]{1,0:T(8,128)(2,1)S(1)}, bf16[40,2048]{1,0:T(8,128)(2,1)}, u32[]{:S(2)}) copy-start(bf16[40,2048]{1,0:T(8,128)(2,1)} %attend_kernel.1.refs_1_) | copy-start | bytes 491524
  36.8 25.9 %all-to-all-start.1 = ((bf16[16,80,512]{2,1,0:T(8,128)(2,1)}), bf16[16,80,512]{2,1,0:T(8,128)(2,1)S(1)}, u32[]{:S(2)}, u32[]{:S(2)}) async-start(bf16[16,80,512]{2,1,0:T(8,128)(2,1)} %spread_kernel.1), calls=%async_computation.1 | async-start | bytes 2621440 | tf_op jit(solution)/shard_map/all_to_all | solution.py:54
  45.4 19.4 %copy-start.3 = (bf16[2048,128]{1,0:T(8,128)(2,1)S(1)}, bf16[2048,128]{1,0:T(8,128)(2,1)}, u32[]{:S(2)}) copy-start(bf16[2048,128]{1,0:T(8,128)(2,1)} %refs_5_.2) | copy-start | bytes 1572868
  45.4 14.4 %collective-permute-start.4 = (bf16[40,2048]{1,0:T(8,128)(2,1)S(1)}, bf16[40,2048]{1,0:T(8,128)(2,1)S(1)}, u32[]{:S(2)}, u32[]{:S(2)}) collective-permute-start(bf16[40,2048]{1,0:T(8,128)(2,1)S(1)} %copy-done.13), channel_id=1, source_target_pairs={{0,3},{1,2},{2,1},{3,0},{4,7},{5,6},{6,5},{7,4},{8,11},{9,10},{10,... | collective-permute-start | bytes 491528 | tf_op jit(solution)/shard_map/ppermute | solution.py:31
  47.5 14.1 %collective-permute-start.3 = (bf16[40,2048]{1,0:T(8,128)(2,1)S(1)}, bf16[40,2048]{1,0:T(8,128)(2,1)S(1)}, u32[]{:S(2)}, u32[]{:S(2)}) collective-permute-start(bf16[40,2048]{1,0:T(8,128)(2,1)S(1)} %copy-done.13), channel_id=1, source_target_pairs={{0,2},{1,3},{2,0},{3,1},{4,6},{5,7},{6,4},{7,5},{8,10},{9,11},{10,... | collective-permute-start | bytes 491528 | tf_op jit(solution)/shard_map/ppermute | solution.py:31
  51.9 9.7 %collective-permute-start.2 = (bf16[40,2048]{1,0:T(8,128)(2,1)S(1)}, bf16[40,2048]{1,0:T(8,128)(2,1)S(1)}, u32[]{:S(2)}, u32[]{:S(2)}) collective-permute-start(bf16[40,2048]{1,0:T(8,128)(2,1)S(1)} %copy-done.13), channel_id=1, source_target_pairs={{0,1},{1,0},{2,3},{3,2},{4,5},{5,4},{6,7},{7,6},{8,9},{9,8},{10,11... | collective-permute-start | bytes 491528 | tf_op jit(solution)/shard_map/ppermute | solution.py:31
  62.8 4.9 %collective-permute-start.6 = (bf16[16,80,512]{2,1,0:T(8,128)(2,1)S(1)}, bf16[16,80,512]{2,1,0:T(8,128)(2,1)S(1)}, u32[]{:S(2)}, u32[]{:S(2)}) collective-permute-start(bf16[16,80,512]{2,1,0:T(8,128)(2,1)S(1)} %copy_kernel.1.refs_6_.refs_4_), channel_id=1, source_target_pairs={{0,256},{256,0},{1,257},{257,1},{2,258},{258,2},{3,259},{259,3},{4... | collective-permute-start | bytes 3932168 | tf_op jit(solution)/shard_map/ppermute | solution.py:39
  67.8 15.3 %copy-start.2 = (bf16[4,40,1024]{2,1,0:T(8,128)(2,1)S(1)}, bf16[4,40,1024]{2,1,0:T(8,128)(2,1)}, u32[]{:S(2)}) copy-start(bf16[4,40,1024]{2,1,0:T(8,128)(2,1)} %copy-done.1) | copy-start | bytes 983044
  85.7 4.4 %collective-permute-start.7 = (bf16[160,1536]{1,0:T(8,128)(2,1)S(1)}, bf16[160,1536]{1,0:T(8,128)(2,1)S(1)}, u32[]{:S(2)}, u32[]{:S(2)}) collective-permute-start(bf16[160,1536]{1,0:T(8,128)(2,1)S(1)} %get-tuple-element.32.refs_1_.refs_2_), channel_id=1, source_target_pairs={{0,256},{256,0},{1,257},{257,1},{2,258},{258,2},{3,259},{259,3},{4... | collective-permute-start | bytes 1474568 | tf_op jit(solution)/shard_map/ppermute | solution.py:39
  92.5 11.0 %copy-start.19 = (bf16[2,40,1024]{2,1,0:T(8,128)(2,1)S(1)}, bf16[2,40,1024]{2,1,0:T(8,128)(2,1)}, u32[]{:S(2)}) copy-start(bf16[2,40,1024]{2,1,0:T(8,128)(2,1)} %get-tuple-element.38) | copy-start | bytes 491524
  92.5 13.2 %copy-start.18 = (bf16[2,40,1024]{2,1,0:T(8,128)(2,1)S(1)}, bf16[2,40,1024]{2,1,0:T(8,128)(2,1)}, u32[]{:S(2)}) copy-start(bf16[2,40,1024]{2,1,0:T(8,128)(2,1)} %get-tuple-element.39) | copy-start | bytes 491524
  92.5 29.0 %all-to-all-start.3 = ((bf16[16,32,1024]{2,1,0:T(8,128)(2,1)}), bf16[16,32,1024]{2,1,0:T(8,128)(2,1)S(1)}, u32[]{:S(2)}, u32[]{:S(2)}) async-start(bf16[16,32,1024]{2,1,0:T(8,128)(2,1)} %get-tuple-element.36), calls=%async_computation.3 | async-start | bytes 2097152 | tf_op jit(solution)/shard_map/all_to_all | solution.py:54
  99.9 9.3 %collective-permute-start.8 = (bf16[2,40,1024]{2,1,0:T(8,128)(2,1)S(1)}, bf16[2,40,1024]{2,1,0:T(8,128)(2,1)S(1)}, u32[]{:S(2)}, u32[]{:S(2)}) collective-permute-start(bf16[2,40,1024]{2,1,0:T(8,128)(2,1)S(1)} %copy-done.20), channel_id=1, source_target_pairs={{0,1},{1,0},{2,3},{3,2},{4,5},{5,4},{6,7},{7,6},{8,9},{9,8},{10,11... | collective-permute-start | bytes 491528 | tf_op jit(solution)/shard_map/ppermute | solution.py:31
  103.5 13.8 %collective-permute-start.9 = (bf16[2,40,1024]{2,1,0:T(8,128)(2,1)S(1)}, bf16[2,40,1024]{2,1,0:T(8,128)(2,1)S(1)}, u32[]{:S(2)}, u32[]{:S(2)}) collective-permute-start(bf16[2,40,1024]{2,1,0:T(8,128)(2,1)S(1)} %copy-done.19), channel_id=1, source_target_pairs={{0,2},{1,3},{2,0},{3,1},{4,6},{5,7},{6,4},{7,5},{8,10},{9,11},{10,... | collective-permute-start | bytes 491528 | tf_op jit(solution)/shard_map/ppermute | solution.py:31
  105.8 15.8 %collective-permute-start.10 = (bf16[2,40,1024]{2,1,0:T(8,128)(2,1)S(1)}, bf16[2,40,1024]{2,1,0:T(8,128)(2,1)S(1)}, u32[]{:S(2)}, u32[]{:S(2)}) collective-permute-start(bf16[2,40,1024]{2,1,0:T(8,128)(2,1)S(1)} %copy-done.18), channel_id=1, source_target_pairs={{0,3},{1,2},{2,1},{3,0},{4,7},{5,6},{6,5},{7,4},{8,11},{9,10},{10,... | collective-permute-start | bytes 491528 | tf_op jit(solution)/shard_map/ppermute | solution.py:31
  109.2 12.4 %copy-start.14 = (bf16[2,40,1024]{2,1,0:T(8,128)(2,1)}, bf16[2,40,1024]{2,1,0:T(8,128)(2,1)S(1)}, u32[]{:S(2)}) copy-start(bf16[2,40,1024]{2,1,0:T(8,128)(2,1)S(1)} %collective-permute-done.8.refs_2_.refs_3_) | copy-start | bytes 491524
  123.6 19.9 %all-to-all-start.4 = ((bf16[4,16,512]{2,1,0:T(8,128)(2,1)}), bf16[4,16,512]{2,1,0:T(8,128)(2,1)S(1)}, u32[]{:S(2)}, u32[]{:S(2)}) async-start(bf16[4,16,512]{2,1,0:T(8,128)(2,1)} %plane_sum_kernel.1), calls=%async_computation.4 | async-start | bytes 131072 | tf_op jit(solution)/shard_map/all_to_all | solution.py:54
  (12 other events, 29.7 us)

commit v6 on v5

--- a/solution.py
+++ b/solution.py
@@ -114,13 +114,16 @@
     return copies
 
 
-def project_kernel(side0, side1, qkv, packed):
-    tokens = jnp.concatenate([side0[...].astype(F32), side1[0:72].astype(F32)], axis=0)
-    packed[...] = dot(norm_rows(tokens).astype(BF16), qkv[...]).astype(BF16)
-
-
-def attend_kernel(place, side0, side1, own, got0, got1, qkv, out_w, order, result, merged_in, done):
-    tokens = jnp.concatenate([side0[...].astype(F32), side1[0:72].astype(F32)], axis=0)
+def project_kernel(side0, side1, qkv, tokens, packed, held0, held1, done):
+    for copy in started([(side0, held0, done.at[0]), (side1, held1, done.at[1])]):
+        copy.wait()
+    rows = jnp.concatenate([held0[...].astype(F32), held1[0:72].astype(F32)], axis=0)
+    tokens[...] = rows.astype(BF16)
+    packed[...] = dot(norm_rows(rows).astype(BF16), qkv[...]).astype(BF16)
+
+
+def attend_kernel(place, own_tokens, own, got0, got1, qkv, out_w, order, result, merged_in, done):
+    tokens = own_tokens[...].astype(F32)
     others = jnp.concatenate([got0[...].astype(F32), got1[0:72].astype(F32)], axis=0)
     other_packed = dot(norm_rows(others).astype(BF16), qkv[:, 512:1536]).astype(BF16).astype(F32)
     packed = own[...].astype(F32)
@@ -171,12 +174,11 @@
     return pl.ds(pl.multiple_of((place[0] ^ side) * 1024, 1024), 1024)
 
 
-def merge_near_kernel(place, b0, b1, b2, b3, own_w, near, rows, own, part, blocks, weight, done):
-    copies = started([(block, blocks.at[j], done.at[j]) for j, block in enumerate((b0, b1, b2, b3))])
+def merge_near_kernel(place, own_in, b1, b2, b3, own_w, near, rows, own, part, held, weight, done):
+    (copy,) = started([(own_in, held, done)])
     at = merge_half(place, near, 0, weight)
-    for copy in copies:
-        copy.wait()
-    rows[...] = jnp.concatenate([blocks[j].astype(F32) for j in range(4)], axis=0).astype(BF16)
+    copy.wait()
+    rows[...] = jnp.concatenate([b[...].astype(F32) for b in (held, b1, b2, b3)], axis=0).astype(BF16)
     own[...] = dot(rows[...], own_w[...])
     part[...] = dot(rows[:, at], weight[...])
 
@@ -241,10 +243,8 @@
     )(tokens.transpose(1, 2, 0, 3), cotangent.transpose(1, 2, 0, 3), merge, up, down)
 
 
-def spread_kernel(piece, result, held, done):
-    for copy in started([(piece, held, done.at[0])]):
-        copy.wait()
-    for copy in started([(held, result.at[i], done.at[i]) for i in range(16)]):
+def spread_kernel(piece, result, done):
+    for copy in started([(piece, result.at[i], done.at[i]) for i in range(16)]):
         copy.wait()
 
 
@@ -298,7 +298,7 @@
     copy.wait()
 
 
-def feed_kernel(place, bundle, slope, cots, up, down, near, far, values, grads):
+def feed_kernel(place, bundle, slope, cots, up, down, near, far, farthest, values, grads, leaving, done):
     cots = stacked_rows(cots, slice(0, 1024))
     grad = (dot_nt(cots, down[...]) * slope[:, 0:512]).astype(BF16)
     values[...] = dot(bundle[:, 0:512], down[...])
@@ -319,6 +319,11 @@
     for side, source in enumerate((near, far)):
         at = pl.ds(pl.multiple_of((place[0] ^ side) * 512, 512), 512)
         grads[:, at] = grads[:, at] + dot_nt(grad, up_half(source))
+    at = pl.ds(pl.multiple_of((place[4] ^ 3) * ROWS, 8), ROWS)
+    leaving[0] = values[at, :].astype(BF16)
+    leaving[1] = grads[at, :].astype(BF16)
+    for copy in started([(leaving, farthest, done)]):
+        copy.wait()
 
 
 def sum_of(parts):
@@ -378,7 +383,7 @@
 
 
 def weight_kernel(
-    place, cots, bundle, other, values, grads, s0, s1, s2, s3, result, parts, held, done
+    place, cots, bundle, other, values, grads, s0, s1, s2, result, parts, held, done
 ):
     at = pl.ds(pl.multiple_of(place[0] * 512, 512), 512)
     rows = jnp.concatenate([stacked_rows(cots, at), other[:, 1024:1536]], axis=0)
@@ -388,7 +393,7 @@
         total = dot_tn(rows[:, 256 * z_hi : 256 * z_hi + 256], hidden).astype(BF16)
         held[z_hi] = total.reshape(16, 16, 1024)
         copies += started([(held.at[z_hi], result.at[:, 16 * z_hi : 16 * z_hi + 16, :], done.at[4 + z_hi])])
-    for j, sent in enumerate((s0, s1, s2, s3)):
+    for j, sent in enumerate((s0, s1, s2)):
         at = pl.ds(pl.multiple_of((place[4] ^ j) * ROWS, 8), ROWS)
         parts[j, 0] = values[at, :].astype(BF16)
         parts[j, 1] = grads[at, :].astype(BF16)
@@ -416,30 +421,38 @@
     got0 = swapped(side0, 1)
     got1 = moved(side1, lambda s: (s + 1 if s % 2 else s - 1) % COUNT)
     piece = along_z(piece)
+
     cots = exchanged(cot, "z_near")
-
-    own = call(project_kernel, shaped((144, 1536)), side0, side1, fine_qkv, flops=2 * 10**8)
+    tokens, own = call(
+        project_kernel, (shaped((144, 512)), shaped((144, 1536))), side0, side1, fine_qkv, hbm=range(2),
+        flops=2 * 10**8, after=(cots,),
+        scratch_shapes=[
+            pltpu.VMEM((72, 512), BF16),
+            pltpu.VMEM((96, 512), BF16),
+            pltpu.SemaphoreType.DMA((2,)),
+        ],
+    )
     merged_in = call(
-        attend_kernel, shaped((ROWS, 2048)), place, side0, side1, own, got0, got1, fine_qkv, fine_out,
-        jnp.asarray(merge_order()), scalars=1, hbm_out=1, flops=10**9, after=(cots,),
+        attend_kernel, shaped((ROWS, 2048)), place, tokens, own, got0, got1, fine_qkv, fine_out,
+        jnp.asarray(merge_order()), scalars=1, hbm_out=1, flops=10**9,
         scratch_shapes=[pltpu.VMEM((ROWS, 2048), BF16), pltpu.SemaphoreType.DMA],
     )
     pieces = call(
-        spread_kernel, shaped((16, 80, 512)), piece, hbm=(0,), hbm_out=1, after=(merged_in,),
-        scratch_shapes=[pltpu.VMEM((80, 512), BF16), pltpu.SemaphoreType.DMA((16,))],
+        spread_kernel, shaped((16, 80, 512)), piece, hbm_out=1, after=(merged_in,),
+        scratch_shapes=[pltpu.SemaphoreType.DMA((16,))],
     )
     near = exchanged(pieces, ("y", "x"))
     ins = [merged_in] + [swapped(merged_in, j) for j in (3, 2, 1)][::-1]
-    near = call(copy_kernel, shaped((16, 80, 512)), near, after=ins[1:])
+    near = call(copy_kernel, shaped((16, 80, 512)), near, after=(merged_in,))
     far = across(near)
     narrow = shaped((4 * ROWS, 128), F32)
     rows, own, part = call(
-        merge_near_kernel, (shaped((4 * ROWS, 2048)), narrow, narrow), place, *ins, merge_weight, near,
-        scalars=1, hbm=range(1, 5), flops=2 * 10**8,
+        merge_near_kernel, (shaped((4 * ROWS, 2048)), narrow, narrow),
+        place, *ins, merge_weight, near, scalars=1, hbm=(1,), flops=10**11,
         scratch_shapes=[
-            pltpu.VMEM((4, ROWS, 2048), BF16),
+            pltpu.VMEM((ROWS, 2048), BF16),
             pltpu.VMEM((1024, 128), BF16),
-            pltpu.SemaphoreType.DMA((4,)),
+            pltpu.SemaphoreType.DMA,
         ],
     )
     columns = call(
@@ -460,25 +473,27 @@
         ],
     )
     other = across(bundle)
-    wide = shaped((4 * ROWS, 1024), F32)
-    values, grads = call(
-        feed_kernel, (wide, wide), place, bundle, slope, cots, up_weight, down_weight, near, far, scalars=1,
-        flops=2 * 10**9,
-    )
-    partial = shaped((2, ROWS, 1024))
+    wide, partial = shaped((4 * ROWS, 1024), F32), shaped((2, ROWS, 1024))
+    farthest, values, grads = call(
+        feed_kernel, (partial, wide, wide), place, bundle, slope, cots, up_weight, down_weight, near, far,
+        scalars=1, hbm_out=1, flops=2 * 10**9,
+        scratch_shapes=[pltpu.VMEM((2, ROWS, 1024), BF16), pltpu.SemaphoreType.DMA],
+    )
     *partials, parts = call(
-        weight_kernel, (partial,) * 4 + (shaped((16, 32, 1024)),), place, cots, bundle, other, values, grads,
-        scalars=1, hbm_out=5, flops=3 * 10**8,
+        weight_kernel, (partial,) * 3 + (shaped((16, 32, 1024)),), place, cots, bundle, other, values, grads,
+        scalars=1, hbm_out=4, flops=3 * 10**8,
         scratch_shapes=[
-            pltpu.VMEM((4, 2, ROWS, 1024), BF16),
+            pltpu.VMEM((3, 2, ROWS, 1024), BF16),
             pltpu.VMEM((2, 16, 16, 1024), BF16),
             pltpu.SemaphoreType.DMA((6,)),
         ],
     )
+    partials.append(farthest)
     parts = exchanged(parts, ("y", "x"))
     partials = [partials[0]] + [swapped(partials[j], j) for j in (3, 2, 1)][::-1]
+    over = call(after_kernel, shaped((8, 128), F32), after=partials[3:], flops=10**11)
     parts = call(
-        plane_sum_kernel, shaped((4, 16, 512)), place, parts, scalars=1, after=partials[1:],
+        plane_sum_kernel, shaped((4, 16, 512)), place, parts, scalars=1, after=(over, *partials[1:3]),
         scratch_shapes=[pltpu.VMEM((32, 1024), F32)],
     )
     parts = exchanged(parts, ("z_hi", "z_half"))

time: 145 us -> 141 us (0.972)
  the two profiles are of different devices: /device:TPU:34 before, /device:TPU:1 now
where the time goes in v6:
time: 141 us; the launch traced here: 140 us
  starting transfers between devices  69.8 us (50%)
  waiting for transfers between devices  28.6 us (20%)
  Pallas kernels  23.6 us (17%)
  blocking collectives  15.3 us (11%)
  local copies, waits for them, and re-layouts  2.11 us (1%)
    ppermute x8, starting transfers between devices, moved(): return lax.ppermute(value, LINE, [(s, target(s)) for s in range(COUNT)])  36.2 us
    pallas_call x13, Pallas kernels, call(): pl.pallas_call(body, out_shape=tuple((pltpu.HBM(o.shape, o.dtype) if i <...  21.4 us
    all_to_all x4, starting transfers between devices, exchanged(): return lax.all_to_all(value, axes, 0, 0)  20.5 us
    all_to_all x4, waiting for transfers between devices, exchanged(): return lax.all_to_all(value, axes, 0, 0)  20.2 us
    all_to_all x1, blocking collectives, exchanged(): return lax.all_to_all(value, axes, 0, 0)  15.3 us
    ppermute x2, starting transfers between devices, across(): return lax.ppermute(value, 'lat', [(0, 1), (1, 0)])  11.2 us
    ppermute x8, waiting for transfers between devices, moved(): return lax.ppermute(value, LINE, [(s, target(s)) for s in range(COUNT)])  6.35 us
  transfers between devices with their start and end apart: 15, of which 6 were waited for; matrix products, arithmetic and copies ran while one was open for 0% of the time, Pallas kernels for 10%

profile of v6, /device:TPU:1, one launch (start us, length us, event | category | flops | bytes accessed | tf_op | source)
XLA Modules:
  0.0 140.5 jit_solution(2718931635143993013)
XLA Ops:
  0.6 2.2 %prepare_kernel.1 = (bf16[72,512]{1,0:T(8,128)(2,1)}, bf16[96,512]{1,0:T(8,128)(2,1)}, bf16[80,512]{1,0:T(8,128)(2,1)}, bf16[4,40,1024]{2,1,0:T(8,128)(2,1)}) custom-call(bf16[12,6,2,512]{3,2,1,0:T(2,128)(2,1)} %bitcast.10, bf16[6,3,2,1024]{3,2,1,0:T(2,128)(2,1)} %bitcast.11, bf16[2048,128]{1,0:T(8,128)(2,1)} %refs_5_.4, bf16[1024,512]{1,0:T(8,128)(2,1)} %refs_4_.1, ...), custom_call_target="tpu_custom_call" | custom-call | tf_op jit(solution)/shard_map/prepare_kernel/pallas_call | solution.py:232
  2.9 6.6 %all-to-all-start = ((bf16[4,40,1024]{2,1,0:T(8,128)(2,1)}), bf16[4,40,1024]{2,1,0:T(8,128)(2,1)S(1)}, u32[]{:S(2)}, u32[]{:S(2)}) async-start(bf16[4,40,1024]{2,1,0:T(8,128)(2,1)} %get-tuple-element.27.refs_1_), calls=%async_computation | async-start | bytes 655360 | tf_op jit(solution)/shard_map/all_to_all | solution.py:54
  9.5 15.2 %collective-permute-start.1 = (bf16[96,512]{1,0:T(8,128)(2,1)}, bf16[96,512]{1,0:T(8,128)(2,1)S(1)}, u32[]{:S(2)}, u32[]{:S(2)}) collective-permute-start(bf16[96,512]{1,0:T(8,128)(2,1)} %get-tuple-element.29.refs_1_), channel_id=1, source_target_pairs={{0,255},{1,2},{2,1},{3,4},{4,3},{5,6},{6,5},{7,8},{8,7},{9,10},{10... | collective-permute-start | bytes 294920 | tf_op jit(solution)/shard_map/ppermute | solution.py:31
  30.9 3.6 %attend_kernel.1.refs_1_ = bf16[40,2048]{1,0:T(8,128)(2,1)} custom-call(s32[5]{0:T(128)S(1)} %stack.23.refs_0_, bf16[144,512]{1,0:T(8,128)(2,1)S(1)} %get-tuple-element.30.refs_1_, bf16[144,1536]{1,0:T(8,128)(2,1)S(1)} %get-tuple-element.31.refs_2_, bf16[72,512]{1,0:T(8,128)(2,1)S(1)} %collective-permute-done.refs_3_, ...), custom_call_target="tpu_custom_call" | custom-call | flops 1000000000 | bytes 2951188 | tf_op jit(solution)/shard_map/attend_kernel/pallas_call | solution.py:78
  37.1 4.1 %all-to-all-start.1 = ((bf16[16,80,512]{2,1,0:T(8,128)(2,1)}), bf16[16,80,512]{2,1,0:T(8,128)(2,1)S(1)}, u32[]{:S(2)}, u32[]{:S(2)}) async-start(bf16[16,80,512]{2,1,0:T(8,128)(2,1)} %spread_kernel.1), calls=%async_computation.1 | async-start | bytes 2621440 | tf_op jit(solution)/shard_map/all_to_all | solution.py:54
  41.3 5.4 %collective-permute-start.4 = (bf16[40,2048]{1,0:T(8,128)(2,1)S(1)}, bf16[40,2048]{1,0:T(8,128)(2,1)S(1)}, u32[]{:S(2)}, u32[]{:S(2)}) collective-permute-start(bf16[40,2048]{1,0:T(8,128)(2,1)S(1)} %copy-done.9), channel_id=1, source_target_pairs={{0,3},{1,2},{2,1},{3,0},{4,7},{5,6},{6,5},{7,4},{8,11},{9,10},{10,... | collective-permute-start | bytes 491528 | tf_op jit(solution)/shard_map/ppermute | solution.py:31
  46.7 2.2 %collective-permute-start.3 = (bf16[40,2048]{1,0:T(8,128)(2,1)S(1)}, bf16[40,2048]{1,0:T(8,128)(2,1)S(1)}, u32[]{:S(2)}, u32[]{:S(2)}) collective-permute-start(bf16[40,2048]{1,0:T(8,128)(2,1)S(1)} %copy-done.9), channel_id=1, source_target_pairs={{0,2},{1,3},{2,0},{3,1},{4,6},{5,7},{6,4},{7,5},{8,10},{9,11},{10,... | collective-permute-start | bytes 491528 | tf_op jit(solution)/shard_map/ppermute | solution.py:31
  48.9 2.2 %collective-permute-start.2 = (bf16[40,2048]{1,0:T(8,128)(2,1)S(1)}, bf16[40,2048]{1,0:T(8,128)(2,1)S(1)}, u32[]{:S(2)}, u32[]{:S(2)}) collective-permute-start(bf16[40,2048]{1,0:T(8,128)(2,1)S(1)} %copy-done.9), channel_id=1, source_target_pairs={{0,1},{1,0},{2,3},{3,2},{4,5},{5,4},{6,7},{7,6},{8,9},{9,8},{10,11... | collective-permute-start | bytes 491528 | tf_op jit(solution)/shard_map/ppermute | solution.py:31
  51.1 6.6 %all-to-all-done.1.refs_0_ = bf16[16,80,512]{2,1,0:T(8,128)(2,1)S(1)} async-done(((bf16[16,80,512]{2,1,0:T(8,128)(2,1)}), bf16[16,80,512]{2,1,0:T(8,128)(2,1)S(1)}, u32[]{:S(2)}, u32[]{:S(2)}) %all-to-all-start.1) | async-done | bytes 1310752 | tf_op jit(solution)/shard_map/all_to_all | solution.py:54
  57.9 7.1 %collective-permute-start.6 = (bf16[16,80,512]{2,1,0:T(8,128)(2,1)S(1)}, bf16[16,80,512]{2,1,0:T(8,128)(2,1)S(1)}, u32[]{:S(2)}, u32[]{:S(2)}) collective-permute-start(bf16[16,80,512]{2,1,0:T(8,128)(2,1)S(1)} %copy_kernel.1.refs_6_.refs_4_), channel_id=1, source_target_pairs={{0,256},{256,0},{1,257},{257,1},{2,258},{258,2},{3,259},{259,3},{4... | collective-permute-start | bytes 3932168 | tf_op jit(solution)/shard_map/ppermute | solution.py:39
  68.5 15.3 %all_to_all.25.refs_2_ = bf16[4,4,40,256]{3,2,1,0:T(8,128)(2,1)S(1)} all-to-all(bf16[4,4,40,256]{3,2,1,0:T(8,128)(2,1)S(1)} %merge_kernel.1), channel_id=1, replica_groups=mesh['lat'=2,'z_hi'=2,'y'=4,'x'=4,'z_half'=2,'z_near'=4] {'z_near'}, dimensions={0} | all-to-all | bytes 655360 | tf_op jit(solution)/shard_map/all_to_all | solution.py:54
  83.8 2.6 %hidden_kernel.1 = (bf16[40,1024]{1,0:T(8,128)(2,1)}, bf16[160,1536]{1,0:T(8,128)(2,1)S(1)}, f32[160,1024]{1,0:T(8,128)S(1)}) custom-call(s32[5]{0:T(128)S(1)} %stack.23.refs_0_, bf16[1024,512]{1,0:T(8,128)(2,1)} %refs_4_.1, bf16[4,4,40,256]{3,2,1,0:T(8,128)(2,1)S(1)} %all_to_all.25.refs_2_, bf16[4,40,1024]{2,1,0:T(8,128)(2,1)S(1)} %copy-done.1, ...), custom_call_target="tpu_custom_call" | custom-call | flops 1000000000 | bytes 4325396 | tf_op jit(solution)/shard_map/hidden_kernel/pallas_call | solution.py:78
  86.4 4.1 %collective-permute-start.7 = (bf16[160,1536]{1,0:T(8,128)(2,1)S(1)}, bf16[160,1536]{1,0:T(8,128)(2,1)S(1)}, u32[]{:S(2)}, u32[]{:S(2)}) collective-permute-start(bf16[160,1536]{1,0:T(8,128)(2,1)S(1)} %get-tuple-element.36.refs_1_.refs_2_), channel_id=1, source_target_pairs={{0,256},{256,0},{1,257},{257,1},{2,258},{258,2},{3,259},{259,3},{4... | collective-permute-start | bytes 1474568 | tf_op jit(solution)/shard_map/ppermute | solution.py:39
  90.6 3.1 %feed_kernel.1 = (bf16[2,40,1024]{2,1,0:T(8,128)(2,1)}, f32[160,1024]{1,0:T(8,128)S(1)}, f32[160,1024]{1,0:T(8,128)S(1)}) custom-call(s32[5]{0:T(128)S(1)} %stack.23.refs_0_, bf16[160,1536]{1,0:T(8,128)(2,1)S(1)} %get-tuple-element.36.refs_1_.refs_2_, f32[160,1024]{1,0:T(8,128)S(1)} %get-tuple-element.37.refs_2_, bf16[4,40,1024]{2,1,0:T(8,128)(2,1)S(1)} %copy-done.1, ...), custom_call_target="tpu_custom_call" | custom-call | flops 2000000000 | bytes 6193172 | tf_op jit(solution)/shard_map/feed_kernel/pallas_call | solution.py:78
  93.7 3.1 %collective-permute-start.8 = (bf16[2,40,1024]{2,1,0:T(8,128)(2,1)}, bf16[2,40,1024]{2,1,0:T(8,128)(2,1)S(1)}, u32[]{:S(2)}, u32[]{:S(2)}) collective-permute-start(bf16[2,40,1024]{2,1,0:T(8,128)(2,1)} %get-tuple-element.41), channel_id=1, source_target_pairs={{0,3},{1,2},{2,1},{3,0},{4,7},{5,6},{6,5},{7,4},{8,11},{9,10},{10,... | collective-permute-start | bytes 491528 | tf_op jit(solution)/shard_map/ppermute | solution.py:31
  96.8 2.3 %weight_kernel.1 = (bf16[2,40,1024]{2,1,0:T(8,128)(2,1)}, bf16[2,40,1024]{2,1,0:T(8,128)(2,1)}, bf16[2,40,1024]{2,1,0:T(8,128)(2,1)}, bf16[16,32,1024]{2,1,0:T(8,128)(2,1)}) custom-call(s32[5]{0:T(128)S(1)} %stack.23.refs_0_, bf16[4,40,1024]{2,1,0:T(8,128)(2,1)S(1)} %copy-done.1, bf16[160,1536]{1,0:T(8,128)(2,1)S(1)} %get-tuple-element.36.refs_1_.refs_2_, ...), custom_call_target="tpu_custom_call" | custom-call | flops 300000000 | bytes 2621460 | tf_op jit(solution)/shard_map/weight_kernel/pallas_call | solution.py:78
  99.1 3.8 %all-to-all-start.3 = ((bf16[16,32,1024]{2,1,0:T(8,128)(2,1)}), bf16[16,32,1024]{2,1,0:T(8,128)(2,1)S(1)}, u32[]{:S(2)}, u32[]{:S(2)}) async-start(bf16[16,32,1024]{2,1,0:T(8,128)(2,1)} %get-tuple-element.40), calls=%async_computation.3 | async-start | bytes 2097152 | tf_op jit(solution)/shard_map/all_to_all | solution.py:54
  102.9 1.9 %collective-permute-start.9 = (bf16[2,40,1024]{2,1,0:T(8,128)(2,1)S(1)}, bf16[2,40,1024]{2,1,0:T(8,128)(2,1)S(1)}, u32[]{:S(2)}, u32[]{:S(2)}) collective-permute-start(bf16[2,40,1024]{2,1,0:T(8,128)(2,1)S(1)} %copy-done.14), channel_id=1, source_target_pairs={{0,1},{1,0},{2,3},{3,2},{4,5},{5,4},{6,7},{7,6},{8,9},{9,8},{10,11... | collective-permute-start | bytes 491528 | tf_op jit(solution)/shard_map/ppermute | solution.py:31
  104.9 4.3 %collective-permute-start.10 = (bf16[2,40,1024]{2,1,0:T(8,128)(2,1)S(1)}, bf16[2,40,1024]{2,1,0:T(8,128)(2,1)S(1)}, u32[]{:S(2)}, u32[]{:S(2)}) collective-permute-start(bf16[2,40,1024]{2,1,0:T(8,128)(2,1)S(1)} %copy-done.13), channel_id=1, source_target_pairs={{0,2},{1,3},{2,0},{3,1},{4,6},{5,7},{6,4},{7,5},{8,10},{9,11},{10,... | collective-permute-start | bytes 491528 | tf_op jit(solution)/shard_map/ppermute | solution.py:31
  110.4 6.3 %collective-permute-done.10.refs_4_ = bf16[2,40,1024]{2,1,0:T(8,128)(2,1)S(1)} collective-permute-done((bf16[2,40,1024]{2,1,0:T(8,128)(2,1)S(1)}, bf16[2,40,1024]{2,1,0:T(8,128)(2,1)S(1)}, u32[]{:S(2)}, u32[]{:S(2)}) %collective-permute-start.10) | collective-permute-done | bytes 163872 | tf_op jit(solution)/shard_map/ppermute | solution.py:31
  116.7 3.7 %all-to-all-done.3.refs_1_ = bf16[16,32,1024]{2,1,0:T(8,128)(2,1)S(1)} async-done(((bf16[16,32,1024]{2,1,0:T(8,128)(2,1)}), bf16[16,32,1024]{2,1,0:T(8,128)(2,1)S(1)}, u32[]{:S(2)}, u32[]{:S(2)}) %all-to-all-start.3) | async-done | bytes 1048608 | tf_op jit(solution)/shard_map/all_to_all | solution.py:54
  121.8 6.0 %all-to-all-start.4 = ((bf16[4,16,512]{2,1,0:T(8,128)(2,1)}), bf16[4,16,512]{2,1,0:T(8,128)(2,1)S(1)}, u32[]{:S(2)}, u32[]{:S(2)}) async-start(bf16[4,16,512]{2,1,0:T(8,128)(2,1)} %plane_sum_kernel.1), calls=%async_computation.4 | async-start | bytes 131072 | tf_op jit(solution)/shard_map/all_to_all | solution.py:54
  127.8 2.2 %finish_kernel.1 = (bf16[6,3,2,1024]{3,2,1,0:T(2,128)(2,1)}, bf16[6,3,2,1024]{3,2,1,0:T(2,128)(2,1)}) custom-call(bf16[40,1024]{1,0:T(8,128)(2,1)} %get-tuple-element.44.refs_0_, bf16[4,40,1024]{2,1,0:T(8,128)(2,1)} %get-tuple-element.27.refs_1_, bf16[2,40,1024]{2,1,0:T(8,128)(2,1)} %get-tuple-element.45.refs_2_, bf16[2,40,1024]{2,1,0:T(8,128)(2,1)} %copy-done.10, ...), custom_call_target="tpu_custom_call" | custom-call | bytes 1064960 | tf_op jit(solution)/shard_map/finish_kernel/pallas_call | solution.py:78
  130.1 9.8 %all-to-all-done.4.refs_0_ = bf16[4,16,512]{2,1,0:T(8,128)(2,1)S(1)} async-done(((bf16[4,16,512]{2,1,0:T(8,128)(2,1)}), bf16[4,16,512]{2,1,0:T(8,128)(2,1)S(1)}, u32[]{:S(2)}, u32[]{:S(2)}) %all-to-all-start.4) | async-done | bytes 65568 | tf_op jit(solution)/shard_map/all_to_all | solution.py:54
  (52 shorter events, 15.6 us)
Async XLA Ops:
  0.6 28.7 %copy-start.3 = (bf16[512,1536]{1,0:T(8,128)(2,1)S(1)}, bf16[512,1536]{1,0:T(8,128)(2,1)}, u32[]{:S(2)}) copy-start(bf16[512,1536]{1,0:T(8,128)(2,1)} %refs_5_.3) | copy-start | bytes 4718596
  2.8 28.0 %copy-start.7 = (bf16[512,512]{1,0:T(8,128)(2,1)S(1)}, bf16[512,512]{1,0:T(8,128)(2,1)}, u32[]{:S(2)}) copy-start(bf16[512,512]{1,0:T(8,128)(2,1)} %refs_6_.1) | copy-start | bytes 1572868
  2.9 28.0 %copy-start.8 = (bf16[2,160,144]{2,1,0:T(8,128)(2,1)S(1)}, bf16[2,160,144]{2,1,0:T(8,128)(2,1)}, u32[]{:S(2)}) copy-start(bf16[2,160,144]{2,1,0:T(8,128)(2,1)} %constant.22.clone.refs_7_) | copy-start | bytes 276484
  2.9 25.7 %all-to-all-start = ((bf16[4,40,1024]{2,1,0:T(8,128)(2,1)}), bf16[4,40,1024]{2,1,0:T(8,128)(2,1)S(1)}, u32[]{:S(2)}, u32[]{:S(2)}) async-start(bf16[4,40,1024]{2,1,0:T(8,128)(2,1)} %get-tuple-element.27.refs_1_), calls=%async_computation | async-start | bytes 655360 | tf_op jit(solution)/shard_map/all_to_all | solution.py:54
  9.5 21.4 %collective-permute-start.1 = (bf16[96,512]{1,0:T(8,128)(2,1)}, bf16[96,512]{1,0:T(8,128)(2,1)S(1)}, u32[]{:S(2)}, u32[]{:S(2)}) collective-permute-start(bf16[96,512]{1,0:T(8,128)(2,1)} %get-tuple-element.29.refs_1_), channel_id=1, source_target_pairs={{0,255},{1,2},{2,1},{3,4},{4,3},{5,6},{6,5},{7,8},{8,7},{9,10},{10... | collective-permute-start | bytes 294920 | tf_op jit(solution)/shard_map/ppermute | solution.py:31
  24.7 6.2 %collective-permute-start = (bf16[72,512]{1,0:T(8,128)(2,1)}, bf16[72,512]{1,0:T(8,128)(2,1)S(1)}, u32[]{:S(2)}, u32[]{:S(2)}) collective-permute-start(bf16[72,512]{1,0:T(8,128)(2,1)} %get-tuple-element.28.refs_0_), channel_id=1, source_target_pairs={{0,1},{1,0},{2,3},{3,2},{4,5},{5,4},{6,7},{7,6},{8,9},{9,8},{10,11... | collective-permute-start | bytes 221192 | tf_op jit(solution)/shard_map/ppermute | solution.py:31
  26.6 9.3 %collective-permute-start.5 = (bf16[80,512]{1,0:T(8,128)(2,1)}, bf16[80,512]{1,0:T(8,128)(2,1)S(1)}, u32[]{:S(2)}, u32[]{:S(2)}) collective-permute-start(bf16[80,512]{1,0:T(8,128)(2,1)} %get-tuple-element.32), channel_id=1, source_target_pairs={{0,4},{1,5},{2,6},{3,7},{4,128},{5,129},{6,130},{7,131},{8,12},{9,... | collective-permute-start | bytes 245768 | tf_op jit(solution)/shard_map/ppermute | solution.py:50
  37.1 20.6 %all-to-all-start.1 = ((bf16[16,80,512]{2,1,0:T(8,128)(2,1)}), bf16[16,80,512]{2,1,0:T(8,128)(2,1)S(1)}, u32[]{:S(2)}, u32[]{:S(2)}) async-start(bf16[16,80,512]{2,1,0:T(8,128)(2,1)} %spread_kernel.1), calls=%async_computation.1 | async-start | bytes 2621440 | tf_op jit(solution)/shard_map/all_to_all | solution.py:54
  41.3 23.7 %copy-start.5 = (bf16[2048,128]{1,0:T(8,128)(2,1)S(1)}, bf16[2048,128]{1,0:T(8,128)(2,1)}, u32[]{:S(2)}) copy-start(bf16[2048,128]{1,0:T(8,128)(2,1)} %refs_5_.4) | copy-start | bytes 1572868
  41.3 23.7 %collective-permute-start.4 = (bf16[40,2048]{1,0:T(8,128)(2,1)S(1)}, bf16[40,2048]{1,0:T(8,128)(2,1)S(1)}, u32[]{:S(2)}, u32[]{:S(2)}) collective-permute-start(bf16[40,2048]{1,0:T(8,128)(2,1)S(1)} %copy-done.9), channel_id=1, source_target_pairs={{0,3},{1,2},{2,1},{3,0},{4,7},{5,6},{6,5},{7,4},{8,11},{9,10},{10,... | collective-permute-start | bytes 491528 | tf_op jit(solution)/shard_map/ppermute | solution.py:31
  46.7 18.3 %collective-permute-start.3 = (bf16[40,2048]{1,0:T(8,128)(2,1)S(1)}, bf16[40,2048]{1,0:T(8,128)(2,1)S(1)}, u32[]{:S(2)}, u32[]{:S(2)}) collective-permute-start(bf16[40,2048]{1,0:T(8,128)(2,1)S(1)} %copy-done.9), channel_id=1, source_target_pairs={{0,2},{1,3},{2,0},{3,1},{4,6},{5,7},{6,4},{7,5},{8,10},{9,11},{10,... | collective-permute-start | bytes 491528 | tf_op jit(solution)/shard_map/ppermute | solution.py:31
  48.9 16.1 %collective-permute-start.2 = (bf16[40,2048]{1,0:T(8,128)(2,1)S(1)}, bf16[40,2048]{1,0:T(8,128)(2,1)S(1)}, u32[]{:S(2)}, u32[]{:S(2)}) collective-permute-start(bf16[40,2048]{1,0:T(8,128)(2,1)S(1)} %copy-done.9), channel_id=1, source_target_pairs={{0,1},{1,0},{2,3},{3,2},{4,5},{5,4},{6,7},{7,6},{8,9},{9,8},{10,11... | collective-permute-start | bytes 491528 | tf_op jit(solution)/shard_map/ppermute | solution.py:31
  57.9 9.8 %collective-permute-start.6 = (bf16[16,80,512]{2,1,0:T(8,128)(2,1)S(1)}, bf16[16,80,512]{2,1,0:T(8,128)(2,1)S(1)}, u32[]{:S(2)}, u32[]{:S(2)}) collective-permute-start(bf16[16,80,512]{2,1,0:T(8,128)(2,1)S(1)} %copy_kernel.1.refs_6_.refs_4_), channel_id=1, source_target_pairs={{0,256},{256,0},{1,257},{257,1},{2,258},{258,2},{3,259},{259,3},{4... | collective-permute-start | bytes 3932168 | tf_op jit(solution)/shard_map/ppermute | solution.py:39
  67.6 16.1 %copy-start.1 = (bf16[4,40,1024]{2,1,0:T(8,128)(2,1)S(1)}, bf16[4,40,1024]{2,1,0:T(8,128)(2,1)}, u32[]{:S(2)}) copy-start(bf16[4,40,1024]{2,1,0:T(8,128)(2,1)} %copy-done) | copy-start | bytes 983044
  83.8 6.8 %copy-start.2 = (bf16[1024,512]{1,0:T(8,128)(2,1)S(1)}, bf16[1024,512]{1,0:T(8,128)(2,1)}, u32[]{:S(2)}) copy-start(bf16[1024,512]{1,0:T(8,128)(2,1)} %refs_4_.1) | copy-start | bytes 3145732
  83.8 6.8 %copy-start.4 = (bf16[512,1024]{1,0:T(8,128)(2,1)S(1)}, bf16[512,1024]{1,0:T(8,128)(2,1)}, u32[]{:S(2)}) copy-start(bf16[512,1024]{1,0:T(8,128)(2,1)} %refs_5_.5) | copy-start | bytes 3145732
  86.4 10.4 %collective-permute-start.7 = (bf16[160,1536]{1,0:T(8,128)(2,1)S(1)}, bf16[160,1536]{1,0:T(8,128)(2,1)S(1)}, u32[]{:S(2)}, u32[]{:S(2)}) collective-permute-start(bf16[160,1536]{1,0:T(8,128)(2,1)S(1)} %get-tuple-element.36.refs_1_.refs_2_), channel_id=1, source_target_pairs={{0,256},{256,0},{1,257},{257,1},{2,258},{258,2},{3,259},{259,3},{4... | collective-permute-start | bytes 1474568 | tf_op jit(solution)/shard_map/ppermute | solution.py:39
  93.7 15.5 %collective-permute-start.8 = (bf16[2,40,1024]{2,1,0:T(8,128)(2,1)}, bf16[2,40,1024]{2,1,0:T(8,128)(2,1)S(1)}, u32[]{:S(2)}, u32[]{:S(2)}) collective-permute-start(bf16[2,40,1024]{2,1,0:T(8,128)(2,1)} %get-tuple-element.41), channel_id=1, source_target_pairs={{0,3},{1,2},{2,1},{3,0},{4,7},{5,6},{6,5},{7,4},{8,11},{9,10},{10,... | collective-permute-start | bytes 491528 | tf_op jit(solution)/shard_map/ppermute | solution.py:31
  99.1 5.8 %copy-start.13 = (bf16[2,40,1024]{2,1,0:T(8,128)(2,1)S(1)}, bf16[2,40,1024]{2,1,0:T(8,128)(2,1)}, u32[]{:S(2)}) copy-start(bf16[2,40,1024]{2,1,0:T(8,128)(2,1)} %get-tuple-element.43) | copy-start | bytes 491524
  99.1 21.4 %all-to-all-start.3 = ((bf16[16,32,1024]{2,1,0:T(8,128)(2,1)}), bf16[16,32,1024]{2,1,0:T(8,128)(2,1)S(1)}, u32[]{:S(2)}, u32[]{:S(2)}) async-start(bf16[16,32,1024]{2,1,0:T(8,128)(2,1)} %get-tuple-element.40), calls=%async_computation.3 | async-start | bytes 2097152 | tf_op jit(solution)/shard_map/all_to_all | solution.py:54
  102.9 7.5 %collective-permute-start.9 = (bf16[2,40,1024]{2,1,0:T(8,128)(2,1)S(1)}, bf16[2,40,1024]{2,1,0:T(8,128)(2,1)S(1)}, u32[]{:S(2)}, u32[]{:S(2)}) collective-permute-start(bf16[2,40,1024]{2,1,0:T(8,128)(2,1)S(1)} %copy-done.14), channel_id=1, source_target_pairs={{0,1},{1,0},{2,3},{3,2},{4,5},{5,4},{6,7},{7,6},{8,9},{9,8},{10,11... | collective-permute-start | bytes 491528 | tf_op jit(solution)/shard_map/ppermute | solution.py:31
  104.9 11.9 %collective-permute-start.10 = (bf16[2,40,1024]{2,1,0:T(8,128)(2,1)S(1)}, bf16[2,40,1024]{2,1,0:T(8,128)(2,1)S(1)}, u32[]{:S(2)}, u32[]{:S(2)}) collective-permute-start(bf16[2,40,1024]{2,1,0:T(8,128)(2,1)S(1)} %copy-done.13), channel_id=1, source_target_pairs={{0,2},{1,3},{2,0},{3,1},{4,6},{5,7},{6,4},{7,5},{8,10},{9,11},{10,... | collective-permute-start | bytes 491528 | tf_op jit(solution)/shard_map/ppermute | solution.py:31
  110.4 10.1 %copy-start.10 = (bf16[2,40,1024]{2,1,0:T(8,128)(2,1)}, bf16[2,40,1024]{2,1,0:T(8,128)(2,1)S(1)}, u32[]{:S(2)}) copy-start(bf16[2,40,1024]{2,1,0:T(8,128)(2,1)S(1)} %collective-permute-done.9.refs_3_) | copy-start | bytes 491524
  121.8 18.0 %all-to-all-start.4 = ((bf16[4,16,512]{2,1,0:T(8,128)(2,1)}), bf16[4,16,512]{2,1,0:T(8,128)(2,1)S(1)}, u32[]{:S(2)}, u32[]{:S(2)}) async-start(bf16[4,16,512]{2,1,0:T(8,128)(2,1)} %plane_sum_kernel.1), calls=%async_computation.4 | async-start | bytes 131072 | tf_op jit(solution)/shard_map/all_to_all | solution.py:54
  (6 other events, 13.7 us)

commit v7 on v6

--- a/solution.py
+++ b/solution.py
@@ -271,7 +271,7 @@
 
 
 def hidden_kernel(
-    place, up_hbm, columns, cots, near, far, own_merged, bundle, slope, merged, own, normed, up, done
+    place, up_hbm, columns, cots, near, far, own_merged, slope, bundle, merged, own, normed, up, done
 ):
     (fetch,) = started([(up_hbm, up, done.at[1])])
     lat, half_index, near_index = place[0], place[3], place[4]
@@ -298,31 +298,44 @@
     copy.wait()
 
 
-def feed_kernel(place, bundle, slope, cots, up, down, near, far, farthest, values, grads, leaving, done):
+def feed_kernel(
+    place, up_hbm, down_hbm, slope_hbm, bundle, cots, near, far, s0, s1, s2, s3,
+    values, grads, parts, up, down, slope, done,
+):
+    copies = started([(slope_hbm, slope, done.at[0]), (down_hbm, down, done.at[1]), (up_hbm, up, done.at[2])])
     cots = stacked_rows(cots, slice(0, 1024))
-    grad = (dot_nt(cots, down[...]) * slope[:, 0:512]).astype(BF16)
-    values[...] = dot(bundle[:, 0:512], down[...])
-    grads[...] = dot_nt(grad, up[...])
-    far_grads = []
+    far_values, far_hidden, far_grads = [0.0, 0.0], [], []
     for side, source in enumerate((near, far)):
         at = pl.ds(pl.multiple_of(512 + (place[0] ^ side) * 256, 256), 256)
+        units = bundle[:, at]
         grad = 0.0
         for half in range(2):
-            columns = slice(512 * half, 512 * half + 512)
             part = down_half(source, half)
-            values[:, columns] = values[:, columns] + dot(bundle[:, at], part)
-            grad = grad + dot_nt(cots[:, columns], part)
+            far_values[half] = far_values[half] + dot(units, part)
+            grad = grad + dot_nt(cots[:, 512 * half : 512 * half + 512], part)
+        far_hidden.append(grad)
+    copies[0].wait()
+    for side, grad in enumerate(far_hidden):
+        at = pl.ds(pl.multiple_of(512 + (place[0] ^ side) * 256, 256), 256)
         far_grads.append((grad * slope[:, at]).astype(BF16))
+    copies[1].wait()
+    own_grad = (dot_nt(cots, down[...]) * slope[:, 0:512]).astype(BF16)
+    values[...] = dot(bundle[:, 0:512], down[...]) + jnp.concatenate(far_values, axis=1)
+    copies[2].wait()
+    grads[...] = dot_nt(own_grad, up[...])
     first = jnp.where(place[0] == 0, far_grads[0].astype(F32), far_grads[1].astype(F32)).astype(BF16)
     second = jnp.where(place[0] == 0, far_grads[1].astype(F32), far_grads[0].astype(F32)).astype(BF16)
     grad = jnp.concatenate([first, second], axis=1)
     for side, source in enumerate((near, far)):
         at = pl.ds(pl.multiple_of((place[0] ^ side) * 512, 512), 512)
         grads[:, at] = grads[:, at] + dot_nt(grad, up_half(source))
-    at = pl.ds(pl.multiple_of((place[4] ^ 3) * ROWS, 8), ROWS)
-    leaving[0] = values[at, :].astype(BF16)
-    leaving[1] = grads[at, :].astype(BF16)
-    for copy in started([(leaving, farthest, done)]):
+    copies = []
+    for j, sent in reversed(list(enumerate((s0, s1, s2, s3)))):
+        at = pl.ds(pl.multiple_of((place[4] ^ j) * ROWS, 8), ROWS)
+        parts[j, 0] = values[at, :].astype(BF16)
+        parts[j, 1] = grads[at, :].astype(BF16)
+        copies += started([(parts.at[j], sent, done.at[3 + j])])
+    for copy in copies:
         copy.wait()
 
 
@@ -370,7 +383,7 @@
 def finish(*args):
     tokens = shaped((6, 3, 2, 1024))
     return call(
-        finish_kernel, (tokens, tokens), *args, hbm=range(6), hbm_out=2,
+        finish_kernel, (tokens, tokens), *args, hbm=range(6), hbm_out=2, flops=10**11,
         scratch_shapes=[
             pltpu.VMEM((ROWS, 1024), BF16),
             pltpu.VMEM((ROWS, 1024), BF16),
@@ -382,22 +395,15 @@
     )
 
 
-def weight_kernel(
-    place, cots, bundle, other, values, grads, s0, s1, s2, result, parts, held, done
-):
+def weight_kernel(place, cots, bundle, other, slope, result, slope_hbm, held, done):
+    copies = started([(slope, slope_hbm, done.at[2])])
     at = pl.ds(pl.multiple_of(place[0] * 512, 512), 512)
     rows = jnp.concatenate([stacked_rows(cots, at), other[:, 1024:1536]], axis=0)
     hidden = jnp.concatenate([bundle[:, 0:1024], other[:, 0:1024]], axis=0)
-    copies = []
     for z_hi in range(2):
         total = dot_tn(rows[:, 256 * z_hi : 256 * z_hi + 256], hidden).astype(BF16)
         held[z_hi] = total.reshape(16, 16, 1024)
-        copies += started([(held.at[z_hi], result.at[:, 16 * z_hi : 16 * z_hi + 16, :], done.at[4 + z_hi])])
-    for j, sent in enumerate((s0, s1, s2)):
-        at = pl.ds(pl.multiple_of((place[4] ^ j) * ROWS, 8), ROWS)
-        parts[j, 0] = values[at, :].astype(BF16)
-        parts[j, 1] = grads[at, :].astype(BF16)
-        copies += started([(parts.at[j], sent, done.at[j])])
+        copies += started([(held.at[z_hi], result.at[:, 16 * z_hi : 16 * z_hi + 16, :], done.at[z_hi])])
     for copy in copies:
         copy.wait()
 
@@ -460,9 +466,9 @@
         scratch_shapes=[pltpu.VMEM((1024, 128), BF16)],
     )
     columns = exchanged(columns, "z_near")
-    own_merged, bundle, slope = call(
+    own_merged, slope, bundle = call(
         hidden_kernel,
-        (shaped((ROWS, 1024)), shaped((4 * ROWS, 1536)), shaped((4 * ROWS, 1024), F32)),
+        (shaped((ROWS, 1024)), shaped((4 * ROWS, 1024), F32), shaped((4 * ROWS, 1536))),
         place, up_weight, columns, cots, near, far, scalars=1, hbm=(1,), hbm_out=1, flops=10**9,
         scratch_shapes=[
             pltpu.VMEM((4 * ROWS, 1024), F32),
@@ -473,27 +479,29 @@
         ],
     )
     other = across(bundle)
-    wide, partial = shaped((4 * ROWS, 1024), F32), shaped((2, ROWS, 1024))
-    farthest, values, grads = call(
-        feed_kernel, (partial, wide, wide), place, bundle, slope, cots, up_weight, down_weight, near, far,
-        scalars=1, hbm_out=1, flops=2 * 10**9,
-        scratch_shapes=[pltpu.VMEM((2, ROWS, 1024), BF16), pltpu.SemaphoreType.DMA],
-    )
-    *partials, parts = call(
-        weight_kernel, (partial,) * 3 + (shaped((16, 32, 1024)),), place, cots, bundle, other, values, grads,
-        scalars=1, hbm_out=4, flops=3 * 10**8,
+    parts, slope = call(
+        weight_kernel, (shaped((16, 32, 1024)), shaped((4 * ROWS, 1024), F32)), place, cots, bundle, other, slope,
+        scalars=1, hbm_out=2, flops=3 * 10**8,
+        scratch_shapes=[pltpu.VMEM((2, 16, 16, 1024), BF16), pltpu.SemaphoreType.DMA((3,))],
+    )
+    parts = exchanged(parts, ("y", "x"))
+    partial = shaped((2, ROWS, 1024))
+    partials = call(
+        feed_kernel, (partial,) * 4, place, up_weight, down_weight, slope, bundle, cots, near, far, scalars=1,
+        hbm=range(1, 4), hbm_out=4, flops=2 * 10**9,
         scratch_shapes=[
-            pltpu.VMEM((3, 2, ROWS, 1024), BF16),
-            pltpu.VMEM((2, 16, 16, 1024), BF16),
-            pltpu.SemaphoreType.DMA((6,)),
+            pltpu.VMEM((4 * ROWS, 1024), F32),
+            pltpu.VMEM((4 * ROWS, 1024), F32),
+            pltpu.VMEM((4, 2, ROWS, 1024), BF16),
+            pltpu.VMEM((1024, 512), BF16),
+            pltpu.VMEM((512, 1024), BF16),
+            pltpu.VMEM((4 * ROWS, 1024), F32),
+            pltpu.SemaphoreType.DMA((7,)),
         ],
     )
-    partials.append(farthest)
-    parts = exchanged(parts, ("y", "x"))
     partials = [partials[0]] + [swapped(partials[j], j) for j in (3, 2, 1)][::-1]
-    over = call(after_kernel, shaped((8, 128), F32), after=partials[3:], flops=10**11)
     parts = call(
-        plane_sum_kernel, shaped((4, 16, 512)), place, parts, scalars=1, after=(over, *partials[1:3]),
+        plane_sum_kernel, shaped((4, 16, 512)), place, parts, scalars=1,
         scratch_shapes=[pltpu.VMEM((32, 1024), F32)],
     )
     parts = exchanged(parts, ("z_hi", "z_half"))

time: 141 us -> 137 us (0.972)
  waiting for transfers between devices: 28.6 us -> 21.3 us
  Pallas kernels: 23.6 us -> 26.2 us
    ppermute x8, waiting for transfers between devices: 6.35 us -> 0.02 us  [moved(): return lax.ppermute(value, LINE, [(s, target(s)) for s in range(COUNT)])]
    pallas_call x13 -> x12, Pallas kernels: 21.4 us -> 24 us  [call(): pl.pallas_call(body, out_shape=tuple((pltpu.HBM(o.shape, o.dtype) if i <...]
    all_to_all x4, waiting for transfers between devices: 20.2 us -> 18.1 us  [exchanged(): return lax.all_to_all(value, axes, 0, 0)]
  transfers between devices with their start and end apart: 15 -> 15, of which waited for: 6 -> 6; matrix products, arithmetic and copies ran while one was open for 0% -> 0% of each run, Pallas kernels for 10% -> 12%
where the time goes in v7:
time: 137 us; the launch traced here: 136 us
  starting transfers between devices  70.3 us (51%)
  Pallas kernels  26.2 us (19%)
  waiting for transfers between devices  21.3 us (16%)
  blocking collectives  15.3 us (11%)
  local copies, waits for them, and re-layouts  1.58 us (1%)
    ppermute x8, starting transfers between devices, moved(): return lax.ppermute(value, LINE, [(s, target(s)) for s in range(COUNT)])  36.2 us
    pallas_call x12, Pallas kernels, call(): pl.pallas_call(body, out_shape=tuple((pltpu.HBM(o.shape, o.dtype) if i <...  24 us
    all_to_all x4, starting transfers between devices, exchanged(): return lax.all_to_all(value, axes, 0, 0)  20.9 us
    all_to_all x4, waiting for transfers between devices, exchanged(): return lax.all_to_all(value, axes, 0, 0)  18.1 us
    all_to_all x1, blocking collectives, exchanged(): return lax.all_to_all(value, axes, 0, 0)  15.3 us
    ppermute x2, starting transfers between devices, across(): return lax.ppermute(value, 'lat', [(0, 1), (1, 0)])  11.3 us
  transfers between devices with their start and end apart: 15, of which 6 were waited for; matrix products, arithmetic and copies ran while one was open for 0% of the time, Pallas kernels for 12%

profile of v7, /device:TPU:1, one launch (start us, length us, event | category | flops | bytes accessed | tf_op | source)
XLA Modules:
  0.0 135.6 jit_solution(12192494239544339389)
XLA Ops:
  0.6 2.2 %prepare_kernel.1 = (bf16[72,512]{1,0:T(8,128)(2,1)}, bf16[96,512]{1,0:T(8,128)(2,1)}, bf16[80,512]{1,0:T(8,128)(2,1)}, bf16[4,40,1024]{2,1,0:T(8,128)(2,1)}) custom-call(bf16[12,6,2,512]{3,2,1,0:T(2,128)(2,1)} %bitcast.10, bf16[6,3,2,1024]{3,2,1,0:T(2,128)(2,1)} %bitcast.11, bf16[2048,128]{1,0:T(8,128)(2,1)} %refs_5_.3, bf16[1024,512]{1,0:T(8,128)(2,1)} %refs_1_.3, ...), custom_call_target="tpu_custom_call" | custom-call | tf_op jit(solution)/shard_map/prepare_kernel/pallas_call | solution.py:232
  2.9 6.6 %all-to-all-start = ((bf16[4,40,1024]{2,1,0:T(8,128)(2,1)}), bf16[4,40,1024]{2,1,0:T(8,128)(2,1)S(1)}, u32[]{:S(2)}, u32[]{:S(2)}) async-start(bf16[4,40,1024]{2,1,0:T(8,128)(2,1)} %get-tuple-element.26.refs_1_), calls=%async_computation | async-start | bytes 655360 | tf_op jit(solution)/shard_map/all_to_all | solution.py:54
  9.4 15.2 %collective-permute-start.1 = (bf16[96,512]{1,0:T(8,128)(2,1)}, bf16[96,512]{1,0:T(8,128)(2,1)S(1)}, u32[]{:S(2)}, u32[]{:S(2)}) collective-permute-start(bf16[96,512]{1,0:T(8,128)(2,1)} %get-tuple-element.28.refs_1_), channel_id=1, source_target_pairs={{0,255},{1,2},{2,1},{3,4},{4,3},{5,6},{6,5},{7,8},{8,7},{9,10},{10... | collective-permute-start | bytes 294920 | tf_op jit(solution)/shard_map/ppermute | solution.py:31
  30.9 3.6 %attend_kernel.1.refs_1_ = bf16[40,2048]{1,0:T(8,128)(2,1)} custom-call(s32[5]{0:T(128)S(1)} %stack.23.refs_0_, bf16[144,512]{1,0:T(8,128)(2,1)S(1)} %get-tuple-element.29.refs_1_, bf16[144,1536]{1,0:T(8,128)(2,1)S(1)} %get-tuple-element.30.refs_2_, bf16[72,512]{1,0:T(8,128)(2,1)S(1)} %collective-permute-done.refs_3_, ...), custom_call_target="tpu_custom_call" | custom-call | flops 1000000000 | bytes 2951188 | tf_op jit(solution)/shard_map/attend_kernel/pallas_call | solution.py:78
  37.1 4.0 %all-to-all-start.1 = ((bf16[16,80,512]{2,1,0:T(8,128)(2,1)}), bf16[16,80,512]{2,1,0:T(8,128)(2,1)S(1)}, u32[]{:S(2)}, u32[]{:S(2)}) async-start(bf16[16,80,512]{2,1,0:T(8,128)(2,1)} %spread_kernel.1), calls=%async_computation.1 | async-start | bytes 2621440 | tf_op jit(solution)/shard_map/all_to_all | solution.py:54
  41.1 5.4 %collective-permute-start.4 = (bf16[40,2048]{1,0:T(8,128)(2,1)}, bf16[40,2048]{1,0:T(8,128)(2,1)S(1)}, u32[]{:S(2)}, u32[]{:S(2)}) collective-permute-start(bf16[40,2048]{1,0:T(8,128)(2,1)} %attend_kernel.1.refs_1_), channel_id=1, source_target_pairs={{0,3},{1,2},{2,1},{3,0},{4,7},{5,6},{6,5},{7,4},{8,11},{9,10},{10,... | collective-permute-start | bytes 491528 | tf_op jit(solution)/shard_map/ppermute | solution.py:31
  46.6 2.2 %collective-permute-start.3 = (bf16[40,2048]{1,0:T(8,128)(2,1)}, bf16[40,2048]{1,0:T(8,128)(2,1)S(1)}, u32[]{:S(2)}, u32[]{:S(2)}) collective-permute-start(bf16[40,2048]{1,0:T(8,128)(2,1)} %attend_kernel.1.refs_1_), channel_id=1, source_target_pairs={{0,2},{1,3},{2,0},{3,1},{4,6},{5,7},{6,4},{7,5},{8,10},{9,11},{10,... | collective-permute-start | bytes 491528 | tf_op jit(solution)/shard_map/ppermute | solution.py:31
  48.7 2.2 %collective-permute-start.2 = (bf16[40,2048]{1,0:T(8,128)(2,1)}, bf16[40,2048]{1,0:T(8,128)(2,1)}, u32[]{:S(2)}, u32[]{:S(2)}) collective-permute-start(bf16[40,2048]{1,0:T(8,128)(2,1)} %attend_kernel.1.refs_1_), channel_id=1, source_target_pairs={{0,1},{1,0},{2,3},{3,2},{4,5},{5,4},{6,7},{7,6},{8,9},{9,8},{10,11... | collective-permute-start | bytes 491528 | tf_op jit(solution)/shard_map/ppermute | solution.py:31
  50.9 6.6 %all-to-all-done.1.refs_0_ = bf16[16,80,512]{2,1,0:T(8,128)(2,1)S(1)} async-done(((bf16[16,80,512]{2,1,0:T(8,128)(2,1)}), bf16[16,80,512]{2,1,0:T(8,128)(2,1)S(1)}, u32[]{:S(2)}, u32[]{:S(2)}) %all-to-all-start.1) | async-done | bytes 1310752 | tf_op jit(solution)/shard_map/all_to_all | solution.py:54
  57.7 7.1 %collective-permute-start.6 = (bf16[16,80,512]{2,1,0:T(8,128)(2,1)S(1)}, bf16[16,80,512]{2,1,0:T(8,128)(2,1)S(1)}, u32[]{:S(2)}, u32[]{:S(2)}) collective-permute-start(bf16[16,80,512]{2,1,0:T(8,128)(2,1)S(1)} %copy_kernel.1.refs_6_.refs_4_), channel_id=1, source_target_pairs={{0,256},{256,0},{1,257},{257,1},{2,258},{258,2},{3,259},{259,3},{4... | collective-permute-start | bytes 3932168 | tf_op jit(solution)/shard_map/ppermute | solution.py:39
  64.9 2.3 %merge_near_kernel.1 = (bf16[160,2048]{1,0:T(8,128)(2,1)S(1)}, f32[160,128]{1,0:T(8,128)S(1)}, f32[160,128]{1,0:T(8,128)S(1)}) custom-call(s32[5]{0:T(128)S(1)} %stack.23.refs_0_, bf16[40,2048]{1,0:T(8,128)(2,1)} %attend_kernel.1.refs_1_, bf16[40,2048]{1,0:T(8,128)(2,1)} %collective-permute-done.2.refs_2_, ...), custom_call_target="tpu_custom_call" | custom-call | flops 99999997952 | bytes 2490388 | tf_op jit(solution)/shard_map/merge_near_kernel/pallas_call | solution.py:78
  68.3 15.3 %all_to_all.25.refs_2_ = bf16[4,4,40,256]{3,2,1,0:T(8,128)(2,1)S(1)} all-to-all(bf16[4,4,40,256]{3,2,1,0:T(8,128)(2,1)S(1)} %merge_kernel.1), channel_id=1, replica_groups=mesh['lat'=2,'z_hi'=2,'y'=4,'x'=4,'z_half'=2,'z_near'=4] {'z_near'}, dimensions={0} | all-to-all | bytes 655360 | tf_op jit(solution)/shard_map/all_to_all | solution.py:54
  83.6 2.6 %hidden_kernel.1 = (bf16[40,1024]{1,0:T(8,128)(2,1)}, f32[160,1024]{1,0:T(8,128)S(1)}, bf16[160,1536]{1,0:T(8,128)(2,1)S(1)}) custom-call(s32[5]{0:T(128)S(1)} %stack.23.refs_0_, bf16[1024,512]{1,0:T(8,128)(2,1)} %refs_1_.3, bf16[4,4,40,256]{3,2,1,0:T(8,128)(2,1)S(1)} %all_to_all.25.refs_2_, bf16[4,40,1024]{2,1,0:T(8,128)(2,1)S(1)} %copy-done.1, ...), custom_call_target="tpu_custom_call" | custom-call | flops 1000000000 | bytes 4325396 | tf_op jit(solution)/shard_map/hidden_kernel/pallas_call | solution.py:78
  86.2 4.1 %collective-permute-start.7 = (bf16[160,1536]{1,0:T(8,128)(2,1)S(1)}, bf16[160,1536]{1,0:T(8,128)(2,1)S(1)}, u32[]{:S(2)}, u32[]{:S(2)}) collective-permute-start(bf16[160,1536]{1,0:T(8,128)(2,1)S(1)} %get-tuple-element.35.refs_2_.refs_4_), channel_id=1, source_target_pairs={{0,256},{256,0},{1,257},{257,1},{2,258},{258,2},{3,259},{259,3},{4... | collective-permute-start | bytes 1474568 | tf_op jit(solution)/shard_map/ppermute | solution.py:39
  91.8 2.1 %weight_kernel.1 = (bf16[16,32,1024]{2,1,0:T(8,128)(2,1)}, f32[160,1024]{1,0:T(8,128)}) custom-call(s32[5]{0:T(128)S(1)} %stack.23.refs_0_, bf16[4,40,1024]{2,1,0:T(8,128)(2,1)S(1)} %copy-done.1, bf16[160,1536]{1,0:T(8,128)(2,1)S(1)} %get-tuple-element.35.refs_2_.refs_4_, bf16[160,1536]{1,0:T(8,128)(2,1)S(1)} %collective-permute-done.7.refs_3_, ...), custom_call_target="tpu_custom_call" | custom-call | flops 300000000 | bytes 1966100 | tf_op jit(solution)/shard_map/weight_kernel/pallas_call | solution.py:78
  93.9 4.3 %all-to-all-start.3 = ((bf16[16,32,1024]{2,1,0:T(8,128)(2,1)}), bf16[16,32,1024]{2,1,0:T(8,128)(2,1)}, u32[]{:S(2)}, u32[]{:S(2)}) async-start(bf16[16,32,1024]{2,1,0:T(8,128)(2,1)} %get-tuple-element.37), calls=%async_computation.3 | async-start | bytes 2097152 | tf_op jit(solution)/shard_map/all_to_all | solution.py:54
  98.2 4.9 %feed_kernel.1 = (bf16[2,40,1024]{2,1,0:T(8,128)(2,1)}, bf16[2,40,1024]{2,1,0:T(8,128)(2,1)}, bf16[2,40,1024]{2,1,0:T(8,128)(2,1)}, bf16[2,40,1024]{2,1,0:T(8,128)(2,1)}) custom-call(s32[5]{0:T(128)S(1)} %stack.23.refs_0_, bf16[1024,512]{1,0:T(8,128)(2,1)} %refs_1_.3, bf16[512,1024]{1,0:T(8,128)(2,1)} %refs_2_.3, f32[160,1024]{1,0:T(8,128)} %get-tuple-element.39.refs_3_, ...), custom_call_target="tpu_custom_call" | custom-call | flops 2000000000 | bytes 6193172 | tf_op jit(solution)/shard_map/feed_kernel/pallas_call | solution.py:78
  105.2 3.3 %collective-permute-start.9 = (bf16[2,40,1024]{2,1,0:T(8,128)(2,1)}, bf16[2,40,1024]{2,1,0:T(8,128)(2,1)S(1)}, u32[]{:S(2)}, u32[]{:S(2)}) collective-permute-start(bf16[2,40,1024]{2,1,0:T(8,128)(2,1)} %get-tuple-element.42), channel_id=1, source_target_pairs={{0,2},{1,3},{2,0},{3,1},{4,6},{5,7},{6,4},{7,5},{8,10},{9,11},{10,... | collective-permute-start | bytes 491528 | tf_op jit(solution)/shard_map/ppermute | solution.py:31
  108.5 4.0 %collective-permute-start.10 = (bf16[2,40,1024]{2,1,0:T(8,128)(2,1)}, bf16[2,40,1024]{2,1,0:T(8,128)(2,1)S(1)}, u32[]{:S(2)}, u32[]{:S(2)}) collective-permute-start(bf16[2,40,1024]{2,1,0:T(8,128)(2,1)} %get-tuple-element.43), channel_id=1, source_target_pairs={{0,3},{1,2},{2,1},{3,0},{4,7},{5,6},{6,5},{7,4},{8,11},{9,10},{10,... | collective-permute-start | bytes 491528 | tf_op jit(solution)/shard_map/ppermute | solution.py:31
  112.5 2.8 %all-to-all-done.3.refs_1_ = bf16[16,32,1024]{2,1,0:T(8,128)(2,1)} async-done(((bf16[16,32,1024]{2,1,0:T(8,128)(2,1)}), bf16[16,32,1024]{2,1,0:T(8,128)(2,1)}, u32[]{:S(2)}, u32[]{:S(2)}) %all-to-all-start.3) | async-done | bytes 1048608 | tf_op jit(solution)/shard_map/all_to_all | solution.py:54
  115.3 2.0 %plane_sum_kernel.1 = bf16[4,16,512]{2,1,0:T(8,128)(2,1)} custom-call(s32[5]{0:T(128)S(1)} %stack.23.refs_0_, bf16[16,32,1024]{2,1,0:T(8,128)(2,1)} %all-to-all-done.3.refs_1_), custom_call_target="tpu_custom_call" | custom-call | bytes 1048596 | tf_op jit(solution)/shard_map/plane_sum_kernel/pallas_call | solution.py:78
  117.3 6.0 %all-to-all-start.4 = ((bf16[4,16,512]{2,1,0:T(8,128)(2,1)}), bf16[4,16,512]{2,1,0:T(8,128)(2,1)S(1)}, u32[]{:S(2)}, u32[]{:S(2)}) async-start(bf16[4,16,512]{2,1,0:T(8,128)(2,1)} %plane_sum_kernel.1), calls=%async_computation.4 | async-start | bytes 131072 | tf_op jit(solution)/shard_map/all_to_all | solution.py:54
  124.1 2.2 %finish_kernel.1 = (bf16[6,3,2,1024]{3,2,1,0:T(2,128)(2,1)}, bf16[6,3,2,1024]{3,2,1,0:T(2,128)(2,1)}) custom-call(bf16[40,1024]{1,0:T(8,128)(2,1)} %get-tuple-element.38.refs_0_, bf16[4,40,1024]{2,1,0:T(8,128)(2,1)} %get-tuple-element.26.refs_1_, bf16[2,40,1024]{2,1,0:T(8,128)(2,1)} %get-tuple-element.40.refs_2_, bf16[2,40,1024]{2,1,0:T(8,128)(2,1)} %copy-done.6, ...), custom_call_target="tpu_custom_call" | custom-call | flops 99999997952 | bytes 1064960 | tf_op jit(solution)/shard_map/finish_kernel/pallas_call | solution.py:78
  126.3 8.7 %all-to-all-done.4.refs_0_ = bf16[4,16,512]{2,1,0:T(8,128)(2,1)S(1)} async-done(((bf16[4,16,512]{2,1,0:T(8,128)(2,1)}), bf16[4,16,512]{2,1,0:T(8,128)(2,1)S(1)}, u32[]{:S(2)}, u32[]{:S(2)}) %all-to-all-start.4) | async-done | bytes 65568 | tf_op jit(solution)/shard_map/all_to_all | solution.py:54
  (39 shorter events, 14.9 us)
Async XLA Ops:
  0.6 28.7 %copy-start.2 = (bf16[512,1536]{1,0:T(8,128)(2,1)S(1)}, bf16[512,1536]{1,0:T(8,128)(2,1)}, u32[]{:S(2)}) copy-start(bf16[512,1536]{1,0:T(8,128)(2,1)} %refs_5_.2) | copy-start | bytes 4718596
  2.8 28.0 %copy-start.4 = (bf16[512,512]{1,0:T(8,128)(2,1)S(1)}, bf16[512,512]{1,0:T(8,128)(2,1)}, u32[]{:S(2)}) copy-start(bf16[512,512]{1,0:T(8,128)(2,1)} %refs_6_.1) | copy-start | bytes 1572868
  2.8 28.0 %copy-start.5 = (bf16[2,160,144]{2,1,0:T(8,128)(2,1)S(1)}, bf16[2,160,144]{2,1,0:T(8,128)(2,1)}, u32[]{:S(2)}) copy-start(bf16[2,160,144]{2,1,0:T(8,128)(2,1)} %constant.22.clone.refs_7_) | copy-start | bytes 276484
  2.9 25.7 %all-to-all-start = ((bf16[4,40,1024]{2,1,0:T(8,128)(2,1)}), bf16[4,40,1024]{2,1,0:T(8,128)(2,1)S(1)}, u32[]{:S(2)}, u32[]{:S(2)}) async-start(bf16[4,40,1024]{2,1,0:T(8,128)(2,1)} %get-tuple-element.26.refs_1_), calls=%async_computation | async-start | bytes 655360 | tf_op jit(solution)/shard_map/all_to_all | solution.py:54
  9.4 21.4 %collective-permute-start.1 = (bf16[96,512]{1,0:T(8,128)(2,1)}, bf16[96,512]{1,0:T(8,128)(2,1)S(1)}, u32[]{:S(2)}, u32[]{:S(2)}) collective-permute-start(bf16[96,512]{1,0:T(8,128)(2,1)} %get-tuple-element.28.refs_1_), channel_id=1, source_target_pairs={{0,255},{1,2},{2,1},{3,4},{4,3},{5,6},{6,5},{7,8},{8,7},{9,10},{10... | collective-permute-start | bytes 294920 | tf_op jit(solution)/shard_map/ppermute | solution.py:31
  24.6 6.2 %collective-permute-start = (bf16[72,512]{1,0:T(8,128)(2,1)}, bf16[72,512]{1,0:T(8,128)(2,1)S(1)}, u32[]{:S(2)}, u32[]{:S(2)}) collective-permute-start(bf16[72,512]{1,0:T(8,128)(2,1)} %get-tuple-element.27.refs_0_), channel_id=1, source_target_pairs={{0,1},{1,0},{2,3},{3,2},{4,5},{5,4},{6,7},{7,6},{8,9},{9,8},{10,11... | collective-permute-start | bytes 221192 | tf_op jit(solution)/shard_map/ppermute | solution.py:31
  26.6 9.3 %collective-permute-start.5 = (bf16[80,512]{1,0:T(8,128)(2,1)}, bf16[80,512]{1,0:T(8,128)(2,1)S(1)}, u32[]{:S(2)}, u32[]{:S(2)}) collective-permute-start(bf16[80,512]{1,0:T(8,128)(2,1)} %get-tuple-element.31), channel_id=1, source_target_pairs={{0,4},{1,5},{2,6},{3,7},{4,128},{5,129},{6,130},{7,131},{8,12},{9,... | collective-permute-start | bytes 245768 | tf_op jit(solution)/shard_map/ppermute | solution.py:50
  28.6 0.7 copy-start
  37.1 20.5 %all-to-all-start.1 = ((bf16[16,80,512]{2,1,0:T(8,128)(2,1)}), bf16[16,80,512]{2,1,0:T(8,128)(2,1)S(1)}, u32[]{:S(2)}, u32[]{:S(2)}) async-start(bf16[16,80,512]{2,1,0:T(8,128)(2,1)} %spread_kernel.1), calls=%async_computation.1 | async-start | bytes 2621440 | tf_op jit(solution)/shard_map/all_to_all | solution.py:54
  41.1 23.7 %copy-start.3 = (bf16[2048,128]{1,0:T(8,128)(2,1)S(1)}, bf16[2048,128]{1,0:T(8,128)(2,1)}, u32[]{:S(2)}) copy-start(bf16[2048,128]{1,0:T(8,128)(2,1)} %refs_5_.3) | copy-start | bytes 1572868
  41.1 23.7 %collective-permute-start.4 = (bf16[40,2048]{1,0:T(8,128)(2,1)}, bf16[40,2048]{1,0:T(8,128)(2,1)S(1)}, u32[]{:S(2)}, u32[]{:S(2)}) collective-permute-start(bf16[40,2048]{1,0:T(8,128)(2,1)} %attend_kernel.1.refs_1_), channel_id=1, source_target_pairs={{0,3},{1,2},{2,1},{3,0},{4,7},{5,6},{6,5},{7,4},{8,11},{9,10},{10,... | collective-permute-start | bytes 491528 | tf_op jit(solution)/shard_map/ppermute | solution.py:31
  46.6 18.3 %collective-permute-start.3 = (bf16[40,2048]{1,0:T(8,128)(2,1)}, bf16[40,2048]{1,0:T(8,128)(2,1)S(1)}, u32[]{:S(2)}, u32[]{:S(2)}) collective-permute-start(bf16[40,2048]{1,0:T(8,128)(2,1)} %attend_kernel.1.refs_1_), channel_id=1, source_target_pairs={{0,2},{1,3},{2,0},{3,1},{4,6},{5,7},{6,4},{7,5},{8,10},{9,11},{10,... | collective-permute-start | bytes 491528 | tf_op jit(solution)/shard_map/ppermute | solution.py:31
  48.7 16.1 %collective-permute-start.2 = (bf16[40,2048]{1,0:T(8,128)(2,1)}, bf16[40,2048]{1,0:T(8,128)(2,1)}, u32[]{:S(2)}, u32[]{:S(2)}) collective-permute-start(bf16[40,2048]{1,0:T(8,128)(2,1)} %attend_kernel.1.refs_1_), channel_id=1, source_target_pairs={{0,1},{1,0},{2,3},{3,2},{4,5},{5,4},{6,7},{7,6},{8,9},{9,8},{10,11... | collective-permute-start | bytes 491528 | tf_op jit(solution)/shard_map/ppermute | solution.py:31
  57.7 9.8 %collective-permute-start.6 = (bf16[16,80,512]{2,1,0:T(8,128)(2,1)S(1)}, bf16[16,80,512]{2,1,0:T(8,128)(2,1)S(1)}, u32[]{:S(2)}, u32[]{:S(2)}) collective-permute-start(bf16[16,80,512]{2,1,0:T(8,128)(2,1)S(1)} %copy_kernel.1.refs_6_.refs_4_), channel_id=1, source_target_pairs={{0,256},{256,0},{1,257},{257,1},{2,258},{258,2},{3,259},{259,3},{4... | collective-permute-start | bytes 3932168 | tf_op jit(solution)/shard_map/ppermute | solution.py:39
  67.5 16.2 %copy-start.1 = (bf16[4,40,1024]{2,1,0:T(8,128)(2,1)S(1)}, bf16[4,40,1024]{2,1,0:T(8,128)(2,1)}, u32[]{:S(2)}) copy-start(bf16[4,40,1024]{2,1,0:T(8,128)(2,1)} %copy-done) | copy-start | bytes 983044
  86.2 5.6 %collective-permute-start.7 = (bf16[160,1536]{1,0:T(8,128)(2,1)S(1)}, bf16[160,1536]{1,0:T(8,128)(2,1)S(1)}, u32[]{:S(2)}, u32[]{:S(2)}) collective-permute-start(bf16[160,1536]{1,0:T(8,128)(2,1)S(1)} %get-tuple-element.35.refs_2_.refs_4_), channel_id=1, source_target_pairs={{0,256},{256,0},{1,257},{257,1},{2,258},{258,2},{3,259},{259,3},{4... | collective-permute-start | bytes 1474568 | tf_op jit(solution)/shard_map/ppermute | solution.py:39
  93.9 21.4 %all-to-all-start.3 = ((bf16[16,32,1024]{2,1,0:T(8,128)(2,1)}), bf16[16,32,1024]{2,1,0:T(8,128)(2,1)}, u32[]{:S(2)}, u32[]{:S(2)}) async-start(bf16[16,32,1024]{2,1,0:T(8,128)(2,1)} %get-tuple-element.37), calls=%async_computation.3 | async-start | bytes 2097152 | tf_op jit(solution)/shard_map/all_to_all | solution.py:54
  103.2 20.1 %collective-permute-start.8 = (bf16[2,40,1024]{2,1,0:T(8,128)(2,1)}, bf16[2,40,1024]{2,1,0:T(8,128)(2,1)S(1)}, u32[]{:S(2)}, u32[]{:S(2)}) collective-permute-start(bf16[2,40,1024]{2,1,0:T(8,128)(2,1)} %get-tuple-element.41), channel_id=1, source_target_pairs={{0,1},{1,0},{2,3},{3,2},{4,5},{5,4},{6,7},{7,6},{8,9},{9,8},{10,11... | collective-permute-start | bytes 491528 | tf_op jit(solution)/shard_map/ppermute | solution.py:31
  105.2 18.1 %collective-permute-start.9 = (bf16[2,40,1024]{2,1,0:T(8,128)(2,1)}, bf16[2,40,1024]{2,1,0:T(8,128)(2,1)S(1)}, u32[]{:S(2)}, u32[]{:S(2)}) collective-permute-start(bf16[2,40,1024]{2,1,0:T(8,128)(2,1)} %get-tuple-element.42), channel_id=1, source_target_pairs={{0,2},{1,3},{2,0},{3,1},{4,6},{5,7},{6,4},{7,5},{8,10},{9,11},{10,... | collective-permute-start | bytes 491528 | tf_op jit(solution)/shard_map/ppermute | solution.py:31
  108.5 14.9 %collective-permute-start.10 = (bf16[2,40,1024]{2,1,0:T(8,128)(2,1)}, bf16[2,40,1024]{2,1,0:T(8,128)(2,1)S(1)}, u32[]{:S(2)}, u32[]{:S(2)}) collective-permute-start(bf16[2,40,1024]{2,1,0:T(8,128)(2,1)} %get-tuple-element.43), channel_id=1, source_target_pairs={{0,3},{1,2},{2,1},{3,0},{4,7},{5,6},{6,5},{7,4},{8,11},{9,10},{10,... | collective-permute-start | bytes 491528 | tf_op jit(solution)/shard_map/ppermute | solution.py:31
  117.3 17.7 %all-to-all-start.4 = ((bf16[4,16,512]{2,1,0:T(8,128)(2,1)}), bf16[4,16,512]{2,1,0:T(8,128)(2,1)S(1)}, u32[]{:S(2)}, u32[]{:S(2)}) async-start(bf16[4,16,512]{2,1,0:T(8,128)(2,1)} %plane_sum_kernel.1), calls=%async_computation.4 | async-start | bytes 131072 | tf_op jit(solution)/shard_map/all_to_all | solution.py:54
  123.3 0.7 copy-start.6
  123.3 0.7 copy-start.7
  123.3 0.7 copy-start.8

commit v8 on v7

--- a/solution.py
+++ b/solution.py
@@ -187,9 +187,7 @@
     at = merge_half(place, far, 1, weight)
     for half, part in enumerate((own[...], part[...] + dot(rows[:, at], weight[...]))):
         for j in range(4):
-            piece = part[ROWS * j : ROWS * j + ROWS].astype(BF16)
-            for copy in range(4):
-                result[copy, place[4] ^ j, :, 128 * half : 128 * half + 128] = piece
+            result[place[4] ^ j, :, 128 * half : 128 * half + 128] = part[ROWS * j : ROWS * j + ROWS].astype(BF16)
 
 
 def prepare_kernel(
@@ -271,16 +269,16 @@
 
 
 def hidden_kernel(
-    place, up_hbm, columns, cots, near, far, own_merged, slope, bundle, merged, own, normed, up, done
+    place, up_hbm, m0, m1, m2, m3, cots, near, far, own_merged, slope, bundle, merged, own, normed, up, done
 ):
     (fetch,) = started([(up_hbm, up, done.at[1])])
     lat, half_index, near_index = place[0], place[3], place[4]
-    for j in range(4):
+    for j, columns in enumerate((m0, m1, m2, m3)):
         for half in range(2):
-            column = pl.multiple_of(((half_index ^ half) * 4 + j) * 128, 128)
+            column = pl.multiple_of(((half_index ^ half) * 4 + (near_index ^ j)) * 128, 128)
             for block in range(4):
                 merged[ROWS * block : ROWS * block + ROWS, pl.ds(column, 128)] = columns[
-                    j, block, :, 128 * half : 128 * half + 128
+                    block, :, 128 * half : 128 * half + 128
                 ].astype(F32)
     own[...] = merged[pl.ds(pl.multiple_of(near_index * ROWS, 8), ROWS), :].astype(BF16)
     (copy,) = started([(own, own_merged, done.at[0])])
@@ -462,14 +460,14 @@
         ],
     )
     columns = call(
-        merge_kernel, shaped((4, 4, ROWS, 256)), place, rows, own, part, far, scalars=1, flops=10**8,
+        merge_kernel, shaped((4, ROWS, 256)), place, rows, own, part, far, scalars=1, flops=10**8,
         scratch_shapes=[pltpu.VMEM((1024, 128), BF16)],
     )
-    columns = exchanged(columns, "z_near")
+    columns = [columns] + [swapped(columns, j) for j in (3, 2, 1)][::-1]
     own_merged, slope, bundle = call(
         hidden_kernel,
         (shaped((ROWS, 1024)), shaped((4 * ROWS, 1024), F32), shaped((4 * ROWS, 1536))),
-        place, up_weight, columns, cots, near, far, scalars=1, hbm=(1,), hbm_out=1, flops=10**9,
+        place, up_weight, *columns, cots, near, far, scalars=1, hbm=(1,), hbm_out=1, flops=10**9,
         scratch_shapes=[
             pltpu.VMEM((4 * ROWS, 1024), F32),
             pltpu.VMEM((ROWS, 1024), BF16),

time: 137 us -> 138 us (level)
  blocking collectives: 15.3 us -> 0 us
  starting transfers between devices: 70.3 us -> 82.8 us
  waiting for transfers between devices: 21.3 us -> 24.3 us
    all_to_all x1 -> x0, blocking collectives: 15.3 us -> none  [exchanged(): return lax.all_to_all(value, axes, 0, 0)]
    ppermute x8 -> x11, starting transfers between devices: 36.2 us -> 47.4 us  [moved(): return lax.ppermute(value, LINE, [(s, target(s)) for s in range(COUNT)])]
    ppermute x8 -> x11, waiting for transfers between devices: 0.02 us -> 3 us  [moved(): return lax.ppermute(value, LINE, [(s, target(s)) for s in range(COUNT)])]
    all_to_all x4, starting transfers between devices: 20.9 us -> 22.7 us  [exchanged(): return lax.all_to_all(value, axes, 0, 0)]
  transfers between devices with their start and end apart: 15 -> 18, of which waited for: 6 -> 8; matrix products, arithmetic and copies ran while one was open for 0% -> 0% of each run, Pallas kernels for 12% -> 12%
where the time goes in v8:
time: 138 us; the launch traced here: 136 us
  starting transfers between devices  82.8 us (60%)
  Pallas kernels  26.2 us (19%)
  waiting for transfers between devices  24.3 us (18%)
  local copies, waits for them, and re-layouts  1.61 us (1%)
    ppermute x11, starting transfers between devices, moved(): return lax.ppermute(value, LINE, [(s, target(s)) for s in range(COUNT)])  47.4 us
    pallas_call x12, Pallas kernels, call(): pl.pallas_call(body, out_shape=tuple((pltpu.HBM(o.shape, o.dtype) if i <...  24 us
    all_to_all x4, starting transfers between devices, exchanged(): return lax.all_to_all(value, axes, 0, 0)  22.7 us
    all_to_all x4, waiting for transfers between devices, exchanged(): return lax.all_to_all(value, axes, 0, 0)  18.2 us
    ppermute x2, starting transfers between devices, across(): return lax.ppermute(value, 'lat', [(0, 1), (1, 0)])  10.8 us
    ppermute x11, waiting for transfers between devices, moved(): return lax.ppermute(value, LINE, [(s, target(s)) for s in range(COUNT)])  3 us
  transfers between devices with their start and end apart: 18, of which 8 were waited for; matrix products, arithmetic and copies ran while one was open for 0% of the time, Pallas kernels for 12%

profile of v8, /device:TPU:1, one launch (start us, length us, event | category | flops | bytes accessed | tf_op | source)
XLA Modules:
  0.0 135.9 jit_solution(8764539969180239622)
XLA Ops:
  0.6 2.2 %prepare_kernel.1 = (bf16[72,512]{1,0:T(8,128)(2,1)}, bf16[96,512]{1,0:T(8,128)(2,1)}, bf16[80,512]{1,0:T(8,128)(2,1)}, bf16[4,40,1024]{2,1,0:T(8,128)(2,1)}) custom-call(bf16[12,6,2,512]{3,2,1,0:T(2,128)(2,1)} %bitcast.10, bf16[6,3,2,1024]{3,2,1,0:T(2,128)(2,1)} %bitcast.11, bf16[2048,128]{1,0:T(8,128)(2,1)} %refs_5_.3, bf16[1024,512]{1,0:T(8,128)(2,1)} %refs_1_.3, ...), custom_call_target="tpu_custom_call" | custom-call | tf_op jit(solution)/shard_map/prepare_kernel/pallas_call | solution.py:230
  2.9 6.6 %all-to-all-start = ((bf16[4,40,1024]{2,1,0:T(8,128)(2,1)}), bf16[4,40,1024]{2,1,0:T(8,128)(2,1)S(1)}, u32[]{:S(2)}, u32[]{:S(2)}) async-start(bf16[4,40,1024]{2,1,0:T(8,128)(2,1)} %get-tuple-element.26.refs_1_), calls=%async_computation | async-start | bytes 655360 | tf_op jit(solution)/shard_map/all_to_all | solution.py:54
  9.5 15.2 %collective-permute-start.1 = (bf16[96,512]{1,0:T(8,128)(2,1)}, bf16[96,512]{1,0:T(8,128)(2,1)S(1)}, u32[]{:S(2)}, u32[]{:S(2)}) collective-permute-start(bf16[96,512]{1,0:T(8,128)(2,1)} %get-tuple-element.28.refs_1_), channel_id=1, source_target_pairs={{0,255},{1,2},{2,1},{3,4},{4,3},{5,6},{6,5},{7,8},{8,7},{9,10},{10... | collective-permute-start | bytes 294920 | tf_op jit(solution)/shard_map/ppermute | solution.py:31
  30.9 3.6 %attend_kernel.1.refs_1_ = bf16[40,2048]{1,0:T(8,128)(2,1)} custom-call(s32[5]{0:T(128)S(1)} %stack.23.refs_0_, bf16[144,512]{1,0:T(8,128)(2,1)S(1)} %get-tuple-element.29.refs_1_, bf16[144,1536]{1,0:T(8,128)(2,1)S(1)} %get-tuple-element.30.refs_2_, bf16[72,512]{1,0:T(8,128)(2,1)S(1)} %collective-permute-done.refs_3_, ...), custom_call_target="tpu_custom_call" | custom-call | flops 1000000000 | bytes 2951188 | tf_op jit(solution)/shard_map/attend_kernel/pallas_call | solution.py:78
  37.1 4.0 %all-to-all-start.1 = ((bf16[16,80,512]{2,1,0:T(8,128)(2,1)}), bf16[16,80,512]{2,1,0:T(8,128)(2,1)S(1)}, u32[]{:S(2)}, u32[]{:S(2)}) async-start(bf16[16,80,512]{2,1,0:T(8,128)(2,1)} %spread_kernel.1), calls=%async_computation.1 | async-start | bytes 2621440 | tf_op jit(solution)/shard_map/all_to_all | solution.py:54
  41.1 5.4 %collective-permute-start.4 = (bf16[40,2048]{1,0:T(8,128)(2,1)}, bf16[40,2048]{1,0:T(8,128)(2,1)S(1)}, u32[]{:S(2)}, u32[]{:S(2)}) collective-permute-start(bf16[40,2048]{1,0:T(8,128)(2,1)} %attend_kernel.1.refs_1_), channel_id=1, source_target_pairs={{0,3},{1,2},{2,1},{3,0},{4,7},{5,6},{6,5},{7,4},{8,11},{9,10},{10,... | collective-permute-start | bytes 491528 | tf_op jit(solution)/shard_map/ppermute | solution.py:31
  48.8 2.2 %collective-permute-start.2 = (bf16[40,2048]{1,0:T(8,128)(2,1)}, bf16[40,2048]{1,0:T(8,128)(2,1)}, u32[]{:S(2)}, u32[]{:S(2)}) collective-permute-start(bf16[40,2048]{1,0:T(8,128)(2,1)} %attend_kernel.1.refs_1_), channel_id=1, source_target_pairs={{0,1},{1,0},{2,3},{3,2},{4,5},{5,4},{6,7},{7,6},{8,9},{9,8},{10,11... | collective-permute-start | bytes 491528 | tf_op jit(solution)/shard_map/ppermute | solution.py:31
  51.0 6.7 %all-to-all-done.1.refs_0_ = bf16[16,80,512]{2,1,0:T(8,128)(2,1)S(1)} async-done(((bf16[16,80,512]{2,1,0:T(8,128)(2,1)}), bf16[16,80,512]{2,1,0:T(8,128)(2,1)S(1)}, u32[]{:S(2)}, u32[]{:S(2)}) %all-to-all-start.1) | async-done | bytes 1310752 | tf_op jit(solution)/shard_map/all_to_all | solution.py:54
  57.7 7.1 %collective-permute-start.6 = (bf16[16,80,512]{2,1,0:T(8,128)(2,1)S(1)}, bf16[16,80,512]{2,1,0:T(8,128)(2,1)S(1)}, u32[]{:S(2)}, u32[]{:S(2)}) collective-permute-start(bf16[16,80,512]{2,1,0:T(8,128)(2,1)S(1)} %copy_kernel.1.refs_6_.refs_7_), channel_id=1, source_target_pairs={{0,256},{256,0},{1,257},{257,1},{2,258},{258,2},{3,259},{259,3},{4... | collective-permute-start | bytes 3932168 | tf_op jit(solution)/shard_map/ppermute | solution.py:39
  64.9 2.3 %merge_near_kernel.1 = (bf16[160,2048]{1,0:T(8,128)(2,1)S(1)}, f32[160,128]{1,0:T(8,128)S(1)}, f32[160,128]{1,0:T(8,128)S(1)}) custom-call(s32[5]{0:T(128)S(1)} %stack.23.refs_0_, bf16[40,2048]{1,0:T(8,128)(2,1)} %attend_kernel.1.refs_1_, bf16[40,2048]{1,0:T(8,128)(2,1)} %collective-permute-done.2.refs_2_, ...), custom_call_target="tpu_custom_call" | custom-call | flops 99999997952 | bytes 2490388 | tf_op jit(solution)/shard_map/merge_near_kernel/pallas_call | solution.py:78
  68.3 3.6 %collective-permute-start.9 = (bf16[4,40,256]{2,1,0:T(8,128)(2,1)S(1)}, bf16[4,40,256]{2,1,0:T(8,128)(2,1)S(1)}, u32[]{:S(2)}, u32[]{:S(2)}) collective-permute-start(bf16[4,40,256]{2,1,0:T(8,128)(2,1)S(1)} %merge_kernel.1.refs_2_), channel_id=1, source_target_pairs={{0,3},{1,2},{2,1},{3,0},{4,7},{5,6},{6,5},{7,4},{8,11},{9,10},{10,... | collective-permute-start | bytes 245768 | tf_op jit(solution)/shard_map/ppermute | solution.py:31
  71.9 5.4 %collective-permute-start.8 = (bf16[4,40,256]{2,1,0:T(8,128)(2,1)S(1)}, bf16[4,40,256]{2,1,0:T(8,128)(2,1)S(1)}, u32[]{:S(2)}, u32[]{:S(2)}) collective-permute-start(bf16[4,40,256]{2,1,0:T(8,128)(2,1)S(1)} %merge_kernel.1.refs_2_), channel_id=1, source_target_pairs={{0,2},{1,3},{2,0},{3,1},{4,6},{5,7},{6,4},{7,5},{8,10},{9,11},{10,... | collective-permute-start | bytes 245768 | tf_op jit(solution)/shard_map/ppermute | solution.py:31
  77.3 2.2 %collective-permute-start.7 = (bf16[4,40,256]{2,1,0:T(8,128)(2,1)S(1)}, bf16[4,40,256]{2,1,0:T(8,128)(2,1)S(1)}, u32[]{:S(2)}, u32[]{:S(2)}) collective-permute-start(bf16[4,40,256]{2,1,0:T(8,128)(2,1)S(1)} %merge_kernel.1.refs_2_), channel_id=1, source_target_pairs={{0,1},{1,0},{2,3},{3,2},{4,5},{5,4},{6,7},{7,6},{8,9},{9,8},{10,11... | collective-permute-start | bytes 245768 | tf_op jit(solution)/shard_map/ppermute | solution.py:31
  79.9 2.6 %collective-permute-done.7.refs_3_ = bf16[4,40,256]{2,1,0:T(8,128)(2,1)S(1)} collective-permute-done((bf16[4,40,256]{2,1,0:T(8,128)(2,1)S(1)}, bf16[4,40,256]{2,1,0:T(8,128)(2,1)S(1)}, u32[]{:S(2)}, u32[]{:S(2)}) %collective-permute-start.7) | collective-permute-done | bytes 81952 | tf_op jit(solution)/shard_map/ppermute | solution.py:31
  82.5 2.6 %hidden_kernel.1 = (bf16[40,1024]{1,0:T(8,128)(2,1)}, f32[160,1024]{1,0:T(8,128)S(1)}, bf16[160,1536]{1,0:T(8,128)(2,1)S(1)}) custom-call(s32[5]{0:T(128)S(1)} %stack.23.refs_0_, bf16[1024,512]{1,0:T(8,128)(2,1)} %refs_1_.3, bf16[4,40,256]{2,1,0:T(8,128)(2,1)S(1)} %merge_kernel.1.refs_2_, bf16[4,40,256]{2,1,0:T(8,128)(2,1)S(1)} %collective-permute-done.7.refs_3_, ...), custom_call_target="tpu_custom_call" | custom-call | flops 1000000000 | bytes 4325396 | tf_op jit(solution)/shard_map/hidden_kernel/pallas_call | solution.py:78
  85.1 3.6 %collective-permute-start.10 = (bf16[160,1536]{1,0:T(8,128)(2,1)S(1)}, bf16[160,1536]{1,0:T(8,128)(2,1)S(1)}, u32[]{:S(2)}, u32[]{:S(2)}) collective-permute-start(bf16[160,1536]{1,0:T(8,128)(2,1)S(1)} %get-tuple-element.35.refs_2_.refs_4_), channel_id=1, source_target_pairs={{0,256},{256,0},{1,257},{257,1},{2,258},{258,2},{3,259},{259,3},{4... | collective-permute-start | bytes 1474568 | tf_op jit(solution)/shard_map/ppermute | solution.py:39
  92.4 4.4 %all-to-all-start.2 = ((bf16[16,32,1024]{2,1,0:T(8,128)(2,1)}), bf16[16,32,1024]{2,1,0:T(8,128)(2,1)}, u32[]{:S(2)}, u32[]{:S(2)}) async-start(bf16[16,32,1024]{2,1,0:T(8,128)(2,1)} %get-tuple-element.37), calls=%async_computation.2 | async-start | bytes 2097152 | tf_op jit(solution)/shard_map/all_to_all | solution.py:54
  96.8 4.9 %feed_kernel.1 = (bf16[2,40,1024]{2,1,0:T(8,128)(2,1)}, bf16[2,40,1024]{2,1,0:T(8,128)(2,1)}, bf16[2,40,1024]{2,1,0:T(8,128)(2,1)}, bf16[2,40,1024]{2,1,0:T(8,128)(2,1)}) custom-call(s32[5]{0:T(128)S(1)} %stack.23.refs_0_, bf16[1024,512]{1,0:T(8,128)(2,1)} %refs_1_.3, bf16[512,1024]{1,0:T(8,128)(2,1)} %refs_2_.3, f32[160,1024]{1,0:T(8,128)} %get-tuple-element.39.refs_3_, ...), custom_call_target="tpu_custom_call" | custom-call | flops 2000000000 | bytes 6193172 | tf_op jit(solution)/shard_map/feed_kernel/pallas_call | solution.py:78
  103.9 4.5 %collective-permute-start.12 = (bf16[2,40,1024]{2,1,0:T(8,128)(2,1)}, bf16[2,40,1024]{2,1,0:T(8,128)(2,1)S(1)}, u32[]{:S(2)}, u32[]{:S(2)}) collective-permute-start(bf16[2,40,1024]{2,1,0:T(8,128)(2,1)} %get-tuple-element.42), channel_id=1, source_target_pairs={{0,2},{1,3},{2,0},{3,1},{4,6},{5,7},{6,4},{7,5},{8,10},{9,11},{10,... | collective-permute-start | bytes 491528 | tf_op jit(solution)/shard_map/ppermute | solution.py:31
  108.5 2.5 %collective-permute-start.13 = (bf16[2,40,1024]{2,1,0:T(8,128)(2,1)}, bf16[2,40,1024]{2,1,0:T(8,128)(2,1)S(1)}, u32[]{:S(2)}, u32[]{:S(2)}) collective-permute-start(bf16[2,40,1024]{2,1,0:T(8,128)(2,1)} %get-tuple-element.43), channel_id=1, source_target_pairs={{0,3},{1,2},{2,1},{3,0},{4,7},{5,6},{6,5},{7,4},{8,11},{9,10},{10,... | collective-permute-start | bytes 491528 | tf_op jit(solution)/shard_map/ppermute | solution.py:31
  111.0 2.8 %all-to-all-done.2.refs_1_ = bf16[16,32,1024]{2,1,0:T(8,128)(2,1)} async-done(((bf16[16,32,1024]{2,1,0:T(8,128)(2,1)}), bf16[16,32,1024]{2,1,0:T(8,128)(2,1)}, u32[]{:S(2)}, u32[]{:S(2)}) %all-to-all-start.2) | async-done | bytes 1048608 | tf_op jit(solution)/shard_map/all_to_all | solution.py:54
  115.9 7.7 %all-to-all-start.3 = ((bf16[4,16,512]{2,1,0:T(8,128)(2,1)}), bf16[4,16,512]{2,1,0:T(8,128)(2,1)S(1)}, u32[]{:S(2)}, u32[]{:S(2)}) async-start(bf16[4,16,512]{2,1,0:T(8,128)(2,1)} %plane_sum_kernel.1), calls=%async_computation.3 | async-start | bytes 131072 | tf_op jit(solution)/shard_map/all_to_all | solution.py:54
  124.4 2.2 %finish_kernel.1 = (bf16[6,3,2,1024]{3,2,1,0:T(2,128)(2,1)}, bf16[6,3,2,1024]{3,2,1,0:T(2,128)(2,1)}) custom-call(bf16[40,1024]{1,0:T(8,128)(2,1)} %get-tuple-element.38.refs_0_, bf16[4,40,1024]{2,1,0:T(8,128)(2,1)} %get-tuple-element.26.refs_1_, bf16[2,40,1024]{2,1,0:T(8,128)(2,1)} %get-tuple-element.40.refs_2_, bf16[2,40,1024]{2,1,0:T(8,128)(2,1)} %copy-done.6, ...), custom_call_target="tpu_custom_call" | custom-call | flops 99999997952 | bytes 1064960 | tf_op jit(solution)/shard_map/finish_kernel/pallas_call | solution.py:78
  126.6 8.7 %all-to-all-done.3.refs_0_ = bf16[4,16,512]{2,1,0:T(8,128)(2,1)S(1)} async-done(((bf16[4,16,512]{2,1,0:T(8,128)(2,1)}), bf16[4,16,512]{2,1,0:T(8,128)(2,1)S(1)}, u32[]{:S(2)}, u32[]{:S(2)}) %all-to-all-start.3) | async-done | bytes 65568 | tf_op jit(solution)/shard_map/all_to_all | solution.py:54
  (44 shorter events, 21.8 us)
Async XLA Ops:
  0.6 28.7 %copy-start.2 = (bf16[512,1536]{1,0:T(8,128)(2,1)S(1)}, bf16[512,1536]{1,0:T(8,128)(2,1)}, u32[]{:S(2)}) copy-start(bf16[512,1536]{1,0:T(8,128)(2,1)} %refs_5_.2) | copy-start | bytes 4718596
  2.8 28.0 %copy-start.4 = (bf16[512,512]{1,0:T(8,128)(2,1)S(1)}, bf16[512,512]{1,0:T(8,128)(2,1)}, u32[]{:S(2)}) copy-start(bf16[512,512]{1,0:T(8,128)(2,1)} %refs_6_.1) | copy-start | bytes 1572868
  2.9 28.0 %copy-start.5 = (bf16[2,160,144]{2,1,0:T(8,128)(2,1)S(1)}, bf16[2,160,144]{2,1,0:T(8,128)(2,1)}, u32[]{:S(2)}) copy-start(bf16[2,160,144]{2,1,0:T(8,128)(2,1)} %constant.22.clone.refs_7_) | copy-start | bytes 276484
  2.9 25.7 %all-to-all-start = ((bf16[4,40,1024]{2,1,0:T(8,128)(2,1)}), bf16[4,40,1024]{2,1,0:T(8,128)(2,1)S(1)}, u32[]{:S(2)}, u32[]{:S(2)}) async-start(bf16[4,40,1024]{2,1,0:T(8,128)(2,1)} %get-tuple-element.26.refs_1_), calls=%async_computation | async-start | bytes 655360 | tf_op jit(solution)/shard_map/all_to_all | solution.py:54
  9.5 21.4 %collective-permute-start.1 = (bf16[96,512]{1,0:T(8,128)(2,1)}, bf16[96,512]{1,0:T(8,128)(2,1)S(1)}, u32[]{:S(2)}, u32[]{:S(2)}) collective-permute-start(bf16[96,512]{1,0:T(8,128)(2,1)} %get-tuple-element.28.refs_1_), channel_id=1, source_target_pairs={{0,255},{1,2},{2,1},{3,4},{4,3},{5,6},{6,5},{7,8},{8,7},{9,10},{10... | collective-permute-start | bytes 294920 | tf_op jit(solution)/shard_map/ppermute | solution.py:31
  24.6 6.2 %collective-permute-start = (bf16[72,512]{1,0:T(8,128)(2,1)}, bf16[72,512]{1,0:T(8,128)(2,1)S(1)}, u32[]{:S(2)}, u32[]{:S(2)}) collective-permute-start(bf16[72,512]{1,0:T(8,128)(2,1)} %get-tuple-element.27.refs_0_), channel_id=1, source_target_pairs={{0,1},{1,0},{2,3},{3,2},{4,5},{5,4},{6,7},{7,6},{8,9},{9,8},{10,11... | collective-permute-start | bytes 221192 | tf_op jit(solution)/shard_map/ppermute | solution.py:31
  26.6 9.3 %collective-permute-start.5 = (bf16[80,512]{1,0:T(8,128)(2,1)}, bf16[80,512]{1,0:T(8,128)(2,1)S(1)}, u32[]{:S(2)}, u32[]{:S(2)}) collective-permute-start(bf16[80,512]{1,0:T(8,128)(2,1)} %get-tuple-element.31), channel_id=1, source_target_pairs={{0,4},{1,5},{2,6},{3,7},{4,128},{5,129},{6,130},{7,131},{8,12},{9,... | collective-permute-start | bytes 245768 | tf_op jit(solution)/shard_map/ppermute | solution.py:50
  37.1 20.5 %all-to-all-start.1 = ((bf16[16,80,512]{2,1,0:T(8,128)(2,1)}), bf16[16,80,512]{2,1,0:T(8,128)(2,1)S(1)}, u32[]{:S(2)}, u32[]{:S(2)}) async-start(bf16[16,80,512]{2,1,0:T(8,128)(2,1)} %spread_kernel.1), calls=%async_computation.1 | async-start | bytes 2621440 | tf_op jit(solution)/shard_map/all_to_all | solution.py:54
  41.1 23.7 %copy-start.3 = (bf16[2048,128]{1,0:T(8,128)(2,1)S(1)}, bf16[2048,128]{1,0:T(8,128)(2,1)}, u32[]{:S(2)}) copy-start(bf16[2048,128]{1,0:T(8,128)(2,1)} %refs_5_.3) | copy-start | bytes 1572868
  41.1 23.7 %collective-permute-start.4 = (bf16[40,2048]{1,0:T(8,128)(2,1)}, bf16[40,2048]{1,0:T(8,128)(2,1)S(1)}, u32[]{:S(2)}, u32[]{:S(2)}) collective-permute-start(bf16[40,2048]{1,0:T(8,128)(2,1)} %attend_kernel.1.refs_1_), channel_id=1, source_target_pairs={{0,3},{1,2},{2,1},{3,0},{4,7},{5,6},{6,5},{7,4},{8,11},{9,10},{10,... | collective-permute-start | bytes 491528 | tf_op jit(solution)/shard_map/ppermute | solution.py:31
  46.6 18.3 %collective-permute-start.3 = (bf16[40,2048]{1,0:T(8,128)(2,1)}, bf16[40,2048]{1,0:T(8,128)(2,1)S(1)}, u32[]{:S(2)}, u32[]{:S(2)}) collective-permute-start(bf16[40,2048]{1,0:T(8,128)(2,1)} %attend_kernel.1.refs_1_), channel_id=1, source_target_pairs={{0,2},{1,3},{2,0},{3,1},{4,6},{5,7},{6,4},{7,5},{8,10},{9,11},{10,... | collective-permute-start | bytes 491528 | tf_op jit(solution)/shard_map/ppermute | solution.py:31
  48.8 16.1 %collective-permute-start.2 = (bf16[40,2048]{1,0:T(8,128)(2,1)}, bf16[40,2048]{1,0:T(8,128)(2,1)}, u32[]{:S(2)}, u32[]{:S(2)}) collective-permute-start(bf16[40,2048]{1,0:T(8,128)(2,1)} %attend_kernel.1.refs_1_), channel_id=1, source_target_pairs={{0,1},{1,0},{2,3},{3,2},{4,5},{5,4},{6,7},{7,6},{8,9},{9,8},{10,11... | collective-permute-start | bytes 491528 | tf_op jit(solution)/shard_map/ppermute | solution.py:31
  57.7 9.8 %collective-permute-start.6 = (bf16[16,80,512]{2,1,0:T(8,128)(2,1)S(1)}, bf16[16,80,512]{2,1,0:T(8,128)(2,1)S(1)}, u32[]{:S(2)}, u32[]{:S(2)}) collective-permute-start(bf16[16,80,512]{2,1,0:T(8,128)(2,1)S(1)} %copy_kernel.1.refs_6_.refs_7_), channel_id=1, source_target_pairs={{0,256},{256,0},{1,257},{257,1},{2,258},{258,2},{3,259},{259,3},{4... | collective-permute-start | bytes 3932168 | tf_op jit(solution)/shard_map/ppermute | solution.py:39
  67.2 15.4 %copy-start.1 = (bf16[4,40,1024]{2,1,0:T(8,128)(2,1)S(1)}, bf16[4,40,1024]{2,1,0:T(8,128)(2,1)}, u32[]{:S(2)}) copy-start(bf16[4,40,1024]{2,1,0:T(8,128)(2,1)} %copy-done) | copy-start | bytes 983044
  68.3 11.3 %collective-permute-start.9 = (bf16[4,40,256]{2,1,0:T(8,128)(2,1)S(1)}, bf16[4,40,256]{2,1,0:T(8,128)(2,1)S(1)}, u32[]{:S(2)}, u32[]{:S(2)}) collective-permute-start(bf16[4,40,256]{2,1,0:T(8,128)(2,1)S(1)} %merge_kernel.1.refs_2_), channel_id=1, source_target_pairs={{0,3},{1,2},{2,1},{3,0},{4,7},{5,6},{6,5},{7,4},{8,11},{9,10},{10,... | collective-permute-start | bytes 245768 | tf_op jit(solution)/shard_map/ppermute | solution.py:31
  71.9 8.0 %collective-permute-start.8 = (bf16[4,40,256]{2,1,0:T(8,128)(2,1)S(1)}, bf16[4,40,256]{2,1,0:T(8,128)(2,1)S(1)}, u32[]{:S(2)}, u32[]{:S(2)}) collective-permute-start(bf16[4,40,256]{2,1,0:T(8,128)(2,1)S(1)} %merge_kernel.1.refs_2_), channel_id=1, source_target_pairs={{0,2},{1,3},{2,0},{3,1},{4,6},{5,7},{6,4},{7,5},{8,10},{9,11},{10,... | collective-permute-start | bytes 245768 | tf_op jit(solution)/shard_map/ppermute | solution.py:31
  77.3 5.2 %collective-permute-start.7 = (bf16[4,40,256]{2,1,0:T(8,128)(2,1)S(1)}, bf16[4,40,256]{2,1,0:T(8,128)(2,1)S(1)}, u32[]{:S(2)}, u32[]{:S(2)}) collective-permute-start(bf16[4,40,256]{2,1,0:T(8,128)(2,1)S(1)} %merge_kernel.1.refs_2_), channel_id=1, source_target_pairs={{0,1},{1,0},{2,3},{3,2},{4,5},{5,4},{6,7},{7,6},{8,9},{9,8},{10,11... | collective-permute-start | bytes 245768 | tf_op jit(solution)/shard_map/ppermute | solution.py:31
  85.1 5.1 %collective-permute-start.10 = (bf16[160,1536]{1,0:T(8,128)(2,1)S(1)}, bf16[160,1536]{1,0:T(8,128)(2,1)S(1)}, u32[]{:S(2)}, u32[]{:S(2)}) collective-permute-start(bf16[160,1536]{1,0:T(8,128)(2,1)S(1)} %get-tuple-element.35.refs_2_.refs_4_), channel_id=1, source_target_pairs={{0,256},{256,0},{1,257},{257,1},{2,258},{258,2},{3,259},{259,3},{4... | collective-permute-start | bytes 1474568 | tf_op jit(solution)/shard_map/ppermute | solution.py:39
  92.4 21.4 %all-to-all-start.2 = ((bf16[16,32,1024]{2,1,0:T(8,128)(2,1)}), bf16[16,32,1024]{2,1,0:T(8,128)(2,1)}, u32[]{:S(2)}, u32[]{:S(2)}) async-start(bf16[16,32,1024]{2,1,0:T(8,128)(2,1)} %get-tuple-element.37), calls=%async_computation.2 | async-start | bytes 2097152 | tf_op jit(solution)/shard_map/all_to_all | solution.py:54
  101.7 21.9 %collective-permute-start.11 = (bf16[2,40,1024]{2,1,0:T(8,128)(2,1)}, bf16[2,40,1024]{2,1,0:T(8,128)(2,1)S(1)}, u32[]{:S(2)}, u32[]{:S(2)}) collective-permute-start(bf16[2,40,1024]{2,1,0:T(8,128)(2,1)} %get-tuple-element.41), channel_id=1, source_target_pairs={{0,1},{1,0},{2,3},{3,2},{4,5},{5,4},{6,7},{7,6},{8,9},{9,8},{10,11... | collective-permute-start | bytes 491528 | tf_op jit(solution)/shard_map/ppermute | solution.py:31
  103.9 19.7 %collective-permute-start.12 = (bf16[2,40,1024]{2,1,0:T(8,128)(2,1)}, bf16[2,40,1024]{2,1,0:T(8,128)(2,1)S(1)}, u32[]{:S(2)}, u32[]{:S(2)}) collective-permute-start(bf16[2,40,1024]{2,1,0:T(8,128)(2,1)} %get-tuple-element.42), channel_id=1, source_target_pairs={{0,2},{1,3},{2,0},{3,1},{4,6},{5,7},{6,4},{7,5},{8,10},{9,11},{10,... | collective-permute-start | bytes 491528 | tf_op jit(solution)/shard_map/ppermute | solution.py:31
  108.5 15.1 %collective-permute-start.13 = (bf16[2,40,1024]{2,1,0:T(8,128)(2,1)}, bf16[2,40,1024]{2,1,0:T(8,128)(2,1)S(1)}, u32[]{:S(2)}, u32[]{:S(2)}) collective-permute-start(bf16[2,40,1024]{2,1,0:T(8,128)(2,1)} %get-tuple-element.43), channel_id=1, source_target_pairs={{0,3},{1,2},{2,1},{3,0},{4,7},{5,6},{6,5},{7,4},{8,11},{9,10},{10,... | collective-permute-start | bytes 491528 | tf_op jit(solution)/shard_map/ppermute | solution.py:31
  115.9 19.4 %all-to-all-start.3 = ((bf16[4,16,512]{2,1,0:T(8,128)(2,1)}), bf16[4,16,512]{2,1,0:T(8,128)(2,1)S(1)}, u32[]{:S(2)}, u32[]{:S(2)}) async-start(bf16[4,16,512]{2,1,0:T(8,128)(2,1)} %plane_sum_kernel.1), calls=%async_computation.3 | async-start | bytes 131072 | tf_op jit(solution)/shard_map/all_to_all | solution.py:54
  123.6 0.8 copy-start.8
  (3 other events, 2.1 us)

commit v9 on v7

--- a/solution.py
+++ b/solution.py
@@ -286,13 +286,15 @@
     (copy,) = started([(own, own_merged, done.at[0])])
     normed[...] = norm_rows(merged[...]).astype(BF16)
     fetch.wait()
-    value, slope[:, 0:512] = gelu_parts(dot(normed[...], up[...]))
+    value, rate = gelu_parts(dot(normed[...], up[...]))
+    slope[:, 0:512] = rate.astype(BF16)
     bundle[:, 0:512] = value.astype(BF16)
     preact = 0.0
     for side, source in enumerate((near, far)):
         at = pl.ds(pl.multiple_of((lat ^ side) * 512, 512), 512)
         preact = preact + dot(normed[:, at], up_half(source))
-    value, slope[:, 512:1024] = gelu_parts(preact)
+    value, rate = gelu_parts(preact)
+    slope[:, 512:1024] = rate.astype(BF16)
     bundle[:, 512:1024] = value.astype(BF16)
     bundle[:, 1024:1536] = stacked_rows(cots, pl.ds(pl.multiple_of((1 - lat) * 512, 512), 512))
     copy.wait()
@@ -317,9 +319,9 @@
     copies[0].wait()
     for side, grad in enumerate(far_hidden):
         at = pl.ds(pl.multiple_of(512 + (place[0] ^ side) * 256, 256), 256)
-        far_grads.append((grad * slope[:, at]).astype(BF16))
+        far_grads.append((grad * slope[:, at].astype(F32)).astype(BF16))
     copies[1].wait()
-    own_grad = (dot_nt(cots, down[...]) * slope[:, 0:512]).astype(BF16)
+    own_grad = (dot_nt(cots, down[...]) * slope[:, 0:512].astype(F32)).astype(BF16)
     values[...] = dot(bundle[:, 0:512], down[...]) + jnp.concatenate(far_values, axis=1)
     copies[2].wait()
     grads[...] = dot_nt(own_grad, up[...])
@@ -468,7 +470,7 @@
     columns = exchanged(columns, "z_near")
     own_merged, slope, bundle = call(
         hidden_kernel,
-        (shaped((ROWS, 1024)), shaped((4 * ROWS, 1024), F32), shaped((4 * ROWS, 1536))),
+        (shaped((ROWS, 1024)), shaped((4 * ROWS, 1024)), shaped((4 * ROWS, 1536))),
         place, up_weight, columns, cots, near, far, scalars=1, hbm=(1,), hbm_out=1, flops=10**9,
         scratch_shapes=[
             pltpu.VMEM((4 * ROWS, 1024), F32),
@@ -480,7 +482,7 @@
     )
     other = across(bundle)
     parts, slope = call(
-        weight_kernel, (shaped((16, 32, 1024)), shaped((4 * ROWS, 1024), F32)), place, cots, bundle, other, slope,
+        weight_kernel, (shaped((16, 32, 1024)), shaped((4 * ROWS, 1024))), place, cots, bundle, other, slope,
         scalars=1, hbm_out=2, flops=3 * 10**8,
         scratch_shapes=[pltpu.VMEM((2, 16, 16, 1024), BF16), pltpu.SemaphoreType.DMA((3,))],
     )
@@ -495,7 +497,7 @@
             pltpu.VMEM((4, 2, ROWS, 1024), BF16),
             pltpu.VMEM((1024, 512), BF16),
             pltpu.VMEM((512, 1024), BF16),
-            pltpu.VMEM((4 * ROWS, 1024), F32),
+            pltpu.VMEM((4 * ROWS, 1024), BF16),
             pltpu.SemaphoreType.DMA((7,)),
         ],
     )

time: 137 us -> 137 us (level)
  no operation moved by 1% of the time
where the time goes in v9:
time: 137 us; the launch traced here: 136 us
  starting transfers between devices  70.2 us (51%)
  Pallas kernels  26.1 us (19%)
  waiting for transfers between devices  21.4 us (16%)
  blocking collectives  15.3 us (11%)
  local copies, waits for them, and re-layouts  1.59 us (1%)
    ppermute x8, starting transfers between devices, moved(): return lax.ppermute(value, LINE, [(s, target(s)) for s in range(COUNT)])  36.2 us
    pallas_call x12, Pallas kernels, call(): pl.pallas_call(body, out_shape=tuple((pltpu.HBM(o.shape, o.dtype) if i <...  23.9 us
    all_to_all x4, starting transfers between devices, exchanged(): return lax.all_to_all(value, axes, 0, 0)  20.9 us
    all_to_all x4, waiting for transfers between devices, exchanged(): return lax.all_to_all(value, axes, 0, 0)  18.2 us
    all_to_all x1, blocking collectives, exchanged(): return lax.all_to_all(value, axes, 0, 0)  15.3 us
    ppermute x2, starting transfers between devices, across(): return lax.ppermute(value, 'lat', [(0, 1), (1, 0)])  11.3 us
  transfers between devices with their start and end apart: 15, of which 6 were waited for; matrix products, arithmetic and copies ran while one was open for 0% of the time, Pallas kernels for 12%

profile of v9, /device:TPU:1, one launch (start us, length us, event | category | flops | bytes accessed | tf_op | source)
XLA Modules:
  0.0 135.6 jit_solution(2956919192733383525)
XLA Ops:
  0.6 2.2 %prepare_kernel.1 = (bf16[72,512]{1,0:T(8,128)(2,1)}, bf16[96,512]{1,0:T(8,128)(2,1)}, bf16[80,512]{1,0:T(8,128)(2,1)}, bf16[4,40,1024]{2,1,0:T(8,128)(2,1)}) custom-call(bf16[12,6,2,512]{3,2,1,0:T(2,128)(2,1)} %bitcast.10, bf16[6,3,2,1024]{3,2,1,0:T(2,128)(2,1)} %bitcast.11, bf16[2048,128]{1,0:T(8,128)(2,1)} %refs_5_.3, bf16[1024,512]{1,0:T(8,128)(2,1)} %refs_1_.3, ...), custom_call_target="tpu_custom_call" | custom-call | tf_op jit(solution)/shard_map/prepare_kernel/pallas_call | solution.py:232
  2.9 6.6 %all-to-all-start = ((bf16[4,40,1024]{2,1,0:T(8,128)(2,1)}), bf16[4,40,1024]{2,1,0:T(8,128)(2,1)S(1)}, u32[]{:S(2)}, u32[]{:S(2)}) async-start(bf16[4,40,1024]{2,1,0:T(8,128)(2,1)} %get-tuple-element.26.refs_1_), calls=%async_computation | async-start | bytes 655360 | tf_op jit(solution)/shard_map/all_to_all | solution.py:54
  9.4 15.2 %collective-permute-start.1 = (bf16[96,512]{1,0:T(8,128)(2,1)}, bf16[96,512]{1,0:T(8,128)(2,1)S(1)}, u32[]{:S(2)}, u32[]{:S(2)}) collective-permute-start(bf16[96,512]{1,0:T(8,128)(2,1)} %get-tuple-element.28.refs_1_), channel_id=1, source_target_pairs={{0,255},{1,2},{2,1},{3,4},{4,3},{5,6},{6,5},{7,8},{8,7},{9,10},{10... | collective-permute-start | bytes 294920 | tf_op jit(solution)/shard_map/ppermute | solution.py:31
  30.9 3.6 %attend_kernel.1.refs_1_ = bf16[40,2048]{1,0:T(8,128)(2,1)} custom-call(s32[5]{0:T(128)S(1)} %stack.23.refs_0_, bf16[144,512]{1,0:T(8,128)(2,1)S(1)} %get-tuple-element.29.refs_1_, bf16[144,1536]{1,0:T(8,128)(2,1)S(1)} %get-tuple-element.30.refs_2_, bf16[72,512]{1,0:T(8,128)(2,1)S(1)} %collective-permute-done.refs_3_, ...), custom_call_target="tpu_custom_call" | custom-call | flops 1000000000 | bytes 2951188 | tf_op jit(solution)/shard_map/attend_kernel/pallas_call | solution.py:78
  37.1 4.0 %all-to-all-start.1 = ((bf16[16,80,512]{2,1,0:T(8,128)(2,1)}), bf16[16,80,512]{2,1,0:T(8,128)(2,1)S(1)}, u32[]{:S(2)}, u32[]{:S(2)}) async-start(bf16[16,80,512]{2,1,0:T(8,128)(2,1)} %spread_kernel.1), calls=%async_computation.1 | async-start | bytes 2621440 | tf_op jit(solution)/shard_map/all_to_all | solution.py:54
  41.1 5.4 %collective-permute-start.4 = (bf16[40,2048]{1,0:T(8,128)(2,1)}, bf16[40,2048]{1,0:T(8,128)(2,1)S(1)}, u32[]{:S(2)}, u32[]{:S(2)}) collective-permute-start(bf16[40,2048]{1,0:T(8,128)(2,1)} %attend_kernel.1.refs_1_), channel_id=1, source_target_pairs={{0,3},{1,2},{2,1},{3,0},{4,7},{5,6},{6,5},{7,4},{8,11},{9,10},{10,... | collective-permute-start | bytes 491528 | tf_op jit(solution)/shard_map/ppermute | solution.py:31
  46.5 2.2 %collective-permute-start.3 = (bf16[40,2048]{1,0:T(8,128)(2,1)}, bf16[40,2048]{1,0:T(8,128)(2,1)S(1)}, u32[]{:S(2)}, u32[]{:S(2)}) collective-permute-start(bf16[40,2048]{1,0:T(8,128)(2,1)} %attend_kernel.1.refs_1_), channel_id=1, source_target_pairs={{0,2},{1,3},{2,0},{3,1},{4,6},{5,7},{6,4},{7,5},{8,10},{9,11},{10,... | collective-permute-start | bytes 491528 | tf_op jit(solution)/shard_map/ppermute | solution.py:31
  48.7 2.2 %collective-permute-start.2 = (bf16[40,2048]{1,0:T(8,128)(2,1)}, bf16[40,2048]{1,0:T(8,128)(2,1)}, u32[]{:S(2)}, u32[]{:S(2)}) collective-permute-start(bf16[40,2048]{1,0:T(8,128)(2,1)} %attend_kernel.1.refs_1_), channel_id=1, source_target_pairs={{0,1},{1,0},{2,3},{3,2},{4,5},{5,4},{6,7},{7,6},{8,9},{9,8},{10,11... | collective-permute-start | bytes 491528 | tf_op jit(solution)/shard_map/ppermute | solution.py:31
  50.9 6.6 %all-to-all-done.1.refs_0_ = bf16[16,80,512]{2,1,0:T(8,128)(2,1)S(1)} async-done(((bf16[16,80,512]{2,1,0:T(8,128)(2,1)}), bf16[16,80,512]{2,1,0:T(8,128)(2,1)S(1)}, u32[]{:S(2)}, u32[]{:S(2)}) %all-to-all-start.1) | async-done | bytes 1310752 | tf_op jit(solution)/shard_map/all_to_all | solution.py:54
  57.7 7.1 %collective-permute-start.6 = (bf16[16,80,512]{2,1,0:T(8,128)(2,1)S(1)}, bf16[16,80,512]{2,1,0:T(8,128)(2,1)S(1)}, u32[]{:S(2)}, u32[]{:S(2)}) collective-permute-start(bf16[16,80,512]{2,1,0:T(8,128)(2,1)S(1)} %copy_kernel.1.refs_6_.refs_4_), channel_id=1, source_target_pairs={{0,256},{256,0},{1,257},{257,1},{2,258},{258,2},{3,259},{259,3},{4... | collective-permute-start | bytes 3932168 | tf_op jit(solution)/shard_map/ppermute | solution.py:39
  64.9 2.3 %merge_near_kernel.1 = (bf16[160,2048]{1,0:T(8,128)(2,1)S(1)}, f32[160,128]{1,0:T(8,128)S(1)}, f32[160,128]{1,0:T(8,128)S(1)}) custom-call(s32[5]{0:T(128)S(1)} %stack.23.refs_0_, bf16[40,2048]{1,0:T(8,128)(2,1)} %attend_kernel.1.refs_1_, bf16[40,2048]{1,0:T(8,128)(2,1)} %collective-permute-done.2.refs_2_, ...), custom_call_target="tpu_custom_call" | custom-call | flops 99999997952 | bytes 2490388 | tf_op jit(solution)/shard_map/merge_near_kernel/pallas_call | solution.py:78
  68.3 15.3 %all_to_all.25.refs_2_ = bf16[4,4,40,256]{3,2,1,0:T(8,128)(2,1)S(1)} all-to-all(bf16[4,4,40,256]{3,2,1,0:T(8,128)(2,1)S(1)} %merge_kernel.1), channel_id=1, replica_groups=mesh['lat'=2,'z_hi'=2,'y'=4,'x'=4,'z_half'=2,'z_near'=4] {'z_near'}, dimensions={0} | all-to-all | bytes 655360 | tf_op jit(solution)/shard_map/all_to_all | solution.py:54
  83.6 2.6 %hidden_kernel.1 = (bf16[40,1024]{1,0:T(8,128)(2,1)}, bf16[160,1024]{1,0:T(8,128)(2,1)S(1)}, bf16[160,1536]{1,0:T(8,128)(2,1)S(1)}) custom-call(s32[5]{0:T(128)S(1)} %stack.23.refs_0_, bf16[1024,512]{1,0:T(8,128)(2,1)} %refs_1_.3, bf16[4,4,40,256]{3,2,1,0:T(8,128)(2,1)S(1)} %all_to_all.25.refs_2_, bf16[4,40,1024]{2,1,0:T(8,128)(2,1)S(1)} %copy-done.1, ...), custom_call_target="tpu_custom_call" | custom-call | flops 1000000000 | bytes 4325396 | tf_op jit(solution)/shard_map/hidden_kernel/pallas_call | solution.py:78
  86.2 4.1 %collective-permute-start.7 = (bf16[160,1536]{1,0:T(8,128)(2,1)S(1)}, bf16[160,1536]{1,0:T(8,128)(2,1)S(1)}, u32[]{:S(2)}, u32[]{:S(2)}) collective-permute-start(bf16[160,1536]{1,0:T(8,128)(2,1)S(1)} %get-tuple-element.35.refs_2_.refs_4_), channel_id=1, source_target_pairs={{0,256},{256,0},{1,257},{257,1},{2,258},{258,2},{3,259},{259,3},{4... | collective-permute-start | bytes 1474568 | tf_op jit(solution)/shard_map/ppermute | solution.py:39
  91.8 2.1 %weight_kernel.1 = (bf16[16,32,1024]{2,1,0:T(8,128)(2,1)}, bf16[160,1024]{1,0:T(8,128)(2,1)}) custom-call(s32[5]{0:T(128)S(1)} %stack.23.refs_0_, bf16[4,40,1024]{2,1,0:T(8,128)(2,1)S(1)} %copy-done.1, bf16[160,1536]{1,0:T(8,128)(2,1)S(1)} %get-tuple-element.35.refs_2_.refs_4_, bf16[160,1536]{1,0:T(8,128)(2,1)S(1)} %collective-permute-done.7.refs_3_, ...), custom_call_target="tpu_custom_call" | custom-call | flops 300000000 | bytes 1638420 | tf_op jit(solution)/shard_map/weight_kernel/pallas_call | solution.py:78
  93.9 4.3 %all-to-all-start.3 = ((bf16[16,32,1024]{2,1,0:T(8,128)(2,1)}), bf16[16,32,1024]{2,1,0:T(8,128)(2,1)}, u32[]{:S(2)}, u32[]{:S(2)}) async-start(bf16[16,32,1024]{2,1,0:T(8,128)(2,1)} %get-tuple-element.37), calls=%async_computation.3 | async-start | bytes 2097152 | tf_op jit(solution)/shard_map/all_to_all | solution.py:54
  98.2 4.8 %feed_kernel.1 = (bf16[2,40,1024]{2,1,0:T(8,128)(2,1)}, bf16[2,40,1024]{2,1,0:T(8,128)(2,1)}, bf16[2,40,1024]{2,1,0:T(8,128)(2,1)}, bf16[2,40,1024]{2,1,0:T(8,128)(2,1)}) custom-call(s32[5]{0:T(128)S(1)} %stack.23.refs_0_, bf16[1024,512]{1,0:T(8,128)(2,1)} %refs_1_.3, bf16[512,1024]{1,0:T(8,128)(2,1)} %refs_2_.3, ...), custom_call_target="tpu_custom_call" | custom-call | flops 2000000000 | bytes 5865492 | tf_op jit(solution)/shard_map/feed_kernel/pallas_call | solution.py:78
  105.1 3.3 %collective-permute-start.9 = (bf16[2,40,1024]{2,1,0:T(8,128)(2,1)}, bf16[2,40,1024]{2,1,0:T(8,128)(2,1)S(1)}, u32[]{:S(2)}, u32[]{:S(2)}) collective-permute-start(bf16[2,40,1024]{2,1,0:T(8,128)(2,1)} %get-tuple-element.42), channel_id=1, source_target_pairs={{0,2},{1,3},{2,0},{3,1},{4,6},{5,7},{6,4},{7,5},{8,10},{9,11},{10,... | collective-permute-start | bytes 491528 | tf_op jit(solution)/shard_map/ppermute | solution.py:31
  108.4 4.0 %collective-permute-start.10 = (bf16[2,40,1024]{2,1,0:T(8,128)(2,1)}, bf16[2,40,1024]{2,1,0:T(8,128)(2,1)S(1)}, u32[]{:S(2)}, u32[]{:S(2)}) collective-permute-start(bf16[2,40,1024]{2,1,0:T(8,128)(2,1)} %get-tuple-element.43), channel_id=1, source_target_pairs={{0,3},{1,2},{2,1},{3,0},{4,7},{5,6},{6,5},{7,4},{8,11},{9,10},{10,... | collective-permute-start | bytes 491528 | tf_op jit(solution)/shard_map/ppermute | solution.py:31
  112.4 3.0 %all-to-all-done.3.refs_1_ = bf16[16,32,1024]{2,1,0:T(8,128)(2,1)} async-done(((bf16[16,32,1024]{2,1,0:T(8,128)(2,1)}), bf16[16,32,1024]{2,1,0:T(8,128)(2,1)}, u32[]{:S(2)}, u32[]{:S(2)}) %all-to-all-start.3) | async-done | bytes 1048608 | tf_op jit(solution)/shard_map/all_to_all | solution.py:54
  115.3 2.0 %plane_sum_kernel.1 = bf16[4,16,512]{2,1,0:T(8,128)(2,1)} custom-call(s32[5]{0:T(128)S(1)} %stack.23.refs_0_, bf16[16,32,1024]{2,1,0:T(8,128)(2,1)} %all-to-all-done.3.refs_1_), custom_call_target="tpu_custom_call" | custom-call | bytes 1048596 | tf_op jit(solution)/shard_map/plane_sum_kernel/pallas_call | solution.py:78
  117.4 5.9 %all-to-all-start.4 = ((bf16[4,16,512]{2,1,0:T(8,128)(2,1)}), bf16[4,16,512]{2,1,0:T(8,128)(2,1)S(1)}, u32[]{:S(2)}, u32[]{:S(2)}) async-start(bf16[4,16,512]{2,1,0:T(8,128)(2,1)} %plane_sum_kernel.1), calls=%async_computation.4 | async-start | bytes 131072 | tf_op jit(solution)/shard_map/all_to_all | solution.py:54
  124.1 2.2 %finish_kernel.1 = (bf16[6,3,2,1024]{3,2,1,0:T(2,128)(2,1)}, bf16[6,3,2,1024]{3,2,1,0:T(2,128)(2,1)}) custom-call(bf16[40,1024]{1,0:T(8,128)(2,1)} %get-tuple-element.38.refs_0_, bf16[4,40,1024]{2,1,0:T(8,128)(2,1)} %get-tuple-element.26.refs_1_, bf16[2,40,1024]{2,1,0:T(8,128)(2,1)} %get-tuple-element.40.refs_2_, bf16[2,40,1024]{2,1,0:T(8,128)(2,1)} %copy-done.6, ...), custom_call_target="tpu_custom_call" | custom-call | flops 99999997952 | bytes 1064960 | tf_op jit(solution)/shard_map/finish_kernel/pallas_call | solution.py:78
  126.3 8.6 %all-to-all-done.4.refs_0_ = bf16[4,16,512]{2,1,0:T(8,128)(2,1)S(1)} async-done(((bf16[4,16,512]{2,1,0:T(8,128)(2,1)}), bf16[4,16,512]{2,1,0:T(8,128)(2,1)S(1)}, u32[]{:S(2)}, u32[]{:S(2)}) %all-to-all-start.4) | async-done | bytes 65568 | tf_op jit(solution)/shard_map/all_to_all | solution.py:54
  (39 shorter events, 14.9 us)
Async XLA Ops:
  0.6 28.7 %copy-start.2 = (bf16[512,1536]{1,0:T(8,128)(2,1)S(1)}, bf16[512,1536]{1,0:T(8,128)(2,1)}, u32[]{:S(2)}) copy-start(bf16[512,1536]{1,0:T(8,128)(2,1)} %refs_5_.2) | copy-start | bytes 4718596
  2.8 28.0 %copy-start.4 = (bf16[512,512]{1,0:T(8,128)(2,1)S(1)}, bf16[512,512]{1,0:T(8,128)(2,1)}, u32[]{:S(2)}) copy-start(bf16[512,512]{1,0:T(8,128)(2,1)} %refs_6_.1) | copy-start | bytes 1572868
  2.8 28.0 %copy-start.5 = (bf16[2,160,144]{2,1,0:T(8,128)(2,1)S(1)}, bf16[2,160,144]{2,1,0:T(8,128)(2,1)}, u32[]{:S(2)}) copy-start(bf16[2,160,144]{2,1,0:T(8,128)(2,1)} %constant.22.clone.refs_7_) | copy-start | bytes 276484
  2.9 25.7 %all-to-all-start = ((bf16[4,40,1024]{2,1,0:T(8,128)(2,1)}), bf16[4,40,1024]{2,1,0:T(8,128)(2,1)S(1)}, u32[]{:S(2)}, u32[]{:S(2)}) async-start(bf16[4,40,1024]{2,1,0:T(8,128)(2,1)} %get-tuple-element.26.refs_1_), calls=%async_computation | async-start | bytes 655360 | tf_op jit(solution)/shard_map/all_to_all | solution.py:54
  9.4 21.4 %collective-permute-start.1 = (bf16[96,512]{1,0:T(8,128)(2,1)}, bf16[96,512]{1,0:T(8,128)(2,1)S(1)}, u32[]{:S(2)}, u32[]{:S(2)}) collective-permute-start(bf16[96,512]{1,0:T(8,128)(2,1)} %get-tuple-element.28.refs_1_), channel_id=1, source_target_pairs={{0,255},{1,2},{2,1},{3,4},{4,3},{5,6},{6,5},{7,8},{8,7},{9,10},{10... | collective-permute-start | bytes 294920 | tf_op jit(solution)/shard_map/ppermute | solution.py:31
  24.6 6.2 %collective-permute-start = (bf16[72,512]{1,0:T(8,128)(2,1)}, bf16[72,512]{1,0:T(8,128)(2,1)S(1)}, u32[]{:S(2)}, u32[]{:S(2)}) collective-permute-start(bf16[72,512]{1,0:T(8,128)(2,1)} %get-tuple-element.27.refs_0_), channel_id=1, source_target_pairs={{0,1},{1,0},{2,3},{3,2},{4,5},{5,4},{6,7},{7,6},{8,9},{9,8},{10,11... | collective-permute-start | bytes 221192 | tf_op jit(solution)/shard_map/ppermute | solution.py:31
  26.6 9.3 %collective-permute-start.5 = (bf16[80,512]{1,0:T(8,128)(2,1)}, bf16[80,512]{1,0:T(8,128)(2,1)S(1)}, u32[]{:S(2)}, u32[]{:S(2)}) collective-permute-start(bf16[80,512]{1,0:T(8,128)(2,1)} %get-tuple-element.31), channel_id=1, source_target_pairs={{0,4},{1,5},{2,6},{3,7},{4,128},{5,129},{6,130},{7,131},{8,12},{9,... | collective-permute-start | bytes 245768 | tf_op jit(solution)/shard_map/ppermute | solution.py:50
  28.6 0.7 copy-start
  37.1 20.5 %all-to-all-start.1 = ((bf16[16,80,512]{2,1,0:T(8,128)(2,1)}), bf16[16,80,512]{2,1,0:T(8,128)(2,1)S(1)}, u32[]{:S(2)}, u32[]{:S(2)}) async-start(bf16[16,80,512]{2,1,0:T(8,128)(2,1)} %spread_kernel.1), calls=%async_computation.1 | async-start | bytes 2621440 | tf_op jit(solution)/shard_map/all_to_all | solution.py:54
  41.1 23.7 %copy-start.3 = (bf16[2048,128]{1,0:T(8,128)(2,1)S(1)}, bf16[2048,128]{1,0:T(8,128)(2,1)}, u32[]{:S(2)}) copy-start(bf16[2048,128]{1,0:T(8,128)(2,1)} %refs_5_.3) | copy-start | bytes 1572868
  41.1 23.7 %collective-permute-start.4 = (bf16[40,2048]{1,0:T(8,128)(2,1)}, bf16[40,2048]{1,0:T(8,128)(2,1)S(1)}, u32[]{:S(2)}, u32[]{:S(2)}) collective-permute-start(bf16[40,2048]{1,0:T(8,128)(2,1)} %attend_kernel.1.refs_1_), channel_id=1, source_target_pairs={{0,3},{1,2},{2,1},{3,0},{4,7},{5,6},{6,5},{7,4},{8,11},{9,10},{10,... | collective-permute-start | bytes 491528 | tf_op jit(solution)/shard_map/ppermute | solution.py:31
  46.5 18.3 %collective-permute-start.3 = (bf16[40,2048]{1,0:T(8,128)(2,1)}, bf16[40,2048]{1,0:T(8,128)(2,1)S(1)}, u32[]{:S(2)}, u32[]{:S(2)}) collective-permute-start(bf16[40,2048]{1,0:T(8,128)(2,1)} %attend_kernel.1.refs_1_), channel_id=1, source_target_pairs={{0,2},{1,3},{2,0},{3,1},{4,6},{5,7},{6,4},{7,5},{8,10},{9,11},{10,... | collective-permute-start | bytes 491528 | tf_op jit(solution)/shard_map/ppermute | solution.py:31
  48.7 16.1 %collective-permute-start.2 = (bf16[40,2048]{1,0:T(8,128)(2,1)}, bf16[40,2048]{1,0:T(8,128)(2,1)}, u32[]{:S(2)}, u32[]{:S(2)}) collective-permute-start(bf16[40,2048]{1,0:T(8,128)(2,1)} %attend_kernel.1.refs_1_), channel_id=1, source_target_pairs={{0,1},{1,0},{2,3},{3,2},{4,5},{5,4},{6,7},{7,6},{8,9},{9,8},{10,11... | collective-permute-start | bytes 491528 | tf_op jit(solution)/shard_map/ppermute | solution.py:31
  57.7 9.8 %collective-permute-start.6 = (bf16[16,80,512]{2,1,0:T(8,128)(2,1)S(1)}, bf16[16,80,512]{2,1,0:T(8,128)(2,1)S(1)}, u32[]{:S(2)}, u32[]{:S(2)}) collective-permute-start(bf16[16,80,512]{2,1,0:T(8,128)(2,1)S(1)} %copy_kernel.1.refs_6_.refs_4_), channel_id=1, source_target_pairs={{0,256},{256,0},{1,257},{257,1},{2,258},{258,2},{3,259},{259,3},{4... | collective-permute-start | bytes 3932168 | tf_op jit(solution)/shard_map/ppermute | solution.py:39
  67.5 16.1 %copy-start.1 = (bf16[4,40,1024]{2,1,0:T(8,128)(2,1)S(1)}, bf16[4,40,1024]{2,1,0:T(8,128)(2,1)}, u32[]{:S(2)}) copy-start(bf16[4,40,1024]{2,1,0:T(8,128)(2,1)} %copy-done) | copy-start | bytes 983044
  86.2 5.6 %collective-permute-start.7 = (bf16[160,1536]{1,0:T(8,128)(2,1)S(1)}, bf16[160,1536]{1,0:T(8,128)(2,1)S(1)}, u32[]{:S(2)}, u32[]{:S(2)}) collective-permute-start(bf16[160,1536]{1,0:T(8,128)(2,1)S(1)} %get-tuple-element.35.refs_2_.refs_4_), channel_id=1, source_target_pairs={{0,256},{256,0},{1,257},{257,1},{2,258},{258,2},{3,259},{259,3},{4... | collective-permute-start | bytes 1474568 | tf_op jit(solution)/shard_map/ppermute | solution.py:39
  93.9 21.4 %all-to-all-start.3 = ((bf16[16,32,1024]{2,1,0:T(8,128)(2,1)}), bf16[16,32,1024]{2,1,0:T(8,128)(2,1)}, u32[]{:S(2)}, u32[]{:S(2)}) async-start(bf16[16,32,1024]{2,1,0:T(8,128)(2,1)} %get-tuple-element.37), calls=%async_computation.3 | async-start | bytes 2097152 | tf_op jit(solution)/shard_map/all_to_all | solution.py:54
  103.1 20.2 %collective-permute-start.8 = (bf16[2,40,1024]{2,1,0:T(8,128)(2,1)}, bf16[2,40,1024]{2,1,0:T(8,128)(2,1)S(1)}, u32[]{:S(2)}, u32[]{:S(2)}) collective-permute-start(bf16[2,40,1024]{2,1,0:T(8,128)(2,1)} %get-tuple-element.41), channel_id=1, source_target_pairs={{0,1},{1,0},{2,3},{3,2},{4,5},{5,4},{6,7},{7,6},{8,9},{9,8},{10,11... | collective-permute-start | bytes 491528 | tf_op jit(solution)/shard_map/ppermute | solution.py:31
  105.1 18.2 %collective-permute-start.9 = (bf16[2,40,1024]{2,1,0:T(8,128)(2,1)}, bf16[2,40,1024]{2,1,0:T(8,128)(2,1)S(1)}, u32[]{:S(2)}, u32[]{:S(2)}) collective-permute-start(bf16[2,40,1024]{2,1,0:T(8,128)(2,1)} %get-tuple-element.42), channel_id=1, source_target_pairs={{0,2},{1,3},{2,0},{3,1},{4,6},{5,7},{6,4},{7,5},{8,10},{9,11},{10,... | collective-permute-start | bytes 491528 | tf_op jit(solution)/shard_map/ppermute | solution.py:31
  108.4 14.9 %collective-permute-start.10 = (bf16[2,40,1024]{2,1,0:T(8,128)(2,1)}, bf16[2,40,1024]{2,1,0:T(8,128)(2,1)S(1)}, u32[]{:S(2)}, u32[]{:S(2)}) collective-permute-start(bf16[2,40,1024]{2,1,0:T(8,128)(2,1)} %get-tuple-element.43), channel_id=1, source_target_pairs={{0,3},{1,2},{2,1},{3,0},{4,7},{5,6},{6,5},{7,4},{8,11},{9,10},{10,... | collective-permute-start | bytes 491528 | tf_op jit(solution)/shard_map/ppermute | solution.py:31
  117.4 17.6 %all-to-all-start.4 = ((bf16[4,16,512]{2,1,0:T(8,128)(2,1)}), bf16[4,16,512]{2,1,0:T(8,128)(2,1)S(1)}, u32[]{:S(2)}, u32[]{:S(2)}) async-start(bf16[4,16,512]{2,1,0:T(8,128)(2,1)} %plane_sum_kernel.1), calls=%async_computation.4 | async-start | bytes 131072 | tf_op jit(solution)/shard_map/all_to_all | solution.py:54
  123.3 0.7 copy-start.6
  123.3 0.7 copy-start.7
  123.3 0.8 copy-start.8
